TPU v7x, 32 devices: a whole 2x2x4 slice. The times are simulated.
32 devices in a mesh: dp: 16 (over z, y, x), ffn: 2 (over core).
Axes of the slice: x: 2, y: 2, z: 4, core: 2. Of those that a mesh axis runs over, the one named last changes fastest.
Arguments:
- states: bfloat16 [32768, 384], P('dp'), may hold values from -8 to 8
- teacher_states: bfloat16 [32768, 768], P('dp'), may hold values from -6 to 6
- lengths: int32 [32], P('dp'), may hold values from 128 to 1024
- domain_ids: int32 [32], P('dp'), may hold values from 0 to 7
- domain_weight: float32 [8], replicated, may hold values from 0.5 to 2
- teacher_qkv: bfloat16 [768, 3, 768], P(None, None, 'ffn'), may hold values from -0.21875 to 0.21875
- attn_a: float32 [384, 1536], P('dp'), may hold values from -0.8164966 to 0.8164966
- ffn_in: float32 [384, 1536], P('dp', 'ffn'), may hold values from -0.4082483 to 0.4082483
- ffn_out: float32 [384, 1536], P('dp', 'ffn'), may hold values from -0.15625 to 0.15625
- attn_b: float32 [384, 3, 384], P('dp', None, 'ffn'), may hold values from -0.3125 to 0.3125
- vec_d: float32 [384, 8], P('dp'), may hold values from -1.5 to 3
- mom1_attn_a: float32 [384, 1536], P('dp'), may hold values from -0.0004272461 to 0.0004272461
- mom1_ffn_in: float32 [384, 1536], P('dp', 'ffn'), may hold values from -0.0004272461 to 0.0004272461
- mom1_ffn_out: float32 [384, 1536], P('dp', 'ffn'), may hold values from -0.0004272461 to 0.0004272461
- mom1_attn_b: float32 [384, 3, 384], P('dp', None, 'ffn'), may hold values from -0.0004272461 to 0.0004272461
- mom1_vec_d: float32 [384, 8], P('dp'), may hold values from -0.001953125 to 0.001953125
- mom2_attn_a: float32 [384, 1536], P('dp'), may hold values from 2.257426e-10 to 3.6118817e-09
- mom2_ffn_in: float32 [384, 1536], P('dp', 'ffn'), may hold values from 2.257426e-10 to 3.6118817e-09
- mom2_ffn_out: float32 [384, 1536], P('dp', 'ffn'), may hold values from 2.257426e-10 to 3.6118817e-09
- mom2_attn_b: float32 [384, 3, 384], P('dp', None, 'ffn'), may hold values from 2.257426e-10 to 3.6118817e-09
- mom2_vec_d: float32 [384, 8], P('dp'), may hold values from 3.6118817e-09 to 5.643565e-08
Outputs:
- grad_norm: float32 [], replicated
- new_attn_a: float32 [384, 1536], P('dp')
- new_ffn_in: float32 [384, 1536], P('dp', 'ffn')
- new_ffn_out: float32 [384, 1536], P('dp', 'ffn')
- new_attn_b: float32 [384, 3, 384], P('dp', None, 'ffn')
- new_vec_d: float32 [384, 8], P('dp')
- out_mom1_attn_a: float32 [384, 1536], P('dp')
- out_mom1_ffn_in: float32 [384, 1536], P('dp', 'ffn')
- out_mom1_ffn_out: float32 [384, 1536], P('dp', 'ffn')
- out_mom1_attn_b: float32 [384, 3, 384], P('dp', None, 'ffn')
- out_mom1_vec_d: float32 [384, 8], P('dp')
- out_mom2_attn_a: float32 [384, 1536], P('dp')
- out_mom2_ffn_in: float32 [384, 1536], P('dp', 'ffn')
- out_mom2_ffn_out: float32 [384, 1536], P('dp', 'ffn')
- out_mom2_attn_b: float32 [384, 3, 384], P('dp', None, 'ffn')
- out_mom2_vec_d: float32 [384, 8], P('dp')
All inputs are finite; a program needn't handle non-finite values.
Results may differ from a plain program's by a relative error of at most 0.0072.
Values may be sent and summed in bfloat16 or wider, within the bound.
No kernel may reach another device: no remote copies, remote signals or barrier semaphores. Data moves between devices by JAX's collectives and lax.ppermute only.
A program may use at most 320 MiB of HBM per device.

v0:
```python
import jax
import jax.numpy as jnp
from jax import lax
from jax.sharding import PartitionSpec as P

HEADS = 12
MICRO = 2
STEP = 10


NORM_EPSILON = 1e-12
CLIP_NORM = 1.0
BETA_ONE = 0.9
BETA_TWO = 0.999
ADAM_EPSILON = 1e-08
RATE_MATRIX = 0.04
RATE_VECTOR = 0.2
DECAY_RATE = 0.01
MASK_VALUE = -1e30
ROW_DIMS = (((0,), (0,)), ((), ()))
COLUMN_DIMS = (((1,), (1,)), ((), ()))


def layer_norm(resid, gain, shift):
    centred = resid - jnp.mean(resid, axis=-1, keepdims=True)
    inverse = lax.rsqrt(jnp.mean(centred * centred, axis=-1, keepdims=True) + NORM_EPSILON)
    normed = centred * inverse
    return (normed * gain + shift, normed, inverse)


def norm_back(grad_out, normed, inverse, gain):
    scaled = grad_out * gain
    inner = (
        scaled
        - jnp.mean(scaled, axis=-1, keepdims=True)
        - normed * jnp.mean(scaled * normed, axis=-1, keepdims=True)
    )
    return (inverse * inner, jnp.sum(grad_out * normed, axis=0), jnp.sum(grad_out, axis=0))


def block_softmax(query, keys, values, lengths, first_row, position, block_rows, head_count):
    sequence_rows = keys.shape[1]
    features = query.shape[1]
    head_size = features // head_count
    offset = position * block_rows
    sequence = (first_row + offset) // sequence_rows
    query_block = query.reshape(block_rows, head_count, head_size)
    key_rows = lax.dynamic_index_in_dim(keys, sequence, 0, keepdims=False).reshape(
        sequence_rows, head_count, head_size
    )
    value_rows = lax.dynamic_index_in_dim(values, sequence, 0, keepdims=False).reshape(
        sequence_rows, head_count, head_size
    )
    length = lax.dynamic_index_in_dim(lengths, sequence, 0, keepdims=False)
    scores = jnp.einsum(
        "qhd,khd->hqk", query_block, key_rows, preferred_element_type=jnp.float32
    ) * head_size ** (-0.5)
    scores = jnp.where(jnp.arange(sequence_rows) < length, scores, MASK_VALUE)
    return (query_block, key_rows, value_rows, jax.nn.softmax(scores, axis=-1), sequence, offset)


def attend_forward(query, keys, values, lengths, first_row, head_count):
    row_count, features = query.shape
    block_rows = min(512, row_count)

    def one_block(position):
        query_block, key_rows, value_rows, softmaxed, sequence, offset = block_softmax(
            query, keys, values, lengths, first_row, position, block_rows, head_count
        )
        mixed = jnp.einsum(
            "hqk,khd->qhd",
            softmaxed.astype(jnp.bfloat16),
            value_rows,
            preferred_element_type=jnp.float32,
        )
        return mixed.reshape(block_rows, features)

    return lax.map(one_block, jnp.arange(row_count // block_rows)).reshape(row_count, features)


def attend_backward(query, keys, values, lengths, first_row, head_count, grad_mixed):
    row_count, features = query.shape
    sequence_rows = keys.shape[1]
    head_size = features // head_count
    scaling = head_size ** (-0.5)
    block_rows = min(512, row_count)

    def one_block(running, position):
        key_grad, value_grad = running
        query_block, key_rows, value_rows, softmaxed, sequence, offset = block_softmax(
            query, keys, values, lengths, first_row, position, block_rows, head_count
        )
        grad_block = grad_mixed.reshape(block_rows, head_count, head_size)
        prob_grad = jnp.einsum(
            "qhd,khd->hqk", grad_block, value_rows, preferred_element_type=jnp.float32
        )
        score_grad = (
            softmaxed * (prob_grad - jnp.sum(prob_grad * softmaxed, axis=-1, keepdims=True))
        ).astype(jnp.bfloat16)
        query_part = (
            jnp.einsum("hqk,khd->qhd", score_grad, key_rows, preferred_element_type=jnp.float32)
            * scaling
        )
        key_add = (
            jnp.einsum("hqk,qhd->khd", score_grad, query_block, preferred_element_type=jnp.float32)
            * scaling
        )
        value_add = jnp.einsum(
            "hqk,qhd->khd",
            softmaxed.astype(jnp.bfloat16),
            grad_block,
            preferred_element_type=jnp.float32,
        )
        key_old = lax.dynamic_index_in_dim(key_grad, sequence, 0, keepdims=False)
        value_old = lax.dynamic_index_in_dim(value_grad, sequence, 0, keepdims=False)
        key_grad = lax.dynamic_update_index_in_dim(
            key_grad, key_old + key_add.reshape(sequence_rows, features), sequence, 0
        )
        value_grad = lax.dynamic_update_index_in_dim(
            value_grad, value_old + value_add.reshape(sequence_rows, features), sequence, 0
        )
        return ((key_grad, value_grad), query_part.reshape(block_rows, features))

    zeros = jnp.zeros(keys.shape, jnp.float32)
    (key_grad, value_grad), query_grad = lax.scan(
        one_block, (zeros, zeros), jnp.arange(row_count // block_rows)
    )
    return (query_grad.reshape(row_count, features), key_grad, value_grad)


def relation_grads(student, teacher, length, weight, head_count):
    sequence_rows = student.shape[0]
    head_size = student.shape[2] // head_count
    teacher_size = teacher.shape[2] // head_count
    student_scale = head_size ** (-0.5)
    teacher_scale = teacher_size ** (-0.5)
    block_rows = min(512, sequence_rows)
    query = student[:, 0].reshape(sequence_rows, head_count, head_size)
    keys = student[:, 1].reshape(sequence_rows, head_count, head_size)
    values = student[:, 2].reshape(sequence_rows, head_count, head_size)
    teacher_query = teacher[:, 0].reshape(sequence_rows, head_count, teacher_size)
    teacher_keys = teacher[:, 1].reshape(sequence_rows, head_count, teacher_size)
    teacher_values = teacher[:, 2].reshape(sequence_rows, head_count, teacher_size)
    live = jnp.arange(sequence_rows) < length

    def logits(left, right, scaling):
        return jnp.where(
            live,
            jnp.einsum("qhd,khd->hqk", left, right, preferred_element_type=jnp.float32) * scaling,
            MASK_VALUE,
        )

    def one_block(running, position):
        key_grad, value_grad = running
        offset = position * block_rows
        query_block = lax.dynamic_slice_in_dim(query, offset, block_rows, 0)
        value_block = lax.dynamic_slice_in_dim(values, offset, block_rows, 0)
        teacher_qblock = lax.dynamic_slice_in_dim(teacher_query, offset, block_rows, 0)
        teacher_vblock = lax.dynamic_slice_in_dim(teacher_values, offset, block_rows, 0)
        row_weight = jnp.where(offset + jnp.arange(block_rows) < length, weight, 0.0)[None, :, None]
        attention = jax.nn.softmax(
            logits(query_block, keys, student_scale), axis=-1
        ) - jax.nn.softmax(logits(teacher_qblock, teacher_keys, teacher_scale), axis=-1)
        att_grad = (attention * row_weight).astype(jnp.bfloat16)
        relation = jax.nn.softmax(
            logits(value_block, values, student_scale), axis=-1
        ) - jax.nn.softmax(logits(teacher_vblock, teacher_values, teacher_scale), axis=-1)
        rel_grad = (relation * row_weight).astype(jnp.bfloat16)
        query_part = (
            jnp.einsum("hqk,khd->qhd", att_grad, keys, preferred_element_type=jnp.float32)
            * student_scale
        )
        key_grad = (
            key_grad
            + jnp.einsum("hqk,qhd->khd", att_grad, query_block, preferred_element_type=jnp.float32)
            * student_scale
        )
        value_rows = (
            jnp.einsum("hqk,khd->qhd", rel_grad, values, preferred_element_type=jnp.float32)
            * student_scale
        )
        value_grad = (
            value_grad
            + jnp.einsum("hqk,qhd->khd", rel_grad, value_block, preferred_element_type=jnp.float32)
            * student_scale
        )
        return ((key_grad, value_grad), (query_part, value_rows))

    zeros = jnp.zeros((sequence_rows, head_count, head_size), jnp.float32)
    (key_grad, value_grad), (query_grad, value_rows) = lax.scan(
        one_block, (zeros, zeros), jnp.arange(sequence_rows // block_rows)
    )
    value_grad = value_grad + value_rows.reshape(sequence_rows, head_count, head_size)
    flat = head_count * head_size
    return jnp.stack(
        [
            query_grad.reshape(sequence_rows, flat),
            key_grad.reshape(sequence_rows, flat),
            value_grad.reshape(sequence_rows, flat),
        ],
        axis=1,
    )


def adam_update(weight, gradient, first, second, clipped, rate, decay):
    scaled = gradient * clipped
    first_new = BETA_ONE * first + (1.0 - BETA_ONE) * scaled
    second_new = BETA_TWO * second + (1.0 - BETA_TWO) * scaled * scaled
    ratio = (
        first_new
        / (1.0 - BETA_ONE**STEP)
        / (jnp.sqrt(second_new / (1.0 - BETA_TWO**STEP)) + ADAM_EPSILON)
    )
    return (weight - rate * (ratio + decay * weight), first_new, second_new)


def per_device(
    states,
    teacher_states,
    lengths,
    domain_ids,
    domain_weight,
    teacher_qkv,
    attn_a,
    ffn_in,
    ffn_out,
    attn_b,
    vec_d,
    mom1_attn_a,
    mom1_ffn_in,
    mom1_ffn_out,
    mom1_attn_b,
    mom1_vec_d,
    mom2_attn_a,
    mom2_ffn_in,
    mom2_ffn_out,
    mom2_attn_b,
    mom2_vec_d,
):
    cores = lax.axis_size("ffn")
    core = lax.axis_index("ffn")
    replicas = lax.axis_size("dp")
    sequence_count = lengths.shape[0]
    sequence_rows = states.shape[0] // sequence_count
    per_group = sequence_count // MICRO
    group_rows = per_group * sequence_rows
    own_rows = group_rows // cores
    first_row = core * own_rows
    features = states.shape[1]
    local_heads = HEADS // cores
    teacher_flat = teacher_qkv.reshape(teacher_qkv.shape[0], -1)
    masters = (attn_a, ffn_in, ffn_out, attn_b, vec_d)
    matched = domain_ids[:, None] == jnp.arange(domain_weight.shape[0])[None, :]
    sequence_weight = jnp.sum(jnp.where(matched, domain_weight[None, :], 0.0), axis=1) / HEADS

    def group_gradients(current, states_rows, teacher_rows, group_lengths, group_weight):
        attn_full, in_full, out_full, rel_full, vec_full = current
        vectors = vec_full.astype(jnp.float32)
        query_bias, value_bias, output_bias, gain_one, shift_one, down_bias, gain_two, shift_two = [
            vectors[:, column] for column in range(8)
        ]
        states_own = lax.dynamic_slice_in_dim(states_rows, first_row, own_rows, 0)
        key_value = jnp.dot(
            states_rows, attn_full[:, features : 3 * features], preferred_element_type=jnp.float32
        )
        keys = (
            key_value[:, :features].astype(jnp.bfloat16).reshape(per_group, sequence_rows, features)
        )
        values = (
            (key_value[:, features:] + value_bias)
            .astype(jnp.bfloat16)
            .reshape(per_group, sequence_rows, features)
        )
        query = (
            jnp.dot(states_own, attn_full[:, :features], preferred_element_type=jnp.float32)
            + query_bias
        ).astype(jnp.bfloat16)
        mixed = attend_forward(query, keys, values, group_lengths, first_row, HEADS).astype(
            jnp.bfloat16
        )
        output_proj = attn_full[:, 3 * features :]
        resid_one = (
            states_own.astype(jnp.float32)
            + lax.dot_general(mixed, output_proj, COLUMN_DIMS, preferred_element_type=jnp.float32)
            + output_bias
        )
        hidden_one, normed_one, inverse_one = layer_norm(resid_one, gain_one, shift_one)
        portion = lax.all_gather(hidden_one.astype(jnp.bfloat16), "ffn", axis=0, tiled=True)
        hidden_all = portion
        pre_act = jnp.dot(portion, in_full, preferred_element_type=jnp.float32)
        activated = jax.nn.gelu(pre_act, approximate=False).astype(jnp.bfloat16)
        resid_two = (
            hidden_one
            + lax.psum_scatter(
                lax.dot_general(
                    activated, out_full, COLUMN_DIMS, preferred_element_type=jnp.float32
                ).astype(jnp.bfloat16),
                "ffn",
                scatter_dimension=0,
                tiled=True,
            ).astype(jnp.float32)
            + down_bias
        )
        hidden_two, normed_two, inverse_two = layer_norm(resid_two, gain_two, shift_two)
        rel_flat = rel_full.reshape(rel_full.shape[0], -1)
        portion = lax.all_gather(hidden_two.astype(jnp.bfloat16), "ffn", axis=0, tiled=True)
        second_all = portion
        student = jnp.dot(portion, rel_flat, preferred_element_type=jnp.float32).astype(
            jnp.bfloat16
        )
        teacher = jnp.dot(teacher_rows, teacher_flat, preferred_element_type=jnp.float32).astype(
            jnp.bfloat16
        )
        relation_all = lax.map(
            lambda element: relation_grads(
                element[0], element[1], element[2], element[3], local_heads
            ),
            (
                student.reshape(per_group, sequence_rows, 3, -1),
                teacher.reshape(per_group, sequence_rows, 3, -1),
                group_lengths,
                group_weight,
            ),
        )
        projection_grad = relation_all.reshape(group_rows, -1).astype(jnp.bfloat16)
        grad_rel = lax.dot_general(
            second_all, projection_grad, ROW_DIMS, preferred_element_type=jnp.float32
        ).reshape(rel_full.shape)
        grad_two = lax.psum_scatter(
            lax.dot_general(
                projection_grad, rel_flat, COLUMN_DIMS, preferred_element_type=jnp.float32
            ).astype(jnp.bfloat16),
            "ffn",
            scatter_dimension=0,
            tiled=True,
        ).astype(jnp.float32)
        resid_grad_two, grad_gain_two, grad_shift_two = norm_back(
            grad_two, normed_two, inverse_two, gain_two
        )
        grad_down_bias = jnp.sum(resid_grad_two, axis=0)

        def spread(portion):
            upstream = jnp.dot(portion, out_full, preferred_element_type=jnp.float32)
            unused, pullback = jax.vjp(
                lambda inputs: jax.nn.gelu(inputs, approximate=False), pre_act
            )
            return (portion, pullback(upstream)[0].astype(jnp.bfloat16))

        branch_all, pre_grad = spread(
            lax.all_gather(resid_grad_two.astype(jnp.bfloat16), "ffn", axis=0, tiled=True)
        )
        grad_out_w = lax.dot_general(
            branch_all, activated, ROW_DIMS, preferred_element_type=jnp.float32
        )
        grad_in_w = lax.dot_general(
            hidden_all, pre_grad, ROW_DIMS, preferred_element_type=jnp.float32
        )
        grad_one = (
            lax.psum_scatter(
                lax.dot_general(
                    pre_grad, in_full, COLUMN_DIMS, preferred_element_type=jnp.float32
                ).astype(jnp.bfloat16),
                "ffn",
                scatter_dimension=0,
                tiled=True,
            ).astype(jnp.float32)
            + resid_grad_two
        )
        resid_grad_one, grad_gain_one, grad_shift_one = norm_back(
            grad_one, normed_one, inverse_one, gain_one
        )
        branch_grad = resid_grad_one.astype(jnp.bfloat16)
        grad_output = lax.dot_general(
            branch_grad, mixed, ROW_DIMS, preferred_element_type=jnp.float32
        )
        mixed_grad = jnp.dot(branch_grad, output_proj, preferred_element_type=jnp.float32).astype(
            jnp.bfloat16
        )
        query_grad, key_part, value_part = attend_backward(
            query, keys, values, group_lengths, first_row, HEADS, mixed_grad
        )
        key_grad, value_grad = (
            lax.psum_scatter(
                key_part.reshape(group_rows, features).astype(jnp.bfloat16),
                "ffn",
                scatter_dimension=0,
                tiled=True,
            ).astype(jnp.float32),
            lax.psum_scatter(
                value_part.reshape(group_rows, features).astype(jnp.bfloat16),
                "ffn",
                scatter_dimension=0,
                tiled=True,
            ).astype(jnp.float32),
        )
        projections = jnp.concatenate(
            [
                query_grad.astype(jnp.bfloat16),
                key_grad.astype(jnp.bfloat16),
                value_grad.astype(jnp.bfloat16),
            ],
            axis=1,
        )
        grad_attn = jnp.concatenate(
            [
                lax.dot_general(
                    states_own, projections, ROW_DIMS, preferred_element_type=jnp.float32
                ),
                grad_output,
            ],
            axis=1,
        )
        grad_vec = jnp.stack(
            [
                jnp.sum(projections[:, :features], axis=0, dtype=jnp.float32),
                jnp.sum(projections[:, 2 * features :], axis=0, dtype=jnp.float32),
                jnp.sum(branch_grad, axis=0, dtype=jnp.float32),
                grad_gain_one,
                grad_shift_one,
                grad_down_bias,
                grad_gain_two,
                grad_shift_two,
            ],
            axis=1,
        )
        return (grad_attn, grad_in_w, grad_out_w, grad_rel, grad_vec)

    running = tuple(
        (
            jnp.zeros((master.shape[0] * replicas,) + master.shape[1:], jnp.float32)
            for master in masters
        )
    )
    shards = tuple((jnp.zeros(master.shape, jnp.float32) for master in masters))
    for group_index in range(MICRO):
        row_start = group_index * group_rows
        seq_start = group_index * per_group
        current = (
            lax.all_gather(attn_a.astype(jnp.bfloat16), "dp", axis=0, tiled=True),
            lax.all_gather(ffn_in.astype(jnp.bfloat16), "dp", axis=0, tiled=True),
            lax.all_gather(ffn_out.astype(jnp.bfloat16), "dp", axis=0, tiled=True),
            lax.all_gather(attn_b.astype(jnp.bfloat16), "dp", axis=0, tiled=True),
            lax.all_gather(vec_d.astype(jnp.bfloat16), "dp", axis=0, tiled=True),
        )
        parts = group_gradients(
            current,
            states[row_start : row_start + group_rows],
            teacher_states[row_start : row_start + group_rows],
            lengths[seq_start : seq_start + per_group],
            sequence_weight[seq_start : seq_start + per_group],
        )
        running = tuple((earlier + later for earlier, later in zip(running, parts)))
    shards = (
        lax.psum_scatter(running[0], "dp", scatter_dimension=0, tiled=True),
        lax.psum_scatter(running[1], "dp", scatter_dimension=0, tiled=True),
        lax.psum_scatter(running[2], "dp", scatter_dimension=0, tiled=True),
        lax.psum_scatter(running[3], "dp", scatter_dimension=0, tiled=True),
        lax.psum_scatter(running[4], "dp", scatter_dimension=0, tiled=True),
    )
    grad_attn, grad_vec = lax.psum((shards[0], shards[4]), "ffn")
    gradients = (grad_attn, shards[1], shards[2], shards[3], grad_vec)
    squares = (
        (jnp.sum(grad_attn * grad_attn) + jnp.sum(grad_vec * grad_vec)) / cores
        + jnp.sum(shards[1] * shards[1])
        + jnp.sum(shards[2] * shards[2])
        + jnp.sum(shards[3] * shards[3])
    )
    grad_norm = jnp.sqrt(lax.psum(squares, ("dp", "ffn")))
    clipped = jnp.minimum(1.0, CLIP_NORM / grad_norm)
    firsts = (mom1_attn_a, mom1_ffn_in, mom1_ffn_out, mom1_attn_b, mom1_vec_d)
    seconds = (mom2_attn_a, mom2_ffn_in, mom2_ffn_out, mom2_attn_b, mom2_vec_d)
    rates = (RATE_MATRIX, RATE_MATRIX, RATE_MATRIX, RATE_MATRIX, RATE_VECTOR)
    decays = (DECAY_RATE, DECAY_RATE, DECAY_RATE, DECAY_RATE, 0.0)
    news = [
        adam_update(
            masters[number],
            gradients[number],
            firsts[number],
            seconds[number],
            clipped,
            rates[number],
            decays[number],
        )
        for number in range(5)
    ]
    return (
        grad_norm,
        news[0][0],
        news[1][0],
        news[2][0],
        news[3][0],
        news[4][0],
        news[0][1],
        news[1][1],
        news[2][1],
        news[3][1],
        news[4][1],
        news[0][2],
        news[1][2],
        news[2][2],
        news[3][2],
        news[4][2],
    )


def solution(mesh):
    in_specs = (
        P("dp", None),
        P("dp", None),
        P("dp"),
        P("dp"),
        P(),
        P(None, None, "ffn"),
        P("dp", None),
        P("dp", "ffn"),
        P("dp", "ffn"),
        P("dp", None, "ffn"),
        P("dp", None),
        P("dp", None),
        P("dp", "ffn"),
        P("dp", "ffn"),
        P("dp", None, "ffn"),
        P("dp", None),
        P("dp", None),
        P("dp", "ffn"),
        P("dp", "ffn"),
        P("dp", None, "ffn"),
        P("dp", None),
    )
    out_specs = (
        P(),
        P("dp", None),
        P("dp", "ffn"),
        P("dp", "ffn"),
        P("dp", None, "ffn"),
        P("dp", None),
        P("dp", None),
        P("dp", "ffn"),
        P("dp", "ffn"),
        P("dp", None, "ffn"),
        P("dp", None),
        P("dp", None),
        P("dp", "ffn"),
        P("dp", "ffn"),
        P("dp", None, "ffn"),
        P("dp", None),
    )
    return jax.shard_map(
        per_device, mesh=mesh, in_specs=in_specs, out_specs=out_specs, check_vma=False
    )
```

profile of v0, /device:TPU:0, one launch (start us, length us, event | category | flops | bytes accessed | tf_op | source)
XLA Modules:
  0.0 1676.4 jit_solution(11257882475895519405)
XLA Ops:
  9.5 42.7 %all-gather = bf16[16,24,8]{1,2,0:T(8,128)(2,1)S(1)} all-gather(bf16[1,24,8]{1,2,0:T(8,128)(2,1)S(1)} %convert_bitcast_fusion), channel_id=1, replica_groups=mesh['dp'=16,'ffn'=2] {'dp'}, dimensions={0}, use_global_device_ids=true | all-gather | bytes 6528 | tf_op jit(solution)/shard_map/all_gather | solution.py:443
  64.2 41.4 %all_gather.44 = bf16[384,3,192]{2,0,1:T(8,128)(2,1)} all-gather(bf16[24,3,192]{2,0,1:T(8,128)(2,1)} %convert_element_type.303), channel_id=1, replica_groups=mesh['dp'=16,'ffn'=2] {'dp'}, dimensions={0}, use_global_device_ids=true | all-gather | bytes 470016 | tf_op jit(solution)/shard_map/all_gather | solution.py:442
  105.6 44.1 %all_gather.41 = bf16[384,768]{1,0:T(8,128)(2,1)} all-gather(bf16[24,768]{1,0:T(8,128)(2,1)} %convert_element_type.297), channel_id=1, replica_groups=mesh['dp'=16,'ffn'=2] {'dp'}, dimensions={0}, use_global_device_ids=true | all-gather | bytes 626688 | tf_op jit(solution)/shard_map/all_gather | solution.py:440
  149.7 41.4 %all_gather.42 = bf16[384,768]{1,0:T(8,128)(2,1)} all-gather(bf16[24,768]{1,0:T(8,128)(2,1)} %convert_element_type.299), channel_id=1, replica_groups=mesh['dp'=16,'ffn'=2] {'dp'}, dimensions={0}, use_global_device_ids=true | all-gather | bytes 626688 | tf_op jit(solution)/shard_map/all_gather | solution.py:441
  202.1 14.3 fusion.352
  216.4 10.3 fusion.258
  229.3 14.1 fusion.350
  243.4 10.7 fusion.261
  318.4 286.5 %while.51 = (s32[]{:T(128)}, f32[1024,6,32]{0,2,1:T(8,128)}, f32[1024,6,32]{0,2,1:T(8,128)S(1)}, bf16[2,512,6,32]{1,0,3,2:T(2,128)(2,1)}, f32[2,512,6,32]{1,0,3,...) while((s32[]{:T(128)}, f32[1024,6,32]{0,2,1:T(8,128)}, ...), condition=%wide.region_43.44_spmd.clone.clone.clone, body=%wide.region_34.43_spmd.clone.clone.clone.sunk | while | flops 2920753664 | bytes 220804416 | solution.py:190
  367.5 22.2 %multiply_convert_fusion.21 = bf16[6,512,1024]{2,1,0:T(8,128)(2,1)} fusion(f32[6,512,1024]{2,1,0:T(8,128)} %subtract_exponential_fusion.17, f32[6,512,1024]{2,1,0:T(8,128)} %fusion.569, f32[512]{0:T(512)S(1)} %fusion.566, f32[6,512,1024]{2,1,0:T(8,128)} %fusion.570, pred[1024]{0:T(1024)(128)(4,1)S(1)} %iota_compare_fusion.7), kind=kOutput, calls=%fused_computation.99.clone.1 | output fusion | flops 31465470 | bytes 44043264 | tf_op jit(solution)/shard_map/while/body/eval_jaxpr/while/body/eval_jaxpr/div | solution.py:165
  429.0 22.1 %multiply_convert_fusion.20 = bf16[6,512,1024]{2,1,0:T(8,128)(2,1)} fusion(f32[6,512,1024]{2,1,0:T(8,128)} %subtract_exponential_fusion.16, f32[6,512,1024]{2,1,0:T(8,128)} %fusion.565, f32[512]{0:T(512)S(1)} %fusion.566, f32[6,512,1024]{2,1,0:T(8,128)} %fusion.567, pred[1024]{0:T(1024)(128)(4,1)S(1)} %iota_compare_fusion.7), kind=kOutput, calls=%fused_computation.104.clone.1 | output fusion | flops 31465470 | bytes 44043264 | tf_op jit(solution)/shard_map/while/body/eval_jaxpr/while/body/eval_jaxpr/div | solution.py:161
  500.2 22.2 %multiply_convert_fusion.21 = bf16[6,512,1024]{2,1,0:T(8,128)(2,1)} fusion(f32[6,512,1024]{2,1,0:T(8,128)} %subtract_exponential_fusion.17, f32[6,512,1024]{2,1,0:T(8,128)} %fusion.569, f32[512]{0:T(512)S(1)} %fusion.566, f32[6,512,1024]{2,1,0:T(8,128)} %fusion.570, pred[1024]{0:T(1024)(128)(4,1)S(1)} %iota_compare_fusion.7), kind=kOutput, calls=%fused_computation.99.clone.1 | output fusion | flops 31465470 | bytes 44043264 | tf_op jit(solution)/shard_map/while/body/eval_jaxpr/while/body/eval_jaxpr/div | solution.py:165
  561.8 22.1 %multiply_convert_fusion.20 = bf16[6,512,1024]{2,1,0:T(8,128)(2,1)} fusion(f32[6,512,1024]{2,1,0:T(8,128)} %subtract_exponential_fusion.16, f32[6,512,1024]{2,1,0:T(8,128)} %fusion.565, f32[512]{0:T(512)S(1)} %fusion.566, f32[6,512,1024]{2,1,0:T(8,128)} %fusion.567, pred[1024]{0:T(1024)(128)(4,1)S(1)} %iota_compare_fusion.7), kind=kOutput, calls=%fused_computation.104.clone.1 | output fusion | flops 31465470 | bytes 44043264 | tf_op jit(solution)/shard_map/while/body/eval_jaxpr/while/body/eval_jaxpr/div | solution.py:161
  613.1 292.6 %while.50 = (s32[]{:T(128)}, f32[1024,6,32]{0,2,1:T(8,128)}, f32[1024,6,32]{0,2,1:T(8,128)S(1)}, bf16[2,512,6,32]{1,0,3,2:T(2,128)(2,1)}, f32[2,512,6,32]{1,0,3,...) while((s32[]{:T(128)}, f32[1024,6,32]{0,2,1:T(8,128)}, ...), condition=%wide.region_17.18_spmd.clone.clone.clone, body=%wide.region_8.0_spmd.clone.clone.clone.sunk | while | flops 2920753664 | bytes 220804416 | solution.py:190
  661.1 22.2 %multiply_convert_fusion.19 = bf16[6,512,1024]{2,1,0:T(8,128)(2,1)} fusion(f32[6,512,1024]{2,1,0:T(8,128)} %subtract_exponential_fusion.15, f32[6,512,1024]{2,1,0:T(8,128)} %fusion.540, f32[512]{0:T(512)S(1)} %fusion.537, f32[6,512,1024]{2,1,0:T(8,128)} %fusion.541, pred[1024]{0:T(1024)(128)(4,1)S(1)} %iota_compare_fusion.6), kind=kOutput, calls=%fused_computation.10.clone.1 | output fusion | flops 31465470 | bytes 44043264 | tf_op jit(solution)/shard_map/while/body/eval_jaxpr/while/body/eval_jaxpr/div | solution.py:165
  722.6 22.1 %multiply_convert_fusion.18 = bf16[6,512,1024]{2,1,0:T(8,128)(2,1)} fusion(f32[6,512,1024]{2,1,0:T(8,128)} %subtract_exponential_fusion.14, f32[6,512,1024]{2,1,0:T(8,128)} %fusion.536, f32[512]{0:T(512)S(1)} %fusion.537, f32[6,512,1024]{2,1,0:T(8,128)} %fusion.538, pred[1024]{0:T(1024)(128)(4,1)S(1)} %iota_compare_fusion.6), kind=kOutput, calls=%fused_computation.15.clone.1 | output fusion | flops 31465470 | bytes 44043264 | tf_op jit(solution)/shard_map/while/body/eval_jaxpr/while/body/eval_jaxpr/div | solution.py:161
  767.4 9.6 fusion.540
  793.9 22.2 %multiply_convert_fusion.19 = bf16[6,512,1024]{2,1,0:T(8,128)(2,1)} fusion(f32[6,512,1024]{2,1,0:T(8,128)} %subtract_exponential_fusion.15, f32[6,512,1024]{2,1,0:T(8,128)} %fusion.540, f32[512]{0:T(512)S(1)} %fusion.537, f32[6,512,1024]{2,1,0:T(8,128)} %fusion.541, pred[1024]{0:T(1024)(128)(4,1)S(1)} %iota_compare_fusion.6), kind=kOutput, calls=%fused_computation.10.clone.1 | output fusion | flops 31465470 | bytes 44043264 | tf_op jit(solution)/shard_map/while/body/eval_jaxpr/while/body/eval_jaxpr/div | solution.py:165
  855.5 22.1 %multiply_convert_fusion.18 = bf16[6,512,1024]{2,1,0:T(8,128)(2,1)} fusion(f32[6,512,1024]{2,1,0:T(8,128)} %subtract_exponential_fusion.14, f32[6,512,1024]{2,1,0:T(8,128)} %fusion.536, f32[512]{0:T(512)S(1)} %fusion.537, f32[6,512,1024]{2,1,0:T(8,128)} %fusion.538, pred[1024]{0:T(1024)(128)(4,1)S(1)} %iota_compare_fusion.6), kind=kOutput, calls=%fused_computation.15.clone.1 | output fusion | flops 31465470 | bytes 44043264 | tf_op jit(solution)/shard_map/while/body/eval_jaxpr/while/body/eval_jaxpr/div | solution.py:161
  957.3 17.4 %multiply_reduce_fusion = (f32[12,512]{1,0:T(8,128)S(1)}, f32[12,512,1024]{2,1,0:T(8,128)}) fusion(f32[12,512,1024]{2,1,0:T(8,128)} %get-tuple-element.707, f32[12,512]{1,0:T(8,128)S(1)} %copy-done.106, bf16[512,12,32]{0,2,1:T(8,128)(2,1)S(1)} %bitcast.337, bf16[1024,12,32]{0,2,1:T(8,128)(2,1)} %bitcast.327), kind=kOutput, calls=%fused_computation.183 | convolution fusion | flops 421521408 | bytes 51560448 | tf_op jit(solution)/shard_map/while/body/eval_jaxpr/qhd,khd->hqk/dot_general | solution.py:94
  974.7 10.8 fusion.251
  985.6 21.6 %multiply_convert_fusion.4 = bf16[12,512,1024]{2,1,0:T(8,128)(2,1)} fusion(f32[12,512,1024]{2,1,0:T(8,128)} %get-tuple-element.719, f32[12,512]{1,0:T(8,128)S(1)} %get-tuple-element.718, f32[12,512,1024]{2,1,0:T(8,128)} %get-tuple-element.707, f32[12,512]{1,0:T(8,128)S(1)} %copy-done.106), kind=kLoop, calls=%fused_computation.182 | loop fusion | flops 25165824 | bytes 62963712 | tf_op jit(solution)/shard_map/while/body/eval_jaxpr/convert_element_type | solution.py:99
  1009.0 18.9 %multiply_reduce_fusion.1 = (f32[12,512]{1,0:T(8,128)S(1)}, f32[12,512,1024]{2,1,0:T(8,128)}) fusion(f32[12,512,1024]{2,1,0:T(8,128)} %get-tuple-element.711, f32[12,512]{1,0:T(8,128)S(1)} %copy-done.105, bf16[512,12,32]{0,2,1:T(8,128)(2,1)S(1)} %bitcast.335, bf16[1024,12,32]{0,2,1:T(8,128)(2,1)S(1)} %bitcast.326), kind=kOutput, calls=%fused_computation.187 | convolution fusion | flops 421521408 | bytes 51560448 | tf_op jit(solution)/shard_map/while/body/eval_jaxpr/qhd,khd->hqk/dot_general | solution.py:94
  1035.7 11.1 fusion.248
  1046.9 16.7 multiply_convert_fusion.5
  1111.3 96.3 %reduce-scatter.42.cloned.1.call-done = f32[24,3,192]{2,0,1:T(8,128)} async-done(((f32[384,3,192]{2,0,1:T(8,128)}), f32[24,3,192]{2,0,1:T(8,128)}) %reduce-scatter.42.cloned.1.call-update) | async-done | bytes 55312 | tf_op jit(solution)/shard_map/reduce_scatter | solution.py:457
  1209.3 126.4 %reduce-scatter.40.cloned.1.call-done = f32[24,768]{1,0:T(8,128)} async-done(((f32[384,768]{1,0:T(8,128)}), f32[24,768]{1,0:T(8,128)}) %reduce-scatter.40.cloned.1.call-update) | async-done | bytes 73744 | tf_op jit(solution)/shard_map/reduce_scatter | solution.py:456
  1337.2 126.5 %reduce-scatter.38.cloned.1.call-done = f32[24,768]{1,0:T(8,128)} async-done(((f32[384,768]{1,0:T(8,128)}), f32[24,768]{1,0:T(8,128)}) %reduce-scatter.38.cloned.1.call-update) | async-done | bytes 73744 | tf_op jit(solution)/shard_map/reduce_scatter | solution.py:455
  1465.6 75.1 %all-reduce = f32[384,8]{0,1:T(8,128)S(1)} all-reduce(f32[384,8]{0,1:T(8,128)S(1)} %add.435), channel_id=13, replica_groups=mesh['dp'=16,'ffn'=2] {'dp'}, use_global_device_ids=true, to_apply=%region_72.73.clone | all-reduce | flops 3072 | bytes 24576
  1540.6 54.8 %reduce-scatter.36.cloned.1.call-done = f32[24,1536]{1,0:T(8,128)} async-done(((f32[384,1536]{1,0:T(8,128)}), f32[24,1536]{1,0:T(8,128)}) %reduce-scatter.36.cloned.1.call-update) | async-done | bytes 147472 | tf_op jit(solution)/shard_map/reduce_scatter | solution.py:454
  1598.6 16.3 all-reduce.3.cloned.1.call-done
  1619.7 40.6 %psum.23 = f32[]{:T(128)} all-reduce(f32[]{:T(128)S(6)} %add.442), channel_id=1, replica_groups=mesh['dp'=16,'ffn'=2] {'dp','ffn'}, use_global_device_ids=true, to_apply=%region_81.82 | all-reduce | flops 1 | bytes 8 | tf_op jit(solution)/shard_map/psum | solution.py:468
  (559 shorter events, 566.3 us)
Async XLA Ops:
  7.2 189.1 %all-gather.3.cloned.1.call-start = ((), (), s32[]{:S(2)}) async-start(), calls=%async_computation.14 | async-start | bytes 1253376 | tf_op jit(solution)/shard_map/all_gather | solution.py:439
  8.8 297.8 %reduce-scatter.16.cloned.1.call-start = ((), (), s32[]{:S(2)}) async-start(), calls=%async_computation.15 | async-start | bytes 1179648 | tf_op jit(solution)/shard_map/reduce_scatter | solution.py:294
  269.4 37.2 %reduce-scatter.26.cloned.1.call-start = ((), (), s32[]{:S(2)}) async-start(), calls=%async_computation.20 | async-start | bytes 1179648 | tf_op jit(solution)/shard_map/reduce_scatter | solution.py:294
  283.9 629.8 %reduce-scatter.28.cloned.1.call-start = ((), (), s32[]{:S(2)}) async-start(), calls=%async_computation.21 | async-start | bytes 1179648 | tf_op jit(solution)/shard_map/reduce_scatter | solution.py:329
  612.0 307.5 %reduce-scatter.18.cloned.1.call-start = ((), (), s32[]{:S(2)}) async-start(), calls=%async_computation.16 | async-start | bytes 1179648 | tf_op jit(solution)/shard_map/reduce_scatter | solution.py:329
  913.6 28.0 %reduce-scatter.30.cloned.1.call-start = ((), (), s32[]{:S(2)}) async-start(), calls=%async_computation.22 | async-start | bytes 1179648 | tf_op jit(solution)/shard_map/reduce_scatter | solution.py:359
  931.5 21.3 %reduce-scatter.20.cloned.1.call-start = ((), (), s32[]{:S(2)}) async-start(), calls=%async_computation.17 | async-start | bytes 1179648 | tf_op jit(solution)/shard_map/reduce_scatter | solution.py:359
  941.5 160.8 %reduce-scatter.34.cloned.1.call-start = ((), (), s32[]{:S(2)}) async-start(), calls=%async_computation.24 | async-start | bytes 1179648 | tf_op jit(solution)/shard_map/reduce_scatter | solution.py:389
  985.5 116.9 %reduce-scatter.32.cloned.1.call-start = ((), (), s32[]{:S(2)}) async-start(), calls=%async_computation.23 | async-start | bytes 1179648 | tf_op jit(solution)/shard_map/reduce_scatter | solution.py:383
  1035.7 69.8 %reduce-scatter.24.cloned.1.call-start = ((), (), s32[]{:S(2)}) async-start(), calls=%async_computation.19 | async-start | bytes 1179648 | tf_op jit(solution)/shard_map/reduce_scatter | solution.py:389
  1046.8 58.7 %reduce-scatter.22.cloned.1.call-start = ((), (), s32[]{:S(2)}) async-start(), calls=%async_computation.18 | async-start | bytes 1179648 | tf_op jit(solution)/shard_map/reduce_scatter | solution.py:383
  1068.6 138.9 %reduce-scatter.42.cloned.1.call-start = ((), (), s32[]{:S(2)}) async-start(), calls=%async_computation.29 | async-start | bytes 1253376 | tf_op jit(solution)/shard_map/reduce_scatter | solution.py:457
  1074.1 261.6 %reduce-scatter.40.cloned.1.call-start = ((), (), s32[]{:S(2)}) async-start(), calls=%async_computation.28 | async-start | bytes 1253376 | tf_op jit(solution)/shard_map/reduce_scatter | solution.py:456
  1078.3 385.3 %reduce-scatter.38.cloned.1.call-start = ((), (), s32[]{:S(2)}) async-start(), calls=%async_computation.27 | async-start | bytes 1253376 | tf_op jit(solution)/shard_map/reduce_scatter | solution.py:455
  1084.0 511.4 %reduce-scatter.36.cloned.1.call-start = ((), (), s32[]{:S(2)}) async-start(), calls=%async_computation.25 | async-start | bytes 2506752 | tf_op jit(solution)/shard_map/reduce_scatter | solution.py:454
  1107.6 357.5 %copy-start.68 = (bf16[512,384]{0,1:T(8,128)(2,1)S(1)}, bf16[512,384]{0,1:T(8,128)(2,1)}, u32[]{:S(2)}) copy-start(bf16[512,384]{0,1:T(8,128)(2,1)} %reduce-scatter.34.cloned.1.call-done) | copy-start | bytes 1179652
  1109.4 551.6 %copy-start.113 = (f32[24,8]{0,1:T(8,128)S(1)}, f32[24,8]{0,1:T(8,128)}, u32[]{:S(2)}) copy-start(f32[24,8]{0,1:T(8,128)} %param.35) | copy-start | bytes 2308
  1109.4 551.6 %copy-start.127 = (f32[24,8]{0,1:T(8,128)S(1)}, f32[24,8]{0,1:T(8,128)}, u32[]{:S(2)}) copy-start(f32[24,8]{0,1:T(8,128)} %param.40) | copy-start | bytes 2308
  1109.4 551.6 %copy-start.128 = (f32[24,8]{0,1:T(8,128)S(1)}, f32[24,8]{0,1:T(8,128)}, u32[]{:S(2)}) copy-start(f32[24,8]{0,1:T(8,128)} %param.45) | copy-start | bytes 2308
  1109.4 552.2 %copy-start.76 = (f32[24,3,192]{2,0,1:T(8,128)S(1)}, f32[24,3,192]{2,0,1:T(8,128)}, u32[]{:S(2)}) copy-start(f32[24,3,192]{2,0,1:T(8,128)} %param.34) | copy-start | bytes 165892
  1109.4 552.2 %copy-start.89 = (f32[24,3,192]{2,0,1:T(8,128)S(1)}, f32[24,3,192]{2,0,1:T(8,128)}, u32[]{:S(2)}) copy-start(f32[24,3,192]{2,0,1:T(8,128)} %param.39) | copy-start | bytes 165892
  1109.5 552.2 %copy-start.90 = (f32[24,3,192]{2,0,1:T(8,128)S(1)}, f32[24,3,192]{2,0,1:T(8,128)}, u32[]{:S(2)}) copy-start(f32[24,3,192]{2,0,1:T(8,128)} %param.44) | copy-start | bytes 165892
  1109.5 553.8 %copy-start.78 = (f32[24,768]{1,0:T(8,128)S(1)}, f32[24,768]{1,0:T(8,128)}, u32[]{:S(2)}) copy-start(f32[24,768]{1,0:T(8,128)} %param.33) | copy-start | bytes 221188
  1109.5 553.8 %copy-start.91 = (f32[24,768]{1,0:T(8,128)S(1)}, f32[24,768]{1,0:T(8,128)}, u32[]{:S(2)}) copy-start(f32[24,768]{1,0:T(8,128)} %param.38) | copy-start | bytes 221188
  1109.5 553.8 %copy-start.92 = (f32[24,768]{1,0:T(8,128)S(1)}, f32[24,768]{1,0:T(8,128)}, u32[]{:S(2)}) copy-start(f32[24,768]{1,0:T(8,128)} %param.43) | copy-start | bytes 221188
  1109.5 555.4 %copy-start.80 = (f32[24,768]{1,0:T(8,128)S(1)}, f32[24,768]{1,0:T(8,128)}, u32[]{:S(2)}) copy-start(f32[24,768]{1,0:T(8,128)} %param.32) | copy-start | bytes 221188
  1109.5 555.4 %copy-start.93 = (f32[24,768]{1,0:T(8,128)S(1)}, f32[24,768]{1,0:T(8,128)}, u32[]{:S(2)}) copy-start(f32[24,768]{1,0:T(8,128)} %param.37) | copy-start | bytes 221188
  1109.5 555.4 %copy-start.94 = (f32[24,768]{1,0:T(8,128)S(1)}, f32[24,768]{1,0:T(8,128)}, u32[]{:S(2)}) copy-start(f32[24,768]{1,0:T(8,128)} %param.42) | copy-start | bytes 221188
  1109.5 556.9 %copy-start.59 = (f32[24,1536]{1,0:T(8,128)S(1)}, f32[24,1536]{1,0:T(8,128)}, u32[]{:S(2)}) copy-start(f32[24,1536]{1,0:T(8,128)} %param.31) | copy-start | bytes 442372
  1109.6 556.9 %copy-start.81 = (f32[24,1536]{1,0:T(8,128)S(1)}, f32[24,1536]{1,0:T(8,128)}, u32[]{:S(2)}) copy-start(f32[24,1536]{1,0:T(8,128)} %param.36) | copy-start | bytes 442372
  1109.6 556.9 %copy-start.82 = (f32[24,1536]{1,0:T(8,128)S(1)}, f32[24,1536]{1,0:T(8,128)}, u32[]{:S(2)}) copy-start(f32[24,1536]{1,0:T(8,128)} %param.41) | copy-start | bytes 442372
  1109.6 505.3 %all-reduce.3.cloned.1.call-start = ((), (), s32[]{:S(2)}) async-start(), calls=%async_computation.26 | async-start | bytes 294912 | tf_op jit(solution)/shard_map/psum | solution.py:460
  (131 other events, 2639.8 us)
Sparse Core Ops, SparseCore 0:
  11.4 59.9 all-gather.2
  269.5 5.7 reduce-scatter.15
  284.0 5.7 reduce-scatter.25
  612.1 5.7 reduce-scatter.27
  913.7 5.7 reduce-scatter.17
  931.6 9.4 reduce-scatter.29
  943.4 9.3 reduce-scatter.19
  985.6 9.4 reduce-scatter.33
  1035.8 9.4 reduce-scatter.31
  1047.4 9.3 reduce-scatter.23
  1068.7 9.4 reduce-scatter.21
  1082.8 124.6 reduce-scatter.41
  1212.3 123.3 reduce-scatter.39
  1340.3 123.3 reduce-scatter.37
  1468.4 126.9 reduce-scatter.35
  1597.7 17.1 all-reduce.2
where the time goes:
time: 1690 us; the launch traced here: 1680 us
  matrix products  490 us (29%)
  waiting for transfers between devices  434 us (26%)
  blocking collectives  302 us (18%)
  other arithmetic  260 us (15%)
  local copies, waits for them, and re-layouts  117 us (7%)
  loops' own time  50.3 us (3%)
  between operations  22 us (1%)
    reduce_scatter x1, waiting for transfers between devices, per_device(): lax.psum_scatter(running[1], 'dp', scatter_dimension=0, tiled=True)  126 us
    reduce_scatter x1, waiting for transfers between devices, per_device(): lax.psum_scatter(running[2], 'dp', scatter_dimension=0, tiled=True)  126 us
    reduce_scatter x1, waiting for transfers between devices, per_device(): lax.psum_scatter(running[3], 'dp', scatter_dimension=0, tiled=True)  96.3 us
    div x4, other arithmetic, one_block(): jax.nn.softmax(logits(value_block, values, student_scale), axis=-1)  88.6 us
    div x4, other arithmetic, one_block(): jax.nn.softmax(logits(query_block, keys, student_scale), axis=-1)  88.4 us
    unnamed x1, blocking collectives  75.1 us
    dynamic_update_slice x16, local copies, waits for them, and re-layouts, relation_grads(): lax.scan(one_block, (zeros, zeros), jnp.arange(sequence_rows // block_rows))  69 us
    dot_general x8, matrix products, logits(): jnp.einsum('qhd,khd->hqk', left, right, preferred_element_type=jnp.float32)  55.4 us
  transfers between devices with their start and end apart: 16, of which 7 were waited for; matrix products, arithmetic and copies ran while one was open for 28% of the time, Pallas kernels for 0%

commit v1 on v0

v1 whole, which is shorter than its diff:
```python
import functools

import jax
import jax.numpy as jnp
from jax import lax
from jax.experimental import pallas as pl
from jax.experimental.pallas import tpu as pltpu
from jax.sharding import PartitionSpec as P

HEADS = 12
STEP = 10

NORM_EPSILON = 1e-12
CLIP_NORM = 1.0
BETA_ONE = 0.9
BETA_TWO = 0.999
ADAM_EPSILON = 1e-08
RATE_MATRIX = 0.04
RATE_VECTOR = 0.2
DECAY_RATE = 0.01
MASK_VALUE = -1e30
LOG2_E = 1.4426950408889634
BLOCK = 256
VMEM_BYTES = 56 * 2**20
F32 = jnp.float32
BF16 = jnp.bfloat16


def nn(left, right):
    return lax.dot_general(left, right, (((1,), (0,)), ((), ())), preferred_element_type=F32)


def nt(left, right):
    return lax.dot_general(left, right, (((1,), (1,)), ((), ())), preferred_element_type=F32)


def tn(left, right):
    return lax.dot_general(left, right, (((0,), (0,)), ((), ())), preferred_element_type=F32)


def lanes(block):
    return pl.ds(pl.multiple_of(block * BLOCK, BLOCK), BLOCK)


def live_blocks(len_ref):
    return (len_ref[0] + BLOCK - 1) // BLOCK


def for_size(blocks, most, body):
    for n in range(1, most + 1):
        pl.when(blocks == n)(functools.partial(body, n))


def norm_forward(resid):
    features = resid.shape[0]
    centred = resid - jnp.sum(resid, axis=0, keepdims=True) * (1.0 / features)
    variance = jnp.sum(centred * centred, axis=0, keepdims=True) * (1.0 / features)
    inverse = lax.rsqrt(variance + NORM_EPSILON)
    return centred * inverse, inverse


def norm_backward(scaled, normed, inverse):
    features = scaled.shape[0]
    mean = jnp.sum(scaled, axis=0, keepdims=True) * (1.0 / features)
    slope = jnp.sum(scaled * normed, axis=0, keepdims=True) * (1.0 / features)
    return inverse * (scaled - mean - normed * slope)


def mask_tail(scores, n, length):
    rows = (n - 1) * BLOCK + lax.broadcasted_iota(jnp.int32, (BLOCK, scores.shape[1]), 0)
    tail = jnp.where(rows < length, scores[(n - 1) * BLOCK :], MASK_VALUE)
    if n == 1:
        return tail
    return jnp.concatenate([scores[: (n - 1) * BLOCK], tail], axis=0)


def pad_rows(part, index, count):
    zeros = jnp.zeros_like(part)
    return jnp.concatenate([part if i == index else zeros for i in range(count)], axis=0)


def pad_lanes(pair, index, size):
    lane = lax.broadcasted_iota(jnp.int32, pair.shape, 1)
    return jnp.where((lane >= index * size) & (lane < (index + 1) * size), pair, jnp.zeros_like(pair))


def split_heads(flat, ref, columns, size):
    heads = flat.shape[0] // size
    for head in range(heads):
        ref[head, :, columns] = flat[head * size : (head + 1) * size]


def split_pairs(flat, ref, rows):
    pairs, width = ref.shape[0], ref.shape[2]
    for pair in range(pairs):
        ref[pair, rows, :] = flat[pair * width : (pair + 1) * width].T


def teacher_kernel(len_ref, rows_ref, weight_ref, qt_ref, k_ref, vt_ref, v_ref):
    flat = weight_ref.shape[0] // 3
    size = qt_ref.shape[1]

    def step(block, carry):
        where = lanes(block)
        rows = rows_ref[where, :]
        projected = nt(weight_ref[...], rows).astype(BF16)
        split_heads(projected[:flat], qt_ref, where, size)
        split_pairs(projected[flat : 2 * flat], k_ref, where)
        split_heads(projected[2 * flat :], vt_ref, where, size)
        split_pairs(projected[2 * flat :], v_ref, where)
        return carry

    lax.fori_loop(0, live_blocks(len_ref), step, 0)


def attend_kernel(
    len_ref, xt_ref, weight_ref, vec_ref, qt_ref, kt_ref, vt_ref, q_ref, k_ref, v_ref, ot_ref, lse_ref, at_ref,
    vone_ref,
):
    heads, size, rows = qt_ref.shape
    flat = heads * size
    scaling = LOG2_E * size ** (-0.5)
    blocks = live_blocks(len_ref)
    length = len_ref[0]
    vone_ref[...] = jnp.ones(vone_ref.shape, BF16)

    def project(block, carry):
        where = lanes(block)
        xt = xt_ref[:, where]
        projected = tn(weight_ref[:, : 3 * flat], xt)
        query = (projected[:flat] + vec_ref[:, 0:1]).astype(BF16)
        keys = projected[flat : 2 * flat].astype(BF16)
        values = (projected[2 * flat :] + vec_ref[:, 1:2]).astype(BF16)
        split_heads(query, qt_ref, where, size)
        split_heads(keys, kt_ref, where, size)
        split_heads(values, vt_ref, where, size)
        for head in range(heads):
            vone_ref[head, :size, where] = values[head * size : (head + 1) * size]
        split_pairs(query, q_ref, where)
        split_pairs(keys, k_ref, where)
        split_pairs(values, v_ref, where)
        return carry

    lax.fori_loop(0, blocks, project, 0)

    def attend(n):
        def step(index, carry):
            block, pair = index // (heads // 2), index % (heads // 2)
            where = lanes(block)
            keys = k_ref[pair, : n * BLOCK, :]
            for half in range(2):
                head = 2 * pair + half
                scores = nn(keys, pad_rows(qt_ref[head, :, where], half, 2))
                scores = mask_tail(scores, n, length)
                top = jnp.max(scores, axis=0, keepdims=True) * scaling
                grown = jnp.exp2(scores * scaling - top).astype(BF16)
                mixed = nn(vone_ref[head, :, : n * BLOCK], grown)
                total = mixed[size : size + 1]
                ot_ref[head, :, where] = mixed[:size] * (1.0 / total)
                lse_ref[head, :, where] = jnp.broadcast_to(top + jnp.log2(total), (8, BLOCK))
            return carry

        lax.fori_loop(0, n * (heads // 2), step, 0)

    for_size(blocks, rows // BLOCK, attend)

    def output(block, carry):
        where = lanes(block)
        mixed = ot_ref[:, :, where].reshape(flat, BLOCK).astype(BF16)
        at_ref[:, where] = nn(weight_ref[:, 3 * flat :], mixed).astype(BF16)
        return carry

    lax.fori_loop(0, blocks, output, 0)


def first_norm(xt, own, other, vec_ref):
    resid = xt.astype(F32) + (own.astype(F32) + other.astype(F32)) + vec_ref[:, 2:3]
    return norm_forward(resid)


def erf(value):
    return lax.erf(value)


def feed_kernel(len_ref, xt_ref, own_ref, other_ref, in_ref, out_ref, vec_ref, ht_ref, zt_ref, slope_ref, ft_ref):
    def step(block, carry):
        where = lanes(block)
        normed, _ = first_norm(xt_ref[:, where], own_ref[:, where], other_ref[:, where], vec_ref)
        hidden = normed * vec_ref[:, 3:4] + vec_ref[:, 4:5]
        ht_ref[:, where] = hidden
        pre = tn(in_ref[...], hidden.astype(BF16))
        cdf = 0.5 + 0.5 * erf(pre * (0.5**0.5))
        pdf = jnp.exp2(pre * pre * (-0.5 * LOG2_E)) * 0.3989422804014327
        active = (pre * cdf).astype(BF16)
        zt_ref[:, where] = active
        slope_ref[:, where] = (cdf + pre * pdf).astype(BF16)
        ft_ref[:, where] = nn(out_ref[...], active).astype(BF16)
        return carry

    lax.fori_loop(0, live_blocks(len_ref), step, 0)


def second_norm(ht, own, other, vec_ref):
    resid = ht + (own.astype(F32) + other.astype(F32)) + vec_ref[:, 5:6]
    return norm_forward(resid)


def relation_kernel(
    len_ref, weight_ref, ht_ref, own_ref, other_ref, rel_ref, vec_ref, tqt_ref, tk_ref, tvt_ref, tv_ref,
    grad_ref, dt_ref,
    h2_ref, qt_ref, kt_ref, vt_ref, q_ref, k_ref, v_ref, dqt_ref, dvt_ref, dk_ref, dv_ref,
):
    heads, size, rows = qt_ref.shape
    teacher_size = tqt_ref.shape[1]
    flat = heads * size
    plain = size ** (-0.5)
    scaling = LOG2_E * plain
    teacher_scaling = LOG2_E * teacher_size ** (-0.5)
    blocks = live_blocks(len_ref)
    length = len_ref[0]
    weight = weight_ref[0]

    def project(block, carry):
        where = lanes(block)
        normed, _ = second_norm(ht_ref[:, where], own_ref[:, where], other_ref[:, where], vec_ref)
        hidden = (normed * vec_ref[:, 6:7] + vec_ref[:, 7:8]).astype(BF16)
        h2_ref[:, where] = hidden
        projected = tn(rel_ref[...], hidden).astype(BF16)
        split_heads(projected[:flat], qt_ref, where, size)
        split_heads(projected[flat : 2 * flat], kt_ref, where, size)
        split_heads(projected[2 * flat :], vt_ref, where, size)
        split_pairs(projected[:flat], q_ref, where)
        split_pairs(projected[flat : 2 * flat], k_ref, where)
        split_pairs(projected[2 * flat :], v_ref, where)
        for pair in range(heads // 2):
            dk_ref[pair, where, :] = jnp.zeros((BLOCK, 2 * size), F32)
            dv_ref[pair, where, :] = jnp.zeros((BLOCK, 2 * size), F32)
        return carry

    lax.fori_loop(0, blocks, project, 0)

    def relate(n):
        def grown(left, right, scale):
            scores = mask_tail(nn(left, right), n, length)
            top = jnp.max(scores, axis=0, keepdims=True) * scale
            result = jnp.exp2(scores * scale - top)
            return result, jnp.sum(result, axis=0, keepdims=True)

        def step(index, carry):
            block, pair = index // (heads // 2), index % (heads // 2)
            where = lanes(block)
            column = block * BLOCK + lax.broadcasted_iota(jnp.int32, (1, BLOCK), 1)
            live = jnp.where(column < length, weight, 0.0)

            def relation(left, rightt, right, teacher_left, teacher_rightt, leftt, own_ref, running_ref):
                grads = []
                for half in range(2):
                    head = 2 * pair + half
                    student, student_sum = grown(
                        left[pair, : n * BLOCK, :], pad_rows(rightt[head, :, where], half, 2), scaling
                    )
                    teacher, teacher_sum = grown(
                        teacher_left[pair, : n * BLOCK, :],
                        pad_rows(teacher_rightt[head, :, where], half, 2),
                        teacher_scaling,
                    )
                    grad = (student * (live / student_sum) - teacher * (live / teacher_sum)).astype(BF16)
                    own_ref[head, :, where] = (nn(leftt[head, :, : n * BLOCK], grad) * plain).astype(own_ref.dtype)
                    grads.append(grad)
                queries = right[pair, where, :]
                stacked = jnp.concatenate([pad_lanes(queries, half, size) for half in range(2)], axis=0)
                running_ref[pair, : n * BLOCK, :] += nn(jnp.concatenate(grads, axis=1), stacked)

            relation(k_ref, qt_ref, q_ref, tk_ref, tqt_ref, kt_ref, dqt_ref, dk_ref)
            relation(v_ref, vt_ref, v_ref, tv_ref, tvt_ref, vt_ref, dvt_ref, dv_ref)
            return carry

        lax.fori_loop(0, n * (heads // 2), step, 0)

    for_size(blocks, rows // BLOCK, relate)
    grad_ref[...] = jnp.zeros(grad_ref.shape, F32)

    def finish(block, carry):
        where = lanes(block)
        queries = dqt_ref[:, :, where].reshape(flat, BLOCK)
        keys = jnp.concatenate([dk_ref[pair, where, :].T for pair in range(heads // 2)], axis=0) * plain
        values = jnp.concatenate([dv_ref[pair, where, :].T for pair in range(heads // 2)], axis=0) * plain
        values = values + dvt_ref[:, :, where].reshape(flat, BLOCK)
        grads = jnp.concatenate([queries, keys.astype(BF16), values.astype(BF16)], axis=0)
        grad_ref[...] += nt(h2_ref[:, where], grads)
        dt_ref[:, where] = nn(rel_ref[...], grads).astype(BF16)
        return carry

    lax.fori_loop(0, blocks, finish, 0)


def feed_back_kernel(
    len_ref, ht_ref, own_ref, other_ref, down_own_ref, down_other_ref, zt_ref, slope_ref, in_ref, out_ref, vec_ref,
    grad_in_ref, grad_out_ref, sums_ref, resid_ref, up_ref,
):
    grad_in_ref[...] = jnp.zeros(grad_in_ref.shape, F32)
    grad_out_ref[...] = jnp.zeros(grad_out_ref.shape, F32)
    sums_ref[...] = jnp.zeros(sums_ref.shape, F32)

    def step(block, carry):
        where = lanes(block)
        hidden = ht_ref[:, where]
        normed, inverse = second_norm(hidden, own_ref[:, where], other_ref[:, where], vec_ref)
        grad = down_own_ref[:, where].astype(F32) + down_other_ref[:, where].astype(F32)
        resid = norm_backward(grad * vec_ref[:, 6:7], normed, inverse)
        resid_ref[:, where] = resid
        sums_ref[:, 0:1] += jnp.sum(resid, axis=1, keepdims=True)
        sums_ref[:, 1:2] += jnp.sum(grad * normed, axis=1, keepdims=True)
        sums_ref[:, 2:3] += jnp.sum(grad, axis=1, keepdims=True)
        branch = resid.astype(BF16)
        grad_out_ref[...] += nt(branch, zt_ref[:, where])
        pre_grad = (tn(out_ref[...], branch) * slope_ref[:, where].astype(F32)).astype(BF16)
        grad_in_ref[...] += nt(hidden.astype(BF16), pre_grad)
        up_ref[:, where] = nn(in_ref[...], pre_grad).astype(BF16)
        return carry

    lax.fori_loop(0, live_blocks(len_ref), step, 0)


def attend_back_kernel(
    len_ref, xt_ref, own_ref, other_ref, resid_ref, up_own_ref, up_other_ref, weight_ref, vec_ref,
    qt_ref, kt_ref, q_ref, k_ref, v_ref, ot_ref, lse_ref,
    grad_ref, sums_ref, head_sums_ref,
    dot_ref, do_ref, inner_ref, dqt_ref, dk_ref, dv_ref,
):
    heads, size, rows = qt_ref.shape
    flat = heads * size
    plain = size ** (-0.5)
    scaling = LOG2_E * plain
    blocks = live_blocks(len_ref)
    length = len_ref[0]
    sums_ref[...] = jnp.zeros(sums_ref.shape, F32)
    head_sums_ref[...] = jnp.zeros(head_sums_ref.shape, F32)
    grad_ref[...] = jnp.zeros(grad_ref.shape, F32)

    def start(block, carry):
        where = lanes(block)
        normed, inverse = first_norm(xt_ref[:, where], own_ref[:, where], other_ref[:, where], vec_ref)
        grad = resid_ref[:, where] + (up_own_ref[:, where].astype(F32) + up_other_ref[:, where].astype(F32))
        branch = norm_backward(grad * vec_ref[:, 3:4], normed, inverse).astype(BF16)
        sums_ref[:, 0:1] += jnp.sum(branch.astype(F32), axis=1, keepdims=True)
        sums_ref[:, 1:2] += jnp.sum(grad * normed, axis=1, keepdims=True)
        sums_ref[:, 2:3] += jnp.sum(grad, axis=1, keepdims=True)
        mixed = ot_ref[:, :, where]
        grad_ref[:, 3 * flat :] += nt(branch, mixed.reshape(flat, BLOCK).astype(BF16))
        mixed_grad = tn(weight_ref[:, 3 * flat :], branch).astype(BF16)
        split_heads(mixed_grad, dot_ref, where, size)
        split_pairs(mixed_grad, do_ref, where)
        for head in range(heads):
            product = mixed_grad[head * size : (head + 1) * size].astype(F32) * mixed[head]
            inner_ref[head, :, where] = jnp.broadcast_to(jnp.sum(product, axis=0, keepdims=True), (8, BLOCK))
        for pair in range(heads // 2):
            dk_ref[pair, where, :] = jnp.zeros((BLOCK, 2 * size), F32)
            dv_ref[pair, where, :] = jnp.zeros((BLOCK, 2 * size), F32)
        return carry

    lax.fori_loop(0, blocks, start, 0)

    def attend(n):
        def step(index, carry):
            block, pair = index // (heads // 2), index % (heads // 2)
            where = lanes(block)
            probs, grads = [], []
            for half in range(2):
                head = 2 * pair + half
                scores = mask_tail(nn(k_ref[pair, : n * BLOCK, :], pad_rows(qt_ref[head, :, where], half, 2)), n, length)
                prob = jnp.exp2(scores * scaling - lse_ref[head, 0:1, where])
                prob_grad = nn(v_ref[pair, : n * BLOCK, :], pad_rows(dot_ref[head, :, where], half, 2))
                grad = (prob * (prob_grad - inner_ref[head, 0:1, where])).astype(BF16)
                dqt_ref[head, :, where] = (nn(kt_ref[head, :, : n * BLOCK], grad) * plain).astype(BF16)
                probs.append(prob.astype(BF16))
                grads.append(grad)
            for parts, right, running in ((grads, q_ref, dk_ref), (probs, do_ref, dv_ref)):
                queries = right[pair, where, :]
                stacked = jnp.concatenate([pad_lanes(queries, half, size) for half in range(2)], axis=0)
                running[pair, : n * BLOCK, :] += nn(jnp.concatenate(parts, axis=1), stacked)
            return carry

        lax.fori_loop(0, n * (heads // 2), step, 0)

    for_size(blocks, rows // BLOCK, attend)

    def finish(block, carry):
        where = lanes(block)
        queries = dqt_ref[:, :, where].reshape(flat, BLOCK)
        keys = jnp.concatenate([dk_ref[pair, where, :].T for pair in range(heads // 2)], axis=0) * plain
        values = jnp.concatenate([dv_ref[pair, where, :].T for pair in range(heads // 2)], axis=0).astype(BF16)
        head_sums_ref[:, 0:1] += jnp.sum(queries.astype(F32), axis=1, keepdims=True)
        head_sums_ref[:, 1:2] += jnp.sum(values.astype(F32), axis=1, keepdims=True)
        grads = jnp.concatenate([queries, keys.astype(BF16), values], axis=0)
        grad_ref[:, : 3 * flat] += nt(xt_ref[:, where], grads)
        return carry

    lax.fori_loop(0, blocks, finish, 0)


def call(kernel, name, scalars, arrays, outs, scratch=(), flops=0):
    vmem = pl.BlockSpec(memory_space=pltpu.VMEM)
    smem = pl.BlockSpec(memory_space=pltpu.SMEM)
    return pl.pallas_call(
        kernel,
        name=name,
        out_shape=tuple(jax.ShapeDtypeStruct(shape, dtype) for shape, dtype in outs),
        in_specs=[smem] * len(scalars) + [vmem] * len(arrays),
        out_specs=tuple(vmem for _ in outs),
        scratch_shapes=[pltpu.VMEM(shape, dtype) for shape, dtype in scratch],
        compiler_params=pltpu.CompilerParams(vmem_limit_bytes=VMEM_BYTES),
        cost_estimate=pl.CostEstimate(flops=flops, bytes_accessed=4 << 20, transcendentals=0),
    )(*scalars, *arrays)


def exchange(part):
    cores = lax.axis_size("ffn")
    return lax.ppermute(part, "ffn", [(core, core ^ 1) for core in range(cores)])


def adam_update(weight, gradient, first, second, clipped, rate, decay):
    scaled = gradient * clipped
    first_new = BETA_ONE * first + (1.0 - BETA_ONE) * scaled
    second_new = BETA_TWO * second + (1.0 - BETA_TWO) * scaled * scaled
    ratio = (
        first_new
        / (1.0 - BETA_ONE**STEP)
        / (jnp.sqrt(second_new / (1.0 - BETA_TWO**STEP)) + ADAM_EPSILON)
    )
    return (weight - rate * (ratio + decay * weight), first_new, second_new)


def per_device(
    states, teacher_states, lengths, domain_ids, domain_weight, teacher_qkv,
    attn_a, ffn_in, ffn_out, attn_b, vec_d,
    mom1_attn_a, mom1_ffn_in, mom1_ffn_out, mom1_attn_b, mom1_vec_d,
    mom2_attn_a, mom2_ffn_in, mom2_ffn_out, mom2_attn_b, mom2_vec_d,
):
    cores = lax.axis_size("ffn")
    core = lax.axis_index("ffn")
    replicas = lax.axis_size("dp")
    replica = lax.axis_index("dp")
    sequences = lengths.shape[0]
    rows = states.shape[0] // sequences
    features = states.shape[1]
    heads = HEADS // cores
    flat = features // cores
    size = flat // heads
    pairs = heads // 2
    hidden = ffn_in.shape[1]
    teacher_flat = teacher_qkv.shape[2]
    teacher_size = teacher_flat // heads
    shard = attn_a.shape[0]
    matched = domain_ids[:, None] == jnp.arange(domain_weight.shape[0])[None, :]
    sequence_weight = jnp.sum(jnp.where(matched, domain_weight[None, :], 0.0), axis=1) / HEADS

    attn_own = lax.dynamic_slice_in_dim(attn_a.reshape(shard, 4, features), core * flat, flat, 2).reshape(shard, 4 * flat)
    attn_full = lax.all_gather(attn_own.astype(BF16), "dp", axis=0, tiled=True)
    in_full = lax.all_gather(ffn_in.astype(BF16), "dp", axis=0, tiled=True)
    out_full = lax.all_gather(ffn_out.astype(BF16), "dp", axis=0, tiled=True)
    rel_full = lax.all_gather(attn_b.astype(BF16).reshape(shard, 3 * flat), "dp", axis=0, tiled=True)
    vec_full = lax.all_gather(vec_d.astype(BF16), "dp", axis=0, tiled=True).astype(F32)
    vec_own = lax.dynamic_slice_in_dim(vec_full, core * flat, flat, 0)
    teacher_w = teacher_qkv.reshape(teacher_qkv.shape[0], -1).T
    statest = states.T

    live = [lengths[i : i + 1] for i in range(sequences)]
    weights = [sequence_weight[i : i + 1] for i in range(sequences)]
    xt = [statest[:, i * rows : (i + 1) * rows] for i in range(sequences)]
    each = range(sequences)
    act = ((features, rows), BF16)
    wide = ((features, rows), F32)
    head_t = ((heads, size, rows), BF16)
    pair_rows = ((pairs, rows, 2 * size), BF16)

    teacher = [
        call(
            teacher_kernel, "teacher", (live[i],),
            (teacher_states[i * rows : (i + 1) * rows], teacher_w),
            (
                ((heads, teacher_size, rows), BF16),
                ((pairs, rows, 2 * teacher_size), BF16),
                ((heads, teacher_size, rows), BF16),
                ((pairs, rows, 2 * teacher_size), BF16),
            ),
            flops=2 * rows * 768 * 1152,
        )
        for i in each
    ]
    attended = [
        call(
            attend_kernel, "attend", (live[i],), (xt[i], attn_full, vec_own),
            (head_t, head_t, head_t, pair_rows, pair_rows, pair_rows, ((heads, size, rows), F32),
             ((heads, 8, rows), F32), act),
            scratch=(((heads, size + 16, rows), BF16),),
            flops=6 * 10**9,
        )
        for i in each
    ]
    mixed_other = [exchange(attended[i][8]) for i in each]
    fed = [
        call(
            feed_kernel, "feed", (live[i],),
            (xt[i], attended[i][8], mixed_other[i], in_full, out_full, vec_full),
            (wide, ((hidden, rows), BF16), ((hidden, rows), BF16), act),
            flops=3 * 10**9,
        )
        for i in each
    ]
    fed_other = [exchange(fed[i][3]) for i in each]
    related = [
        call(
            relation_kernel, "relation", (live[i], weights[i]),
            (fed[i][0], fed[i][3], fed_other[i], rel_full, vec_full, *teacher[i]),
            (((features, 3 * flat), F32), act),
            scratch=(
                act, head_t, head_t, head_t, pair_rows, pair_rows, pair_rows,
                head_t, ((heads, size, rows), F32),
                ((pairs, rows, 2 * size), F32), ((pairs, rows, 2 * size), F32),
            ),
            flops=30 * 10**9,
        )
        for i in each
    ]
    down_other = [exchange(related[i][1]) for i in each]
    fed_back = [
        call(
            feed_back_kernel, "feed_back", (live[i],),
            (fed[i][0], fed[i][3], fed_other[i], related[i][1], down_other[i], fed[i][1], fed[i][2],
             in_full, out_full, vec_full),
            (((features, hidden), F32), ((features, hidden), F32), ((features, 8), F32), wide, act),
            flops=4 * 10**9,
        )
        for i in each
    ]
    up_other = [exchange(fed_back[i][4]) for i in each]
    attended_back = [
        call(
            attend_back_kernel, "attend_back", (live[i],),
            (xt[i], attended[i][8], mixed_other[i], fed_back[i][3], fed_back[i][4], up_other[i], attn_full, vec_full,
             attended[i][0], attended[i][1], attended[i][3], attended[i][4], attended[i][5], attended[i][6],
             attended[i][7]),
            (((features, 4 * flat), F32), ((features, 8), F32), ((flat, 8), F32)),
            scratch=(
                head_t, pair_rows, ((heads, 8, rows), F32), head_t,
                ((pairs, rows, 2 * size), F32), ((pairs, rows, 2 * size), F32),
            ),
            flops=15 * 10**9,
        )
        for i in each
    ]

    def total(parts):
        result = parts[0]
        for part in parts[1:]:
            result = result + part
        return result

    def scatter(value):
        return lax.psum_scatter(value, "dp", scatter_dimension=0, tiled=True)

    shard_rel = scatter(total([related[i][0] for i in each]))
    shard_in = scatter(total([fed_back[i][0] for i in each]))
    shard_out = scatter(total([fed_back[i][1] for i in each]))
    shard_attn = scatter(total([attended_back[i][0] for i in each]))
    back_sums = total([fed_back[i][2] for i in each])
    first_sums = total([attended_back[i][1] for i in each])
    head_sums = total([attended_back[i][2] for i in each])
    placed = lax.dynamic_update_slice_in_dim(jnp.zeros((features, 2), F32), head_sums[:, :2] * cores, core * flat, 0)
    vec_local = jnp.concatenate(
        [placed, first_sums[:, :3], back_sums[:, :3]], axis=1
    )
    vec_total = lax.psum(vec_local, ("dp", "ffn")) / cores
    grad_vec = lax.dynamic_slice_in_dim(vec_total, replica * shard, shard, 0)
    halves = lax.all_gather(shard_attn.reshape(shard, 4, flat), "ffn", axis=2, tiled=True)
    grad_attn = halves.reshape(shard, 4 * features)
    grad_rel = shard_rel.reshape(attn_b.shape)
    gradients = (grad_attn, shard_in, shard_out, grad_rel, grad_vec)
    squares = (
        (jnp.sum(grad_attn * grad_attn) + jnp.sum(grad_vec * grad_vec)) / cores
        + jnp.sum(shard_in * shard_in)
        + jnp.sum(shard_out * shard_out)
        + jnp.sum(shard_rel * shard_rel)
    )
    grad_norm = jnp.sqrt(lax.psum(squares, ("dp", "ffn")))
    clipped = jnp.minimum(1.0, CLIP_NORM / grad_norm)
    masters = (attn_a, ffn_in, ffn_out, attn_b, vec_d)
    firsts = (mom1_attn_a, mom1_ffn_in, mom1_ffn_out, mom1_attn_b, mom1_vec_d)
    seconds = (mom2_attn_a, mom2_ffn_in, mom2_ffn_out, mom2_attn_b, mom2_vec_d)
    rates = (RATE_MATRIX, RATE_MATRIX, RATE_MATRIX, RATE_MATRIX, RATE_VECTOR)
    decays = (DECAY_RATE, DECAY_RATE, DECAY_RATE, DECAY_RATE, 0.0)
    news = [
        adam_update(masters[i], gradients[i], firsts[i], seconds[i], clipped, rates[i], decays[i])
        for i in range(5)
    ]
    return (grad_norm, *(new[0] for new in news), *(new[1] for new in news), *(new[2] for new in news))


def solution(mesh):
    matrix = P("dp", None)
    halved = P("dp", "ffn")
    cube = P("dp", None, "ffn")
    trained = (matrix, halved, halved, cube, matrix)
    in_specs = (matrix, matrix, P("dp"), P("dp"), P(), P(None, None, "ffn")) + trained * 3
    out_specs = (P(),) + trained * 3
    return jax.shard_map(per_device, mesh=mesh, in_specs=in_specs, out_specs=out_specs, check_vma=False)
```

time: 1690 us -> 1010 us (0.60)
  matrix products: 490 us -> 0 us
  other arithmetic: 260 us -> 18.5 us
  Pallas kernels: 0 us -> 201 us
  local copies, waits for them, and re-layouts: 117 us -> 18.5 us
  blocking collectives: 302 us -> 379 us
  waiting for transfers between devices: 434 us -> 363 us
  loops' own time: 50.3 us -> 0 us
    dot_general x66 -> x0, matrix products: 312 us -> none  [the longest x8 55.4 us: logits(): jnp.einsum('qhd,khd->hqk', left, right, preferred_element_type=jnp.float32)]
    pallas_call x0 -> x12, Pallas kernels: none -> 201 us  [call(): pl.pallas_call(kernel, name=name, out_shape=tuple((jax.ShapeDtypeStruct(s...]
    div x20 -> x0, other arithmetic: 177 us -> none  [the longest x4 88.6 us: one_block(): jax.nn.softmax(logits(value_block, values, student_scale), axis=-1)]
    psum x1, blocking collectives: 2.44 us -> 111 us  [per_device(): vec_total = lax.psum(vec_local, ('dp', 'ffn')) / cores]
    sub x10 -> x0, matrix products: 102 us -> none  [the longest x4 36.8 us: one_block(): jax.nn.softmax(logits(teacher_vblock, teacher_values, teacher_scale), axi...]
    div x8 -> x0, matrix products: 76.3 us -> none  [the longest x4 38.2 us: one_block(): jax.nn.softmax(logits(teacher_vblock, teacher_values, teacher_scale), axi...]
    unnamed x1 -> x0, blocking collectives: 75.1 us -> none
    dynamic_update_slice x16 -> x1, local copies, waits for them, and re-layouts: 69 us -> 0.16 us  [per_device(): lax.dynamic_update_slice_in_dim(jnp.zeros((features, 2), F32), head_sums[...]
  transfers between devices with their start and end apart: 16 -> 12, of which waited for: 7 -> 5; matrix products, arithmetic and copies ran while one was open for 28% -> 2% of each run, Pallas kernels for 0% -> 13%
where the time goes in v1:
time: 1010 us; the launch traced here: 1000 us
  blocking collectives  379 us (38%)
  waiting for transfers between devices  363 us (36%)
  Pallas kernels  201 us (20%)
  between operations  19.8 us (2%)
  local copies, waits for them, and re-layouts  18.5 us (2%)
  other arithmetic  18.5 us (2%)
    reduce_scatter x3, waiting for transfers between devices, scatter(): return lax.psum_scatter(value, 'dp', scatter_dimension=0, tiled=True)  361 us
    pallas_call x12, Pallas kernels, call(): pl.pallas_call(kernel, name=name, out_shape=tuple((jax.ShapeDtypeStruct(s...  201 us
    psum x1, blocking collectives, per_device(): vec_total = lax.psum(vec_local, ('dp', 'ffn')) / cores  111 us
    all_gather x1, blocking collectives, per_device(): in_full = lax.all_gather(ffn_in.astype(BF16), 'dp', axis=0, tiled=True)  56.1 us
    all_gather x1, blocking collectives, per_device(): attn_full = lax.all_gather(attn_own.astype(BF16), 'dp', axis=0, tiled=True)  48.3 us
    all_gather x1, blocking collectives, per_device(): lax.all_gather(attn_b.astype(BF16).reshape(shard, 3 * flat), 'dp', axis=0...  45.4 us
    all_gather x1, blocking collectives, per_device(): out_full = lax.all_gather(ffn_out.astype(BF16), 'dp', axis=0, tiled=True)  41.2 us
    psum x1, blocking collectives, per_device(): grad_norm = jnp.sqrt(lax.psum(squares, ('dp', 'ffn')))  39.9 us
  transfers between devices with their start and end apart: 12, of which 5 were waited for; matrix products, arithmetic and copies ran while one was open for 2% of the time, Pallas kernels for 13%

profile of v1, /device:TPU:0, one launch (start us, length us, event | category | flops | bytes accessed | tf_op | source)
XLA Modules:
  0.0 1003.0 jit_solution(3286990085368735253)
XLA Ops:
  8.5 1.7 copy.119
  11.9 48.3 %all_gather.18.weight_ref = bf16[384,768]{1,0:T(8,128)(2,1)} all-gather(bf16[24,768]{1,0:T(8,128)(2,1)S(1)} %convert_element_type.22), channel_id=1, replica_groups=mesh['dp'=16,'ffn'=2] {'dp'}, dimensions={0}, use_global_device_ids=true | all-gather | bytes 626688 | tf_op jit(solution)/shard_map/all_gather | solution.py:459
  60.2 35.6 %all-gather = bf16[16,24,8]{1,2,0:T(8,128)(2,1)S(1)} all-gather(bf16[1,24,8]{1,2,0:T(8,128)(2,1)S(1)} %convert_bitcast_fusion), channel_id=1, replica_groups=mesh['dp'=16,'ffn'=2] {'dp'}, dimensions={0}, use_global_device_ids=true | all-gather | bytes 6528 | tf_op jit(solution)/shard_map/all_gather | solution.py:463
  96.6 7.1 attend.2
  103.8 24.9 %attend.3 = (bf16[6,32,1024]{2,1,0:T(8,128)(2,1)}, bf16[6,32,1024]{2,1,0:T(8,128)(2,1)}, bf16[6,32,1024]{2,1,0:T(8,128)(2,1)}, bf16[3,1024,64]{2,1,0:T(8,128)(2,...) custom-call(s32[1]{0:T(128)} %get-tuple-element.221.len_ref, ...), custom_call_target="tpu_custom_call" | custom-call | flops 6000000000 | bytes 4194304 | tf_op jit(solution)/shard_map/attend/pallas_call | solution.py:405
  129.2 56.1 %all_gather.20.in_ref = bf16[384,768]{1,0:T(8,128)(2,1)} all-gather(bf16[24,768]{1,0:T(8,128)(2,1)S(1)} %convert_element_type.25), channel_id=1, replica_groups=mesh['dp'=16,'ffn'=2] {'dp'}, dimensions={0}, use_global_device_ids=true | all-gather | bytes 626688 | tf_op jit(solution)/shard_map/all_gather | solution.py:460
  185.3 4.0 copy.122
  189.5 41.2 %all_gather.21.out_ref = bf16[384,768]{1,0:T(8,128)(2,1)} all-gather(bf16[24,768]{1,0:T(8,128)(2,1)S(1)} %convert_element_type.26), channel_id=1, replica_groups=mesh['dp'=16,'ffn'=2] {'dp'}, dimensions={0}, use_global_device_ids=true | all-gather | bytes 626688 | tf_op jit(solution)/shard_map/all_gather | solution.py:461
  230.6 1.9 fusion.11
  232.6 6.2 feed.2
  238.8 5.0 teacher.2
  244.5 7.1 teacher.3
  251.6 45.4 %all_gather.22.rel_ref = bf16[384,576]{1,0:T(8,128)(2,1)} all-gather(bf16[24,576]{1,0:T(8,128)(2,1)S(1)} %reshape.55), channel_id=1, replica_groups=mesh['dp'=16,'ffn'=2] {'dp'}, dimensions={0}, use_global_device_ids=true | all-gather | bytes 470016 | tf_op jit(solution)/shard_map/all_gather | solution.py:462
  297.0 10.1 %feed.3 = (f32[384,1024]{1,0:T(8,128)}, bf16[768,1024]{1,0:T(8,128)(2,1)}, bf16[768,1024]{1,0:T(8,128)(2,1)}, bf16[384,1024]{1,0:T(8,128)(2,1)}) custom-call(s32[1]{0:T(128)} %get-tuple-element.221.len_ref, bf16[384,1024]{1,0:T(8,128)(2,1)} %get-tuple-element.217.xt_ref, bf16[384,1024]{1,0:T(8,128)(2,1)} %get-tuple-element.88.own_ref, ...), custom_call_target="tpu_custom_call" | custom-call | flops 3000000000 | bytes 4194304 | tf_op jit(solution)/shard_map/feed/pallas_call | solution.py:405
  307.9 12.4 %relation.2 = (f32[384,576]{1,0:T(8,128)}, bf16[384,1024]{1,0:T(8,128)(2,1)}) custom-call(s32[1]{0:T(128)} %get-tuple-element.222.len_ref, f32[1]{0:T(128)} %get-tuple-element.220.weight_ref, f32[384,1024]{1,0:T(8,128)} %get-tuple-element.69.ht_ref, bf16[384,1024]{1,0:T(8,128)(2,1)} %get-tuple-element.70.own_ref, bf16[384,1024]{1,0:T(8,128)(2,1)} %copy-done.31, ...), custom_call_target="tpu_custom_call" | custom-call | flops 30000001024 | bytes 4194304 | tf_op jit(solution)/shard_map/relation/pallas_call | solution.py:405
  321.2 66.1 %relation.3 = (f32[384,576]{1,0:T(8,128)}, bf16[384,1024]{1,0:T(8,128)(2,1)}) custom-call(s32[1]{0:T(128)} %get-tuple-element.221.len_ref, f32[1]{0:T(128)} %get-tuple-element.219.weight_ref, f32[384,1024]{1,0:T(8,128)} %get-tuple-element.89.ht_ref, bf16[384,1024]{1,0:T(8,128)(2,1)} %get-tuple-element.90.own_ref, bf16[384,1024]{1,0:T(8,128)(2,1)} %copy-done.33, ...), custom_call_target="tpu_custom_call" | custom-call | flops 30000001024 | bytes 4194304 | tf_op jit(solution)/shard_map/relation/pallas_call | solution.py:405
  387.3 2.5 add.133
  390.5 1.8 collective-permute-done.2.down_other_ref
  393.3 8.3 feed_back.2
  402.4 13.6 %feed_back.3 = (f32[384,768]{1,0:T(8,128)}, f32[384,768]{1,0:T(8,128)}, f32[384,8]{1,0:T(8,128)}, f32[384,1024]{1,0:T(8,128)}, bf16[384,1024]{1,0:T(8,128)(2,1)}) custom-call(s32[1]{0:T(128)} %get-tuple-element.221.len_ref, f32[384,1024]{1,0:T(8,128)} %get-tuple-element.89.ht_ref, bf16[384,1024]{1,0:T(8,128)(2,1)} %get-tuple-element.90.own_ref, ...), custom_call_target="tpu_custom_call" | custom-call | flops 4000000000 | bytes 4194304 | tf_op jit(solution)/shard_map/feed_back/pallas_call | solution.py:405
  416.1 2.7 add.129
  421.8 9.4 attend_back.2
  431.2 30.9 %attend_back.3 = (f32[384,768]{1,0:T(8,128)}, f32[384,8]{1,0:T(8,128)}, f32[192,8]{1,0:T(8,128)}) custom-call(s32[1]{0:T(128)} %get-tuple-element.221.len_ref, bf16[384,1024]{1,0:T(8,128)(2,1)} %get-tuple-element.217.xt_ref, bf16[384,1024]{1,0:T(8,128)(2,1)} %get-tuple-element.88.own_ref, bf16[384,1024]{1,0:T(8,128)(2,1)} %collective-permute-done.4.other_ref, ...), custom_call_target="tpu_custom_call" | custom-call | flops 15000000512 | bytes 4194304 | tf_op jit(solution)/shard_map/attend_back/pallas_call | solution.py:405
  462.2 2.6 add.123
  466.3 110.5 %psum.14 = f32[384,8]{0,1:T(8,128)S(1)} all-reduce(f32[384,8]{0,1:T(8,128)S(1)} %pad_maximum_fusion), channel_id=1, replica_groups=mesh['dp'=16,'ffn'=2] {'dp','ffn'}, use_global_device_ids=true, to_apply=%region_3.4 | all-reduce | flops 3072 | bytes 24576 | tf_op jit(solution)/shard_map/psum | solution.py:574
  578.9 107.6 %reduce-scatter.9.cloned.1.call-done = f32[24,768]{1,0:T(8,128)} async-done(((f32[384,768]{1,0:T(8,128)}), f32[24,768]{1,0:T(8,128)}) %reduce-scatter.9.cloned.1.call-update) | async-done | bytes 73744 | tf_op jit(solution)/shard_map/reduce_scatter | solution.py:561
  686.5 1.5 multiply_reduce_fusion.2
  688.0 126.6 %reduce-scatter.11.cloned.1.call-done = f32[24,768]{1,0:T(8,128)} async-done(((f32[384,768]{1,0:T(8,128)}), f32[24,768]{1,0:T(8,128)}) %reduce-scatter.11.cloned.1.call-update) | async-done | bytes 73744 | tf_op jit(solution)/shard_map/reduce_scatter | solution.py:561
  814.6 1.5 multiply_reduce_fusion.1
  816.1 126.5 %reduce-scatter.7.cloned.1.call-done = f32[24,768]{1,0:T(8,128)} async-done(((f32[384,768]{1,0:T(8,128)}), f32[24,768]{1,0:T(8,128)}) %reduce-scatter.7.cloned.1.call-update) | async-done | bytes 73744 | tf_op jit(solution)/shard_map/reduce_scatter | solution.py:561
  943.8 2.5 all_gather.23
  950.9 39.9 %psum.15 = f32[]{:T(128)} all-reduce(f32[]{:T(128)S(6)} %add.134), channel_id=1, replica_groups=mesh['dp'=16,'ffn'=2] {'dp','ffn'}, use_global_device_ids=true, to_apply=%region_11.12 | all-reduce | flops 1 | bytes 8 | tf_op jit(solution)/shard_map/psum | solution.py:586
  (145 shorter events, 21.7 us)
Async XLA Ops:
  7.2 570.3 %reduce-scatter.13.cloned.1.call-start = ((), (), s32[]{:S(2)}) async-start(), calls=%async_computation.7 | async-start | bytes 1044480
  10.3 49.9 %copy-start.28 = (f32[24,8]{0,1:T(8,128)S(1)}, f32[24,8]{0,1:T(8,128)}, u32[]{:S(2)}) copy-start(f32[24,8]{0,1:T(8,128)} %param.31) | copy-start | bytes 2308
  103.7 128.8 %collective-permute-start = (bf16[384,1024]{1,0:T(8,128)(2,1)}, bf16[384,1024]{1,0:T(8,128)(2,1)}, u32[]{:S(2)}, u32[]{:S(2)}) collective-permute-start(bf16[384,1024]{1,0:T(8,128)(2,1)} %get-tuple-element.68.own_ref), channel_id=1, source_target_pairs={{0,1},{1,0},{2,3},{3,2},{4,5},{5,4},{6,7},{7,6},{8,9},{9,8},{10,11... | collective-permute-start | bytes 2359304 | tf_op jit(solution)/shard_map/ppermute | solution.py:419
  103.7 25.4 %copy-start.8 = (f32[24,768]{1,0:T(8,128)S(1)}, f32[24,768]{1,0:T(8,128)}, u32[]{:S(2)}) copy-start(f32[24,768]{1,0:T(8,128)} %param.28) | copy-start | bytes 221188
  103.7 81.5 %copy-start.9 = (f32[24,768]{1,0:T(8,128)S(1)}, f32[24,768]{1,0:T(8,128)}, u32[]{:S(2)}) copy-start(f32[24,768]{1,0:T(8,128)} %param.29) | copy-start | bytes 221188
  128.7 168.3 %collective-permute-start.4 = (bf16[384,1024]{1,0:T(8,128)(2,1)}, bf16[384,1024]{1,0:T(8,128)(2,1)}, u32[]{:S(2)}, u32[]{:S(2)}) collective-permute-start(bf16[384,1024]{1,0:T(8,128)(2,1)} %get-tuple-element.88.own_ref), channel_id=1, source_target_pairs={{0,1},{1,0},{2,3},{3,2},{4,5},{5,4},{6,7},{7,6},{8,9},{9,8},{10,11... | collective-permute-start | bytes 2359304 | tf_op jit(solution)/shard_map/ppermute | solution.py:419
  185.3 45.4 %copy-start = (bf16[2048,768]{1,0:T(8,128)(2,1)S(1)}, bf16[2048,768]{1,0:T(8,128)(2,1)}, u32[]{:S(2)}) copy-start(bf16[2048,768]{1,0:T(8,128)(2,1)} %param.22) | copy-start | bytes 9437188
  238.7 68.3 %collective-permute-start.1 = (bf16[384,1024]{1,0:T(8,128)(2,1)}, bf16[384,1024]{1,0:T(8,128)(2,1)S(1)}, u32[]{:S(2)}, u32[]{:S(2)}) collective-permute-start(bf16[384,1024]{1,0:T(8,128)(2,1)} %get-tuple-element.70.own_ref), channel_id=1, source_target_pairs={{0,1},{1,0},{2,3},{3,2},{4,5},{5,4},{6,7},{7,6},{8,9},{9,8},{10,11... | collective-permute-start | bytes 2359304 | tf_op jit(solution)/shard_map/ppermute | solution.py:419
  307.0 13.3 %collective-permute-start.5 = (bf16[384,1024]{1,0:T(8,128)(2,1)}, bf16[384,1024]{1,0:T(8,128)(2,1)S(1)}, u32[]{:S(2)}, u32[]{:S(2)}) collective-permute-start(bf16[384,1024]{1,0:T(8,128)(2,1)} %get-tuple-element.90.own_ref), channel_id=1, source_target_pairs={{0,1},{1,0},{2,3},{3,2},{4,5},{5,4},{6,7},{7,6},{8,9},{9,8},{10,11... | collective-permute-start | bytes 2359304 | tf_op jit(solution)/shard_map/ppermute | solution.py:419
  321.2 66.1 %copy-start.5 = (f32[384,576]{1,0:T(8,128)S(1)}, f32[384,576]{1,0:T(8,128)}, u32[]{:S(2)}) copy-start(f32[384,576]{1,0:T(8,128)} %get-tuple-element.118) | copy-start | bytes 2654212
  389.8 296.7 %reduce-scatter.9.cloned.1.call-start = ((), (), s32[]{:S(2)}) async-start(), calls=%async_computation.5 | async-start | bytes 1253376 | tf_op jit(solution)/shard_map/reduce_scatter | solution.py:561
  389.9 2.5 collective-permute-start.2
  390.5 11.1 %collective-permute-start.6 = (bf16[384,1024]{1,0:T(8,128)(2,1)S(1)}, bf16[384,1024]{1,0:T(8,128)(2,1)S(1)}, u32[]{:S(2)}, u32[]{:S(2)}) collective-permute-start(bf16[384,1024]{1,0:T(8,128)(2,1)S(1)} %copy-done.34), channel_id=1, source_target_pairs={{0,1},{1,0},{2,3},{3,2},{4,5},{5,4},{6,7},{7,6},{8,9},{9,8},{10,11... | collective-permute-start | bytes 2359304 | tf_op jit(solution)/shard_map/ppermute | solution.py:419
  402.4 13.7 %copy-start.4 = (f32[384,768]{1,0:T(8,128)S(1)}, f32[384,768]{1,0:T(8,128)}, u32[]{:S(2)}) copy-start(f32[384,768]{1,0:T(8,128)} %get-tuple-element.114) | copy-start | bytes 3538948
  418.8 395.8 %reduce-scatter.11.cloned.1.call-start = ((), (), s32[]{:S(2)}) async-start(), calls=%async_computation.6 | async-start | bytes 1253376 | tf_op jit(solution)/shard_map/reduce_scatter | solution.py:561
  419.1 2.7 collective-permute-start.3
  419.5 11.7 %collective-permute-start.7 = (bf16[384,1024]{1,0:T(8,128)(2,1)S(1)}, bf16[384,1024]{1,0:T(8,128)(2,1)}, u32[]{:S(2)}, u32[]{:S(2)}) collective-permute-start(bf16[384,1024]{1,0:T(8,128)(2,1)S(1)} %copy-done.32), channel_id=1, source_target_pairs={{0,1},{1,0},{2,3},{3,2},{4,5},{5,4},{6,7},{7,6},{8,9},{9,8},{10,11... | collective-permute-start | bytes 2359304 | tf_op jit(solution)/shard_map/ppermute | solution.py:419
  420.9 521.7 %reduce-scatter.7.cloned.1.call-start = ((), (), s32[]{:S(2)}) async-start(), calls=%async_computation.4 | async-start | bytes 1253376 | tf_op jit(solution)/shard_map/reduce_scatter | solution.py:561
  431.2 30.9 %copy-start.2 = (f32[384,768]{1,0:T(8,128)S(1)}, f32[384,768]{1,0:T(8,128)}, u32[]{:S(2)}) copy-start(f32[384,768]{1,0:T(8,128)} %get-tuple-element.87) | copy-start | bytes 3538948
  943.8 47.8 %copy-start.13 = (f32[24,576]{1,0:T(8,128)S(1)}, f32[24,576]{1,0:T(8,128)}, u32[]{:S(2)}) copy-start(f32[24,576]{1,0:T(8,128)} %reduce-scatter.13.cloned.1.call-done) | copy-start | bytes 165892
  946.3 45.4 %copy-start.29 = (f32[24,8]{0,1:T(8,128)S(1)}, f32[24,8]{0,1:T(8,128)}, u32[]{:S(2)}) copy-start(f32[24,8]{0,1:T(8,128)} %param.36) | copy-start | bytes 2308
  946.3 45.4 %copy-start.30 = (f32[24,8]{0,1:T(8,128)S(1)}, f32[24,8]{0,1:T(8,128)}, u32[]{:S(2)}) copy-start(f32[24,8]{0,1:T(8,128)} %param.41) | copy-start | bytes 2308
  946.3 46.1 %copy-start.18 = (f32[24,1536]{1,0:T(8,128)S(1)}, f32[24,1536]{1,0:T(8,128)}, u32[]{:S(2)}) copy-start(f32[24,1536]{1,0:T(8,128)} %param.32) | copy-start | bytes 442372
  946.3 46.1 %copy-start.19 = (f32[24,1536]{1,0:T(8,128)S(1)}, f32[24,1536]{1,0:T(8,128)}, u32[]{:S(2)}) copy-start(f32[24,1536]{1,0:T(8,128)} %param.37) | copy-start | bytes 442372
  947.3 45.9 %copy-start.26 = (f32[24,3,192]{2,0,1:T(8,128)S(1)}, f32[24,3,192]{2,0,1:T(8,128)}, u32[]{:S(2)}) copy-start(f32[24,3,192]{2,0,1:T(8,128)} %param.35) | copy-start | bytes 165892
  947.3 45.9 %copy-start.27 = (f32[24,3,192]{2,0,1:T(8,128)S(1)}, f32[24,3,192]{2,0,1:T(8,128)}, u32[]{:S(2)}) copy-start(f32[24,3,192]{2,0,1:T(8,128)} %param.40) | copy-start | bytes 165892
  950.6 43.4 %copy-start.10 = (f32[24,768]{1,0:T(8,128)S(1)}, f32[24,768]{1,0:T(8,128)}, u32[]{:S(2)}) copy-start(f32[24,768]{1,0:T(8,128)} %reduce-scatter.9.cloned.1.call-done) | copy-start | bytes 221188
  950.6 43.4 %copy-start.11 = (f32[24,768]{1,0:T(8,128)S(1)}, f32[24,768]{1,0:T(8,128)}, u32[]{:S(2)}) copy-start(f32[24,768]{1,0:T(8,128)} %reduce-scatter.11.cloned.1.call-done) | copy-start | bytes 221188
  950.6 43.4 %copy-start.22 = (f32[24,768]{1,0:T(8,128)S(1)}, f32[24,768]{1,0:T(8,128)}, u32[]{:S(2)}) copy-start(f32[24,768]{1,0:T(8,128)} %param.34) | copy-start | bytes 221188
  950.6 43.4 %copy-start.23 = (f32[24,768]{1,0:T(8,128)S(1)}, f32[24,768]{1,0:T(8,128)}, u32[]{:S(2)}) copy-start(f32[24,768]{1,0:T(8,128)} %param.39) | copy-start | bytes 221188
  950.7 43.4 %copy-start.24 = (f32[24,768]{1,0:T(8,128)S(1)}, f32[24,768]{1,0:T(8,128)}, u32[]{:S(2)}) copy-start(f32[24,768]{1,0:T(8,128)} %param.38) | copy-start | bytes 221188
  950.7 43.4 %copy-start.25 = (f32[24,768]{1,0:T(8,128)S(1)}, f32[24,768]{1,0:T(8,128)}, u32[]{:S(2)}) copy-start(f32[24,768]{1,0:T(8,128)} %param.33) | copy-start | bytes 221188
  (20 other events, 51.8 us)
Sparse Core Ops, SparseCore 0:
  389.9 168.3 reduce-scatter.12
  563.1 123.3 reduce-scatter.8
  691.3 123.2 reduce-scatter.10
  819.2 123.3 reduce-scatter.6

commit v2 on v1

v2 whole, which is shorter than its diff:
```python
import functools

import jax
import jax.numpy as jnp
from jax import lax
from jax.experimental import pallas as pl
from jax.experimental.pallas import tpu as pltpu
from jax.sharding import PartitionSpec as P

HEADS = 12
STEP = 10

NORM_EPSILON = 1e-12
CLIP_NORM = 1.0
BETA_ONE = 0.9
BETA_TWO = 0.999
ADAM_EPSILON = 1e-08
RATE_MATRIX = 0.04
RATE_VECTOR = 0.2
DECAY_RATE = 0.01
MASK_VALUE = -1e30
LOG2_E = 1.4426950408889634
BLOCK = 256
SAFE_EXPONENT = 100.0
VMEM_BYTES = 56 * 2**20
F32 = jnp.float32
BF16 = jnp.bfloat16


def nn(left, right):
    return lax.dot_general(left, right, (((1,), (0,)), ((), ())), preferred_element_type=F32)


def nt(left, right):
    return lax.dot_general(left, right, (((1,), (1,)), ((), ())), preferred_element_type=F32)


def tn(left, right):
    return lax.dot_general(left, right, (((0,), (0,)), ((), ())), preferred_element_type=F32)


def lanes(block):
    return pl.ds(pl.multiple_of(block * BLOCK, BLOCK), BLOCK)


def live_blocks(len_ref):
    return (len_ref[0] + BLOCK - 1) // BLOCK


def for_size(blocks, most, safe, fast, slow):
    for n in range(1, most + 1):
        pl.when(jnp.logical_and(safe, blocks == n))(functools.partial(fast, n))
    pl.when(jnp.logical_not(safe))(slow)


def pipeline(count, first, second, third):
    firsts, seconds = {}, {}
    for t in range(count + 2):
        if t < count:
            firsts[t] = first(t)
        if 0 <= t - 1 < count:
            seconds[t - 1] = second(t - 1, firsts.pop(t - 1))
        if 0 <= t - 2 < count:
            third(t - 2, seconds.pop(t - 2))


def squared_lengths(flat, size):
    features = flat.shape[0]
    groups = -(-features // size // 8) * 8
    row = lax.broadcasted_iota(jnp.int32, (groups, features), 0)
    column = lax.broadcasted_iota(jnp.int32, (groups, features), 1)
    ones = jnp.where((column >= row * size) & (column < (row + 1) * size), 1.0, 0.0).astype(BF16)
    return nn(ones, flat * flat)


def clear_dead(blocks, rows, *refs):
    def step(block, carry):
        for ref in refs:
            ref[:, :, lanes(block)] = jnp.zeros(ref.shape[:2] + (BLOCK,), ref.dtype)
        return carry

    lax.fori_loop(blocks, rows // BLOCK, step, 0)


def norm_forward(resid):
    features = resid.shape[0]
    centred = resid - jnp.sum(resid, axis=0, keepdims=True) * (1.0 / features)
    variance = jnp.sum(centred * centred, axis=0, keepdims=True) * (1.0 / features)
    inverse = lax.rsqrt(variance + NORM_EPSILON)
    return centred * inverse, inverse


def norm_backward(scaled, normed, inverse):
    features = scaled.shape[0]
    mean = jnp.sum(scaled, axis=0, keepdims=True) * (1.0 / features)
    slope = jnp.sum(scaled * normed, axis=0, keepdims=True) * (1.0 / features)
    return inverse * (scaled - mean - normed * slope)


def mask_tail(scores, n, length, start=None):
    start = (n - 1) * BLOCK if start is None else start
    rows = start + lax.broadcasted_iota(jnp.int32, (n * BLOCK - start, scores.shape[1]), 0)
    tail = jnp.where(rows < length, scores[start:], MASK_VALUE)
    if start == 0:
        return tail
    return jnp.concatenate([scores[:start], tail], axis=0)


def pad_rows(part, index, count):
    zeros = jnp.zeros_like(part)
    return jnp.concatenate([part if i == index else zeros for i in range(count)], axis=0)


def pad_lanes(pair, index, size):
    lane = lax.broadcasted_iota(jnp.int32, pair.shape, 1)
    return jnp.where((lane >= index * size) & (lane < (index + 1) * size), pair, jnp.zeros_like(pair))


def split_heads(flat, ref, columns, size):
    heads = flat.shape[0] // size
    for head in range(heads):
        ref[head, :, columns] = flat[head * size : (head + 1) * size]


def split_pairs(flat, ref, rows):
    pairs, width = ref.shape[0], ref.shape[2]
    for pair in range(pairs):
        ref[pair, rows, :] = flat[pair * width : (pair + 1) * width].T


def teacher_kernel(traffic, len_ref, rows_ref, weight_ref, qt_ref, k_ref, vt_ref, v_ref, bound_ref):
    flat = weight_ref.shape[0] // 3
    size = qt_ref.shape[1]
    bound_ref[...] = jnp.zeros(bound_ref.shape, F32)

    def step(block, carry):
        where = lanes(block)
        traffic.take(block)
        rows = rows_ref[where, :]
        projected = nt(weight_ref[...], rows).astype(BF16)
        bound_ref[...] = jnp.maximum(bound_ref[...], squared_lengths(projected, size))
        split_heads(projected[:flat], qt_ref, where, size)
        split_pairs(projected[flat : 2 * flat], k_ref, where)
        split_heads(projected[2 * flat :], vt_ref, where, size)
        split_pairs(projected[2 * flat :], v_ref, where)
        traffic.give(block, 0, 1, 2, 3)
        return carry

    lax.fori_loop(0, live_blocks(len_ref), step, 0)


def attend_kernel(
    traffic, len_ref, xt_ref, weight_ref, vec_ref, qt_ref, kt_ref, q_ref, k_ref, v_ref, ot_ref, lse_ref, at_ref,
    vone_ref, bound_ref,
):
    heads, size, rows = qt_ref.shape
    flat = heads * size
    scaling = LOG2_E * size ** (-0.5)
    blocks = live_blocks(len_ref)
    length = len_ref[0]
    bound_ref[...] = jnp.zeros(bound_ref.shape, F32)

    def project(block, carry):
        where = lanes(block)
        traffic.take(block)
        xt = xt_ref[:, where]
        projected = tn(weight_ref[:, : 3 * flat], xt)
        query = (projected[:flat] + vec_ref[:, 0:1]).astype(BF16)
        keys = projected[flat : 2 * flat].astype(BF16)
        values = (projected[2 * flat :] + vec_ref[:, 1:2]).astype(BF16)
        split_heads(query, qt_ref, where, size)
        split_heads(keys, kt_ref, where, size)
        bound_ref[...] = jnp.maximum(
            bound_ref[...], squared_lengths(jnp.concatenate([query, keys], axis=0), size)
        )
        column = block * BLOCK + lax.broadcasted_iota(jnp.int32, (1, BLOCK), 1)
        live = jnp.where(column < length, 1.0, 0.0)
        live_values = (values.astype(F32) * live).astype(BF16)
        for head in range(heads):
            vone_ref[head, :size, where] = live_values[head * size : (head + 1) * size]
            vone_ref[head, size:, where] = jnp.broadcast_to(live, (16, BLOCK)).astype(BF16)
        split_pairs(query, q_ref, where)
        split_pairs(keys, k_ref, where)
        split_pairs(values, v_ref, where)
        traffic.give(block, 0, 1, 2, 3, 4)
        return carry

    lax.fori_loop(0, blocks, project, 0)

    longest = jnp.max(bound_ref[...], axis=1, keepdims=True)
    safe = jnp.max(longest[:heads] * longest[heads : 2 * heads]) * scaling**2 <= SAFE_EXPONENT**2

    def scores(head, where, n):
        return nn(k_ref[head // 2, : n * BLOCK, :], pad_rows(qt_ref[head, :, where], head % 2, 2))

    def mix(head, where, n, grown, top):
        mixed = nn(vone_ref[head, :, : n * BLOCK], grown)
        total = mixed[size : size + 1]
        ot_ref[head, :, where] = mixed[:size] * (1.0 / total)
        lse_ref[head, :, where] = jnp.broadcast_to(top + jnp.log2(total), (8, BLOCK))

    def fast(n):
        def step(block, carry):
            where = lanes(block)
            pipeline(
                heads,
                lambda head: scores(head, where, n),
                lambda head, score: jnp.exp2(score * scaling).astype(BF16),
                lambda head, grown: mix(head, where, n, grown, 0.0),
            )
            traffic.give(block, 5, 6)
            return carry

        lax.fori_loop(0, n, step, 0)

    def slow():
        most = rows // BLOCK
        clear_dead(blocks, rows, vone_ref)

        def step(block, carry):
            where = lanes(block)
            for head in range(heads):
                score = mask_tail(scores(head, where, most), most, length, 0)
                top = jnp.max(score, axis=0, keepdims=True) * scaling
                mix(head, where, most, jnp.exp2(score * scaling - top).astype(BF16), top)
            traffic.give(block, 5, 6)
            return carry

        lax.fori_loop(0, blocks, step, 0)

    for_size(blocks, rows // BLOCK, safe, fast, slow)

    def output(block, carry):
        where = lanes(block)
        mixed = ot_ref[:, :, where].reshape(flat, BLOCK).astype(BF16)
        at_ref[:, where] = nn(weight_ref[:, 3 * flat :], mixed).astype(BF16)
        traffic.give(block, 7)
        return carry

    lax.fori_loop(0, blocks, output, 0)


def first_norm(xt, own, other, vec_ref):
    resid = xt.astype(F32) + (own.astype(F32) + other.astype(F32)) + vec_ref[:, 2:3]
    return norm_forward(resid)


def erf(value):
    return lax.erf(value)


def feed_kernel(traffic, len_ref, xt_ref, own_ref, other_ref, in_ref, out_ref, vec_ref, ht_ref, zt_ref, slope_ref, ft_ref):
    def step(block, carry):
        where = lanes(block)
        traffic.take(block)
        normed, _ = first_norm(xt_ref[:, where], own_ref[:, where], other_ref[:, where], vec_ref)
        hidden = normed * vec_ref[:, 3:4] + vec_ref[:, 4:5]
        ht_ref[:, where] = hidden
        pre = tn(in_ref[...], hidden.astype(BF16))
        cdf = 0.5 + 0.5 * erf(pre * (0.5**0.5))
        pdf = jnp.exp2(pre * pre * (-0.5 * LOG2_E)) * 0.3989422804014327
        active = (pre * cdf).astype(BF16)
        zt_ref[:, where] = active
        slope_ref[:, where] = (cdf + pre * pdf).astype(BF16)
        ft_ref[:, where] = nn(out_ref[...], active).astype(BF16)
        traffic.give(block, 0, 1, 2, 3)
        return carry

    lax.fori_loop(0, live_blocks(len_ref), step, 0)


def second_norm(ht, own, other, vec_ref):
    resid = ht + (own.astype(F32) + other.astype(F32)) + vec_ref[:, 5:6]
    return norm_forward(resid)


def relation_kernel(
    traffic, len_ref, weight_ref, ht_ref, own_ref, other_ref, rel_ref, vec_ref, tqt_ref, tk_ref, tvt_ref, tv_ref,
    tbound_ref, grad_ref, dt_ref,
    h2_ref, qt_ref, kt_ref, vt_ref, q_ref, k_ref, v_ref, dqt_ref, dvt_ref, dk_ref, dv_ref, bound_ref,
):
    heads, size, rows = qt_ref.shape
    teacher_size = tqt_ref.shape[1]
    flat = heads * size
    plain = size ** (-0.5)
    scaling = LOG2_E * plain
    teacher_scaling = LOG2_E * teacher_size ** (-0.5)
    blocks = live_blocks(len_ref)
    length = len_ref[0]
    weight = weight_ref[0]
    bound_ref[...] = jnp.zeros(bound_ref.shape, F32)

    def project(block, carry):
        where = lanes(block)
        traffic.take(block)
        normed, _ = second_norm(ht_ref[:, where], own_ref[:, where], other_ref[:, where], vec_ref)
        hidden = (normed * vec_ref[:, 6:7] + vec_ref[:, 7:8]).astype(BF16)
        h2_ref[:, where] = hidden
        projected = tn(rel_ref[...], hidden).astype(BF16)
        bound_ref[...] = jnp.maximum(bound_ref[...], squared_lengths(projected, size))
        split_heads(projected[:flat], qt_ref, where, size)
        split_heads(projected[flat : 2 * flat], kt_ref, where, size)
        split_heads(projected[2 * flat :], vt_ref, where, size)
        split_pairs(projected[:flat], q_ref, where)
        split_pairs(projected[flat : 2 * flat], k_ref, where)
        split_pairs(projected[2 * flat :], v_ref, where)
        for pair in range(heads // 2):
            dk_ref[pair, where, :] = jnp.zeros((BLOCK, 2 * size), F32)
            dv_ref[pair, where, :] = jnp.zeros((BLOCK, 2 * size), F32)
        return carry

    lax.fori_loop(0, blocks, project, 0)

    traffic.take_rest()

    def exponents(ref, scale):
        longest = jnp.max(ref[...], axis=1, keepdims=True)
        attention = jnp.max(longest[:heads] * longest[heads : 2 * heads]) * scale**2
        relation = jnp.max(longest[2 * heads : 3 * heads]) * scale
        return jnp.logical_and(attention <= SAFE_EXPONENT**2, relation <= SAFE_EXPONENT)

    safe = jnp.logical_and(exponents(bound_ref, scaling), exponents(tbound_ref, teacher_scaling))
    attention = (k_ref, qt_ref, q_ref, tk_ref, tqt_ref, kt_ref, dqt_ref, dk_ref)
    relation = (v_ref, vt_ref, v_ref, tv_ref, tvt_ref, vt_ref, dvt_ref, dv_ref)
    tasks = [(2 * pair + half, refs) for pair in range(heads // 2) for refs in (attention, relation) for half in range(2)]

    def steps(n, where, mask, grow):
        column = where.start + lax.broadcasted_iota(jnp.int32, (1, BLOCK), 1)
        live = jnp.where(column < length, weight, 0.0)
        kept = {}

        def first(t):
            head, (left, rightt, _, teacher_left, teacher_rightt, _, _, _) = tasks[t]
            student = nn(left[head // 2, : n * BLOCK, :], pad_rows(rightt[head, :, where], head % 2, 2))
            teacher = nn(teacher_left[head // 2, : n * BLOCK, :], pad_rows(teacher_rightt[head, :, where], head % 2, 2))
            return student, teacher

        def second(t, scores):
            student, teacher = grow(mask(scores[0]), scaling), grow(mask(scores[1]), teacher_scaling)
            student_part = live / jnp.sum(student, axis=0, keepdims=True)
            teacher_part = live / jnp.sum(teacher, axis=0, keepdims=True)
            return (student * student_part - teacher * teacher_part).astype(BF16)

        def third(t, grad):
            head, (_, _, right, _, _, leftt, own_ref, running_ref) = tasks[t]
            own_ref[head, :, where] = (nn(leftt[head, :, : n * BLOCK], grad) * plain).astype(own_ref.dtype)
            kept[head % 2] = grad
            if head % 2 == 1:
                queries = right[head // 2, where, :]
                stacked = jnp.concatenate([pad_lanes(queries, half, size) for half in range(2)], axis=0)
                running_ref[head // 2, : n * BLOCK, :] += nn(jnp.concatenate([kept[0], kept[1]], axis=1), stacked)

        return first, second, third

    def fast(n):
        def step(block, carry):
            stages = steps(
                n, lanes(block), lambda score: mask_tail(score, n, length), lambda score, scale: jnp.exp2(score * scale)
            )
            pipeline(len(tasks), *stages)
            return carry

        lax.fori_loop(0, n, step, 0)

    def slow():
        most = rows // BLOCK
        clear_dead(blocks, rows, kt_ref, vt_ref)

        def grow(score, scale):
            return jnp.exp2(score * scale - jnp.max(score, axis=0, keepdims=True) * scale)

        def step(block, carry):
            first, second, third = steps(
                most, lanes(block), lambda score: mask_tail(score, most, length, 0), grow
            )
            for t in range(len(tasks)):
                third(t, second(t, first(t)))
            return carry

        lax.fori_loop(0, blocks, step, 0)

    for_size(blocks, rows // BLOCK, safe, fast, slow)
    grad_ref[...] = jnp.zeros(grad_ref.shape, F32)

    def finish(block, carry):
        where = lanes(block)
        queries = dqt_ref[:, :, where].reshape(flat, BLOCK)
        keys = jnp.concatenate([dk_ref[pair, where, :].T for pair in range(heads // 2)], axis=0) * plain
        values = jnp.concatenate([dv_ref[pair, where, :].T for pair in range(heads // 2)], axis=0) * plain
        values = values + dvt_ref[:, :, where].reshape(flat, BLOCK)
        grads = jnp.concatenate([queries, keys.astype(BF16), values.astype(BF16)], axis=0)
        grad_ref[...] += nt(h2_ref[:, where], grads)
        dt_ref[:, where] = nn(rel_ref[...], grads).astype(BF16)
        traffic.give(block, 1)
        return carry

    lax.fori_loop(0, blocks, finish, 0)


def feed_back_kernel(
    traffic, len_ref, ht_ref, own_ref, other_ref, down_own_ref, down_other_ref, zt_ref, slope_ref, in_ref, out_ref, vec_ref,
    grad_in_ref, grad_out_ref, sums_ref, resid_ref, up_ref,
):
    grad_in_ref[...] = jnp.zeros(grad_in_ref.shape, F32)
    grad_out_ref[...] = jnp.zeros(grad_out_ref.shape, F32)
    sums_ref[...] = jnp.zeros(sums_ref.shape, F32)

    def step(block, carry):
        where = lanes(block)
        traffic.take(block)
        hidden = ht_ref[:, where]
        normed, inverse = second_norm(hidden, own_ref[:, where], other_ref[:, where], vec_ref)
        grad = down_own_ref[:, where].astype(F32) + down_other_ref[:, where].astype(F32)
        resid = norm_backward(grad * vec_ref[:, 6:7], normed, inverse)
        resid_ref[:, where] = resid
        sums_ref[:, 0:1] += jnp.sum(resid, axis=1, keepdims=True)
        sums_ref[:, 1:2] += jnp.sum(grad * normed, axis=1, keepdims=True)
        sums_ref[:, 2:3] += jnp.sum(grad, axis=1, keepdims=True)
        branch = resid.astype(BF16)
        grad_out_ref[...] += nt(branch, zt_ref[:, where])
        pre_grad = (tn(out_ref[...], branch) * slope_ref[:, where].astype(F32)).astype(BF16)
        grad_in_ref[...] += nt(hidden.astype(BF16), pre_grad)
        up_ref[:, where] = nn(in_ref[...], pre_grad).astype(BF16)
        traffic.give(block, 3, 4)
        return carry

    lax.fori_loop(0, live_blocks(len_ref), step, 0)


def attend_back_kernel(
    traffic, len_ref, xt_ref, own_ref, other_ref, resid_ref, up_own_ref, up_other_ref, weight_ref, vec_ref,
    qt_ref, kt_ref, q_ref, k_ref, v_ref, ot_ref, lse_ref,
    grad_ref, sums_ref, head_sums_ref,
    dot_ref, do_ref, inner_ref, dqt_ref, dk_ref, dv_ref,
):
    heads, size, rows = qt_ref.shape
    flat = heads * size
    plain = size ** (-0.5)
    scaling = LOG2_E * plain
    blocks = live_blocks(len_ref)
    length = len_ref[0]
    sums_ref[...] = jnp.zeros(sums_ref.shape, F32)
    head_sums_ref[...] = jnp.zeros(head_sums_ref.shape, F32)
    grad_ref[...] = jnp.zeros(grad_ref.shape, F32)

    def start(block, carry):
        where = lanes(block)
        traffic.take(block)
        normed, inverse = first_norm(xt_ref[:, where], own_ref[:, where], other_ref[:, where], vec_ref)
        grad = resid_ref[:, where] + (up_own_ref[:, where].astype(F32) + up_other_ref[:, where].astype(F32))
        branch = norm_backward(grad * vec_ref[:, 3:4], normed, inverse).astype(BF16)
        sums_ref[:, 0:1] += jnp.sum(branch.astype(F32), axis=1, keepdims=True)
        sums_ref[:, 1:2] += jnp.sum(grad * normed, axis=1, keepdims=True)
        sums_ref[:, 2:3] += jnp.sum(grad, axis=1, keepdims=True)
        mixed = ot_ref[:, :, where]
        grad_ref[:, 3 * flat :] += nt(branch, mixed.reshape(flat, BLOCK).astype(BF16))
        mixed_grad = tn(weight_ref[:, 3 * flat :], branch).astype(BF16)
        split_heads(mixed_grad, dot_ref, where, size)
        split_pairs(mixed_grad, do_ref, where)
        for head in range(heads):
            product = mixed_grad[head * size : (head + 1) * size].astype(F32) * mixed[head]
            inner_ref[head, :, where] = jnp.broadcast_to(jnp.sum(product, axis=0, keepdims=True), (8, BLOCK))
        for pair in range(heads // 2):
            dk_ref[pair, where, :] = jnp.zeros((BLOCK, 2 * size), F32)
            dv_ref[pair, where, :] = jnp.zeros((BLOCK, 2 * size), F32)
        return carry

    lax.fori_loop(0, blocks, start, 0)
    traffic.take_rest()

    def attend(n):
        def step(block, carry):
            where = lanes(block)
            kept = {}

            def first(head):
                pair, half = head // 2, head % 2
                scores = nn(k_ref[pair, : n * BLOCK, :], pad_rows(qt_ref[head, :, where], half, 2))
                prob_grad = nn(v_ref[pair, : n * BLOCK, :], pad_rows(dot_ref[head, :, where], half, 2))
                return scores, prob_grad

            def second(head, parts):
                scores, prob_grad = parts
                prob = jnp.exp2(mask_tail(scores, n, length) * scaling - lse_ref[head, 0:1, where])
                grad = (prob * (prob_grad - inner_ref[head, 0:1, where])).astype(BF16)
                return prob.astype(BF16), grad

            def third(head, parts):
                pair = head // 2
                dqt_ref[head, :, where] = (nn(kt_ref[head, :, : n * BLOCK], parts[1]) * plain).astype(BF16)
                kept[head % 2] = parts
                if head % 2 == 1:
                    for index, right, running in ((1, q_ref, dk_ref), (0, do_ref, dv_ref)):
                        queries = right[pair, where, :]
                        stacked = jnp.concatenate([pad_lanes(queries, half, size) for half in range(2)], axis=0)
                        running[pair, : n * BLOCK, :] += nn(
                            jnp.concatenate([kept[0][index], kept[1][index]], axis=1), stacked
                        )

            pipeline(heads, first, second, third)
            return carry

        lax.fori_loop(0, n, step, 0)

    for n in range(1, rows // BLOCK + 1):
        pl.when(blocks == n)(functools.partial(attend, n))

    def finish(block, carry):
        where = lanes(block)
        queries = dqt_ref[:, :, where].reshape(flat, BLOCK)
        keys = jnp.concatenate([dk_ref[pair, where, :].T for pair in range(heads // 2)], axis=0) * plain
        values = jnp.concatenate([dv_ref[pair, where, :].T for pair in range(heads // 2)], axis=0).astype(BF16)
        head_sums_ref[:, 0:1] += jnp.sum(queries.astype(F32), axis=1, keepdims=True)
        head_sums_ref[:, 1:2] += jnp.sum(values.astype(F32), axis=1, keepdims=True)
        grads = jnp.concatenate([queries, keys.astype(BF16), values], axis=0)
        grad_ref[:, : 3 * flat] += nt(xt_ref[:, where], grads)
        return carry

    lax.fori_loop(0, blocks, finish, 0)


class Traffic:
    def __init__(self, blocks, ins, outs, in_sems, out_sems):
        self.blocks, self.ins, self.outs, self.in_sems, self.out_sems = blocks, ins, outs, in_sems, out_sems

    def copy(self, source, target, axis, block, sem):
        if axis is not None:
            where = (slice(None),) * axis + (lanes(block),)
            source, target = source.at[where], target.at[where]
        return pltpu.make_async_copy(source, target, sem)

    def inward(self, index, block):
        source, target, axis, _ = self.ins[index]
        return self.copy(source, target, axis, block, self.in_sems.at[index, block])

    def outward(self, index, block):
        target, source, axis = self.outs[index]
        return self.copy(source, target, axis, block, self.out_sems.at[index, block])

    def chosen(self, group):
        return [i for i, entry in enumerate(self.ins) if entry[2] is not None and entry[3] == group]

    def start(self):
        for index, entry in enumerate(self.ins):
            if entry[2] is None:
                self.inward(index, 0).start()
        for group in (0, 1):
            indices = self.chosen(group)

            def step(block, carry):
                for index in indices:
                    self.inward(index, block).start()
                return carry

            if indices:
                lax.fori_loop(0, self.blocks, step, 0)
        for index, entry in enumerate(self.ins):
            if entry[2] is None:
                self.inward(index, 0).wait()

    def take(self, block):
        for index in self.chosen(0):
            self.inward(index, block).wait()

    def take_rest(self):
        def step(block, carry):
            for index in self.chosen(1):
                self.inward(index, block).wait()
            return carry

        lax.fori_loop(0, self.blocks, step, 0)

    def give(self, block, *indices):
        for index in indices:
            self.outward(index, block).start()

    def finish(self):
        whole = [i for i, entry in enumerate(self.outs) if entry[2] is None]
        parts = [i for i, entry in enumerate(self.outs) if entry[2] is not None]
        for index in whole:
            self.outward(index, 0).start()

        def step(block, carry):
            for index in parts:
                self.outward(index, block).wait()
            return carry

        if parts:
            lax.fori_loop(0, self.blocks, step, 0)
        for index in whole:
            self.outward(index, 0).wait()


def call(kernel, name, scalars, arrays, outs, scratch=(), flops=0):
    smem = pl.BlockSpec(memory_space=pltpu.SMEM)
    hbm = pl.BlockSpec(memory_space=pl.ANY)
    most = max(array.shape[axis] // BLOCK for array, axis, _ in arrays if axis is not None)
    count, ins, results = len(scalars), len(arrays), len(outs)

    def body(*refs):
        scalar_refs, refs = refs[:count], refs[count:]
        in_refs, refs = refs[:ins], refs[ins:]
        out_refs, refs = refs[:results], refs[results:]
        in_copies, refs = refs[:ins], refs[ins:]
        out_copies, refs = refs[:results], refs[results:]
        in_sems, out_sems, refs = refs[0], refs[1], refs[2:]
        traffic = Traffic(
            live_blocks(scalar_refs[0]),
            [(ref, copy, axis, group) for ref, copy, (_, axis, group) in zip(in_refs, in_copies, arrays)],
            [(ref, copy, axis) for ref, copy, (_, _, axis) in zip(out_refs, out_copies, outs)],
            in_sems,
            out_sems,
        )
        traffic.start()
        kernel(traffic, *scalar_refs, *in_copies, *out_copies, *refs)
        traffic.finish()

    return pl.pallas_call(
        body,
        name=name,
        out_shape=tuple(jax.ShapeDtypeStruct(shape, dtype) for shape, dtype, _ in outs),
        in_specs=[smem] * count + [hbm] * ins,
        out_specs=tuple(hbm for _ in outs),
        scratch_shapes=[pltpu.VMEM(array.shape, array.dtype) for array, _, _ in arrays]
        + [pltpu.VMEM(shape, dtype) for shape, dtype, _ in outs]
        + [pltpu.SemaphoreType.DMA((ins, most)), pltpu.SemaphoreType.DMA((results, most))]
        + [pltpu.VMEM(shape, dtype) for shape, dtype in scratch],
        compiler_params=pltpu.CompilerParams(vmem_limit_bytes=VMEM_BYTES),
        cost_estimate=pl.CostEstimate(flops=flops, bytes_accessed=4 << 20, transcendentals=0),
    )(*scalars, *(array for array, _, _ in arrays))


def exchange(part):
    return swap(part, "ffn", 0)


def total(parts):
    result = parts[0]
    for part in parts[1:]:
        result = result + part
    return result


def swap(value, axis, bit):
    count = lax.axis_size(axis)
    return lax.ppermute(value, axis, [(i, i ^ (1 << bit)) for i in range(count)])


def bit_of(axis, bit):
    return (lax.axis_index(axis) >> bit) & 1


def dp_bits():
    return lax.axis_size("dp").bit_length() - 1


def after(value, *others):
    return lax.optimization_barrier((value, *others))[0]


def gather_step(whole, other, bit):
    dim = dp_bits() - 1 - bit
    upper = bit_of("dp", bit) == 1
    return jnp.where(upper, jnp.concatenate([other, whole], axis=dim), jnp.concatenate([whole, other], axis=dim))


def split_rows(value):
    bits = dp_bits()
    return value.reshape((2,) * bits + (value.shape[0] >> bits,) + value.shape[1:])


def reduce_step(part, bits, tokens=()):
    count = dp_bits()
    dims = [count - 1 - bit for bit in bits]
    mine = [bit_of("dp", bit) for bit in bits]

    def piece(flips):
        result = part
        for dim, bit, flip in zip(dims, mine, flips):
            result = lax.dynamic_slice_in_dim(result, 1 - bit if flip else bit, 1, dim)
        return result

    size = lax.axis_size("dp")
    arrived = []
    for code in range(1, 1 << len(bits)):
        flips = [(code >> i) & 1 for i in range(len(bits))]
        mask = sum(flip << bit for flip, bit in zip(flips, bits))
        arrived.append(lax.ppermute(piece(flips).astype(BF16), "dp", [(i, i ^ mask) for i in range(size)]))
    kept = piece([0] * len(bits))

    def finish(*tokens):
        result = kept
        for other in arrived:
            result = result + (after(other, *tokens) if tokens else other).astype(F32)
        return result

    return finish


def reduce_owner(value):
    count = lax.axis_size("dp")
    rows = value.shape[0] // count
    spread = lax.all_to_all(value.astype(BF16).reshape((count, rows) + value.shape[1:]), "dp", 0, 0, tiled=True)
    return jnp.sum(spread.astype(F32), axis=0)


def all_sum(value):
    count = lax.axis_size("dp") * lax.axis_size("ffn")
    spread = jnp.broadcast_to(value.reshape(1, 1), (count, 128))
    return jnp.sum(lax.all_to_all(spread, ("dp", "ffn"), 0, 0, tiled=True)[:, 0])


def adam_update(weight, gradient, first, second, clipped, rate, decay):
    scaled = gradient * clipped
    first_new = BETA_ONE * first + (1.0 - BETA_ONE) * scaled
    second_new = BETA_TWO * second + (1.0 - BETA_TWO) * scaled * scaled
    ratio = (
        first_new
        / (1.0 - BETA_ONE**STEP)
        / (jnp.sqrt(second_new / (1.0 - BETA_TWO**STEP)) + ADAM_EPSILON)
    )
    return (weight - rate * (ratio + decay * weight), first_new, second_new)


def per_device(
    states, teacher_states, lengths, domain_ids, domain_weight, teacher_qkv,
    attn_a, ffn_in, ffn_out, attn_b, vec_d,
    mom1_attn_a, mom1_ffn_in, mom1_ffn_out, mom1_attn_b, mom1_vec_d,
    mom2_attn_a, mom2_ffn_in, mom2_ffn_out, mom2_attn_b, mom2_vec_d,
):
    cores = lax.axis_size("ffn")
    core = lax.axis_index("ffn")
    replicas = lax.axis_size("dp")
    replica = lax.axis_index("dp")
    sequences = lengths.shape[0]
    rows = states.shape[0] // sequences
    features = states.shape[1]
    heads = HEADS // cores
    flat = features // cores
    size = flat // heads
    pairs = heads // 2
    hidden = ffn_in.shape[1]
    teacher_flat = teacher_qkv.shape[2]
    teacher_size = teacher_flat // heads
    shard = attn_a.shape[0]
    matched = domain_ids[:, None] == jnp.arange(domain_weight.shape[0])[None, :]
    sequence_weight = jnp.sum(jnp.where(matched, domain_weight[None, :], 0.0), axis=1) / HEADS

    teacher_w = teacher_qkv.reshape(teacher_qkv.shape[0], -1).T
    statest = states.T
    live = [lengths[i : i + 1] for i in range(sequences)]
    weights = [sequence_weight[i : i + 1] for i in range(sequences)]
    xt = [statest[:, i * rows : (i + 1) * rows] for i in range(sequences)]
    each = range(sequences)
    act = ((features, rows), BF16)
    wide = ((features, rows), F32)
    head_t = ((heads, size, rows), BF16)
    pair_rows = ((pairs, rows, 2 * size), BF16)

    bound_rows = -(-3 * heads // 8) * 8

    def project_teacher(i, token):
        return call(
            teacher_kernel, "teacher", (live[i],),
            ((after(teacher_states[i * rows : (i + 1) * rows], token), 0, 0), (teacher_w, None, 0)),
            (
                ((heads, teacher_size, rows), BF16, 2),
                ((pairs, rows, 2 * teacher_size), BF16, 1),
                ((heads, teacher_size, rows), BF16, 2),
                ((pairs, rows, 2 * teacher_size), BF16, 1),
                ((bound_rows, BLOCK), F32, None),
            ),
            flops=2 * rows * 768 * 1152,
        )

    attn_own = lax.dynamic_slice_in_dim(attn_a.reshape(shard, 4, features), core * flat, flat, 2).reshape(shard, 4 * flat)
    bits = dp_bits()
    unit = (1,) * bits
    early = jnp.concatenate([attn_own, vec_d], axis=1).astype(BF16).reshape(unit + (shard, -1))
    late = jnp.concatenate([ffn_in, ffn_out, attn_b.reshape(shard, 3 * flat)], axis=1).astype(BF16)
    late = late.reshape(unit + (shard, -1))
    teacher = []
    for step, bit in enumerate(range(bits)[::-1]):
        early_other = swap(early, "dp", bit)
        late_other = swap(late, "dp", bit + 1) if step else None
        if step == 0:
            tokens = (teacher_w, statest)
        elif step <= sequences:
            teacher.append(project_teacher(step - 1, early))
            tokens = teacher[-1]
        else:
            tokens = ()
        early = gather_step(early, after(early_other, *tokens), bit)
        if step:
            late = gather_step(late, after(late_other, *tokens), bit + 1)
    early = early.reshape(features, -1)
    attn_full, vec_full = early[:, : 4 * flat], early[:, 4 * flat :].astype(F32)
    vec_own = lax.dynamic_slice_in_dim(vec_full, core * flat, flat, 0)
    late_other = swap(late, "dp", 0)

    attended = [
        call(
            attend_kernel, "attend", (live[i],),
            ((after(xt[i], late), 1, 0), (attn_full, None, 0), (vec_own, None, 0)),
            ((*head_t, 2), (*head_t, 2), (*pair_rows, 1), (*pair_rows, 1), (*pair_rows, 1),
             ((heads, size, rows), F32, 2), ((heads, 8, rows), F32, 2), (*act, 1)),
            scratch=(((heads, size + 16, rows), BF16), ((-(-2 * heads // 8) * 8, BLOCK), F32)),
            flops=6 * 10**9,
        )
        for i in each
    ]
    late = gather_step(late, after(late_other, *attended), 0).reshape(features, -1)
    in_full, out_full, rel_full = late[:, :hidden], late[:, hidden : 2 * hidden], late[:, 2 * hidden :]
    mixed_other = [exchange(attended[i][7]) for i in each]
    fed = [
        call(
            feed_kernel, "feed", (live[i],),
            ((xt[i], 1, 0), (attended[i][7], 1, 0), (mixed_other[i], 1, 0), (in_full, None, 0), (out_full, None, 0),
             (vec_full, None, 0)),
            ((*wide, 1), ((hidden, rows), BF16, 1), ((hidden, rows), BF16, 1), (*act, 1)),
            flops=3 * 10**9,
        )
        for i in each
    ]
    fed_other = [exchange(fed[i][3]) for i in each]
    related = [
        call(
            relation_kernel, "relation", (live[i], weights[i]),
            ((fed[i][0], 1, 0), (fed[i][3], 1, 0), (fed_other[i], 1, 0), (rel_full, None, 0), (vec_full, None, 0),
             (teacher[i][0], 2, 1), (teacher[i][1], 1, 1), (teacher[i][2], 2, 1), (teacher[i][3], 1, 1),
             (teacher[i][4], None, 0)),
            (((features, 3 * flat), F32, None), (*act, 1)),
            scratch=(
                act, head_t, head_t, head_t, pair_rows, pair_rows, pair_rows,
                head_t, ((heads, size, rows), F32),
                ((pairs, rows, 2 * size), F32), ((pairs, rows, 2 * size), F32), ((bound_rows, BLOCK), F32),
            ),
            flops=30 * 10**9,
        )
        for i in each
    ]
    down_other = [exchange(related[i][1]) for i in each]
    rel_part = split_rows(total([related[i][0] for i in each]))
    fed_back, up_other = [], []
    for i in each:
        finish = reduce_step(rel_part, (i,))
        fed_back.append(
            call(
                feed_back_kernel, "feed_back", (live[i],),
                ((fed[i][0], 1, 0), (fed[i][3], 1, 0), (fed_other[i], 1, 0), (related[i][1], 1, 0), (down_other[i], 1, 0),
                 (fed[i][1], 1, 0), (fed[i][2], 1, 0), (in_full, None, 0), (out_full, None, 0), (vec_full, None, 0)),
                (((features, hidden), F32, None), ((features, hidden), F32, None), ((features, 8), F32, None),
                 (*wide, 1), (*act, 1)),
                flops=4 * 10**9,
            )
        )
        rel_part = finish(*fed_back[i])
        up_other.append(exchange(fed_back[i][4]))
    feed_part = split_rows(
        total([jnp.concatenate([fed_back[i][0], fed_back[i][1]], axis=1) for i in each])
    )
    attended_back = []
    groups = ((0, 1), tuple(range(2, bits)))
    for i in each:
        finish_feed = reduce_step(feed_part, groups[i])
        finish_rel = reduce_step(rel_part, (2 + i,)) if i + 1 < sequences else reduce_step(rel_part, tuple(range(2 + i, bits)))
        attended_back.append(
            call(
                attend_back_kernel, "attend_back", (live[i],),
                ((xt[i], 1, 0), (attended[i][7], 1, 0), (mixed_other[i], 1, 0), (fed_back[i][3], 1, 0),
                 (fed_back[i][4], 1, 0), (up_other[i], 1, 0), (attn_full, None, 0), (vec_full, None, 0),
                 (attended[i][0], 2, 1), (attended[i][1], 2, 1), (attended[i][2], 1, 1), (attended[i][3], 1, 1),
                 (attended[i][4], 1, 1), (attended[i][5], 2, 0), (attended[i][6], 2, 1)),
                (((features, 4 * flat), F32, None), ((features, 8), F32, None), ((flat, 8), F32, None)),
                scratch=(
                    head_t, pair_rows, ((heads, 8, rows), F32), head_t,
                    ((pairs, rows, 2 * size), F32), ((pairs, rows, 2 * size), F32),
                ),
                flops=15 * 10**9,
            )
        )
        feed_part = finish_feed(*attended_back[i])
        rel_part = finish_rel(*attended_back[i])

    shard_rel = rel_part.reshape(shard, -1)
    shard_feed = feed_part.reshape(shard, -1)
    shard_in, shard_out = shard_feed[:, :hidden], shard_feed[:, hidden:]
    back_sums = total([fed_back[i][2] for i in each])
    first_sums = total([attended_back[i][1] for i in each])
    head_sums = total([attended_back[i][2] for i in each])
    placed = lax.dynamic_update_slice_in_dim(jnp.zeros((features, 2), F32), head_sums[:, :2], core * flat, 0)
    attn_local = total([attended_back[i][0] for i in each])
    own = jnp.concatenate([attn_local, placed, first_sums[:, :3], back_sums[:, :3]], axis=1)
    own = reduce_owner(after(own, shard_rel, shard_feed))
    other = swap(own, "ffn", 0)
    grad_rel = shard_rel.reshape(attn_b.shape)
    upper = core == 1
    low, high = jnp.where(upper, other, own), jnp.where(upper, own, other)
    columns = [
        half[:, start : start + flat] for start in range(0, 4 * flat, flat) for half in (low, high)
    ]
    grad_attn = jnp.concatenate(columns, axis=1)
    grad_vec = jnp.concatenate([(low + high)[:, 4 * flat : 4 * flat + 2], own[:, 4 * flat + 2 :]], axis=1)
    gradients = (grad_attn, shard_in, shard_out, grad_rel, grad_vec)
    shared = own[:, 4 * flat + 2 :]
    squares = (
        jnp.sum(own[:, : 4 * flat + 2] * own[:, : 4 * flat + 2])
        + jnp.sum(shared * shared) / cores
        + jnp.sum(shard_feed * shard_feed)
        + jnp.sum(shard_rel * shard_rel)
    )
    grad_norm = jnp.sqrt(all_sum(squares))
    clipped = jnp.minimum(1.0, CLIP_NORM / grad_norm)
    masters = (attn_a, ffn_in, ffn_out, attn_b, vec_d)
    firsts = (mom1_attn_a, mom1_ffn_in, mom1_ffn_out, mom1_attn_b, mom1_vec_d)
    seconds = (mom2_attn_a, mom2_ffn_in, mom2_ffn_out, mom2_attn_b, mom2_vec_d)
    rates = (RATE_MATRIX, RATE_MATRIX, RATE_MATRIX, RATE_MATRIX, RATE_VECTOR)
    decays = (DECAY_RATE, DECAY_RATE, DECAY_RATE, DECAY_RATE, 0.0)
    news = [
        adam_update(masters[i], gradients[i], firsts[i], seconds[i], clipped, rates[i], decays[i])
        for i in range(5)
    ]
    return (grad_norm, *(new[0] for new in news), *(new[1] for new in news), *(new[2] for new in news))


def solution(mesh):
    matrix = P("dp", None)
    halved = P("dp", "ffn")
    cube = P("dp", None, "ffn")
    trained = (matrix, halved, halved, cube, matrix)
    in_specs = (matrix, matrix, P("dp"), P("dp"), P(), P(None, None, "ffn")) + trained * 3
    out_specs = (P(),) + trained * 3
    return jax.shard_map(per_device, mesh=mesh, in_specs=in_specs, out_specs=out_specs, check_vma=False)
```

time: 1010 us -> 379 us (0.38)
  blocking collectives: 379 us -> 31.9 us
  waiting for transfers between devices: 363 us -> 18.4 us
  starting transfers between devices: 2.11 us -> 45.1 us
  Pallas kernels: 201 us -> 239 us
  between operations: 19.8 us -> 6.32 us
    reduce_scatter x3 -> x0, waiting for transfers between devices: 361 us -> none  [scatter(): return lax.psum_scatter(value, 'dp', scatter_dimension=0, tiled=True)]
    all_gather x6 -> x0, blocking collectives: 229 us -> none  [the longest x1 56.1 us: per_device(): in_full = lax.all_gather(ffn_in.astype(BF16), 'dp', axis=0, tiled=True)]
    psum x2 -> x0, blocking collectives: 150 us -> none  [the longest x1 111 us: per_device(): vec_total = lax.psum(vec_local, ('dp', 'ffn')) / cores]
    ppermute x8 -> x27, starting transfers between devices: 1.74 us -> 42.5 us  [the longest x10 27.4 us: reduce_step(): lax.ppermute(piece(flips).astype(BF16), 'dp', [(i, i ^ mask) for i in ran...]
    pallas_call x12, Pallas kernels: 201 us -> 239 us  [call(): pl.pallas_call(body, name=name, out_shape=tuple((jax.ShapeDtypeStruct(sha...]
    all_to_all x0 -> x1, blocking collectives: none -> 31.9 us  [reduce_owner(): lax.all_to_all(value.astype(BF16).reshape((count, rows) + value.shape[1:]...]
  transfers between devices with their start and end apart: 12 -> 28, of which waited for: 5 -> 5; matrix products, arithmetic and copies ran while one was open for 2% -> 6% of each run, Pallas kernels for 13% -> 63%
where the time goes in v2:
time: 379 us; the launch traced here: 381 us
  Pallas kernels  239 us (63%)
  starting transfers between devices  45.1 us (12%)
  blocking collectives  31.9 us (8%)
  local copies, waits for them, and re-layouts  24.2 us (6%)
  waiting for transfers between devices  18.4 us (5%)
  other arithmetic  15.4 us (4%)
  between operations  6.32 us (2%)
    pallas_call x12, Pallas kernels, call(): pl.pallas_call(body, name=name, out_shape=tuple((jax.ShapeDtypeStruct(sha...  239 us
    all_to_all x1, blocking collectives, reduce_owner(): lax.all_to_all(value.astype(BF16).reshape((count, rows) + value.shape[1:]...  31.9 us
    ppermute x10, starting transfers between devices, reduce_step(): lax.ppermute(piece(flips).astype(BF16), 'dp', [(i, i ^ mask) for i in ran...  27.4 us
    ppermute x17, starting transfers between devices, swap(): return lax.ppermute(value, axis, [(i, i ^ 1 << bit) for i in range(count)])  15.1 us
    unnamed x80, local copies, waits for them, and re-layouts  13.2 us
  transfers between devices with their start and end apart: 28, of which 5 were waited for; matrix products, arithmetic and copies ran while one was open for 6% of the time, Pallas kernels for 63%

profile of v2, /device:TPU:0, one launch (start us, length us, event | category | flops | bytes accessed | tf_op | source)
XLA Modules:
  0.0 380.6 jit_solution(16787765798026502649)
XLA Ops:
  2.6 4.1 %collective-permute-start.1 = (bf16[1,1,1,1,24,776]{5,4,0,3,2,1:T(8,128)(2,1)S(1)}, bf16[1,1,1,1,24,776]{5,4,0,3,2,1:T(8,128)(2,1)S(1)}, u32[]{:S(2)}, u32[]{:S(2)}) collective-permute-start(bf16[1,1,1,1,24,776]{5,4,0,3,2,1:T(8,128)(2,1)S(1)} %pad_maximum_fusion.3), channel_id=1, source_target_pairs={{0,16},{2,18},{4,20},{6,22},{8,24},{10,26},{12,28},{14,30},{16,0},... | collective-permute-start | bytes 111752 | tf_op jit(solution)/shard_map/ppermute | solution.py:646
  9.0 1.7 copy.181
  13.2 1.9 fusion.29
  15.8 2.3 copy.185
  18.1 2.0 collective-permute-start.3
  20.0 5.7 %teacher.2 = (bf16[6,64,1024]{2,1,0:T(8,128)(2,1)}, bf16[3,1024,128]{2,1,0:T(8,128)(2,1)}, bf16[6,64,1024]{2,1,0:T(8,128)(2,1)}, bf16[3,1024,128]{2,1,0:T(8,128)(2,1)}, f32[24,256]{1,0:T(8,128)}) custom-call(s32[1]{0:T(128)} %get-tuple-element.325.refs_0_, bf16[1024,768]{1,0:T(8,128)(2,1)} %get-tuple-element.92.refs_1_, bf16[1152,768]{1,0:T(8,128)(2,1)} %bitcast.90), custom_call_target="tpu_custom_call" | custom-call | flops 1811939328 | bytes 4194304 | tf_op jit(solution)/shard_map/teacher/pallas_call | solution.py:618
  26.1 2.8 collective-permute-start.5
  28.9 6.6 %teacher.3 = (bf16[6,64,1024]{2,1,0:T(8,128)(2,1)}, bf16[3,1024,128]{2,1,0:T(8,128)(2,1)}, bf16[6,64,1024]{2,1,0:T(8,128)(2,1)}, bf16[3,1024,128]{2,1,0:T(8,128)(2,1)}, f32[24,256]{1,0:T(8,128)}) custom-call(s32[1]{0:T(128)} %get-tuple-element.326.refs_0_, bf16[1024,768]{1,0:T(8,128)(2,1)} %get-tuple-element.100.refs_1_, bf16[1152,768]{1,0:T(8,128)(2,1)} %bitcast.91), custom_call_target="tpu_custom_call" | custom-call | flops 1811939328 | bytes 4194304 | tf_op jit(solution)/shard_map/teacher/pallas_call | solution.py:618
  35.8 2.0 collective-permute-start.4
  38.0 6.2 %collective-permute-done.6 = bf16[2,2,2,1,24,776]{5,4,3,2,1,0:T(8,128)(2,1)S(1)} collective-permute-done((bf16[2,2,2,1,24,776]{5,4,3,2,1,0:T(8,128)(2,1)S(1)}, bf16[2,2,2,1,24,776]{5,4,3,2,1,0:T(8,128)(2,1)S(1)}, u32[]{:S(2)}, u32[]{:S(2)}) %collective-permute-start.6) | collective-permute-done | bytes 298016 | tf_op jit(solution)/shard_map/ppermute | solution.py:646
  46.1 1.8 collective-permute-start.8
  47.8 11.7 %attend.3 = (bf16[6,32,1024]{2,1,0:T(8,128)(2,1)}, bf16[6,32,1024]{2,1,0:T(8,128)(2,1)}, bf16[3,1024,64]{2,1,0:T(8,128)(2,1)}, bf16[3,1024,64]{2,1,0:T(8,128)(2,...) custom-call(s32[1]{0:T(128)} %get-tuple-element.326.refs_0_, ...), custom_call_target="tpu_custom_call" | custom-call | flops 6000000000 | bytes 4194304 | tf_op jit(solution)/shard_map/attend/pallas_call | solution.py:618
  59.6 8.7 %attend.2 = (bf16[6,32,1024]{2,1,0:T(8,128)(2,1)}, bf16[6,32,1024]{2,1,0:T(8,128)(2,1)}, bf16[3,1024,64]{2,1,0:T(8,128)(2,1)}, bf16[3,1024,64]{2,1,0:T(8,128)(2,...) custom-call(s32[1]{0:T(128)} %get-tuple-element.325.refs_0_, ...), custom_call_target="tpu_custom_call" | custom-call | flops 6000000000 | bytes 4194304 | tf_op jit(solution)/shard_map/attend/pallas_call | solution.py:618
  71.3 8.0 %feed.3 = (f32[384,1024]{1,0:T(8,128)}, bf16[768,1024]{1,0:T(8,128)(2,1)}, bf16[768,1024]{1,0:T(8,128)(2,1)}, bf16[384,1024]{1,0:T(8,128)(2,1)}) custom-call(s32[1]{0:T(128)} %get-tuple-element.326.refs_0_, bf16[384,1024]{1,0:T(8,128)(2,1)} %get-tuple-element.117.refs_1_, bf16[384,1024]{1,0:T(8,128)(2,1)} %get-tuple-element.125.refs_2_, ...), custom_call_target="tpu_custom_call" | custom-call | flops 3000000000 | bytes 4194304 | tf_op jit(solution)/shard_map/feed/pallas_call | solution.py:618
  82.0 6.8 %feed.2 = (f32[384,1024]{1,0:T(8,128)}, bf16[768,1024]{1,0:T(8,128)(2,1)}, bf16[768,1024]{1,0:T(8,128)(2,1)}, bf16[384,1024]{1,0:T(8,128)(2,1)}) custom-call(s32[1]{0:T(128)} %get-tuple-element.325.refs_0_, bf16[384,1024]{1,0:T(8,128)(2,1)} %get-tuple-element.107.refs_1_, bf16[384,1024]{1,0:T(8,128)(2,1)} %get-tuple-element.109.refs_2_, ...), custom_call_target="tpu_custom_call" | custom-call | flops 3000000000 | bytes 4194304 | tf_op jit(solution)/shard_map/feed/pallas_call | solution.py:618
  90.3 75.9 %relation.3 = (f32[384,576]{1,0:T(8,128)}, bf16[384,1024]{1,0:T(8,128)(2,1)}) custom-call(s32[1]{0:T(128)} %get-tuple-element.326.refs_0_, f32[1]{0:T(128)} %get-tuple-element.324.refs_1_, f32[384,1024]{1,0:T(8,128)} %get-tuple-element.135.refs_2_.refs_1_, bf16[384,1024]{1,0:T(8,128)(2,1)} %get-tuple-element.136.refs_3_.refs_2_, ...), custom_call_target="tpu_custom_call" | custom-call | flops 30000001024 | bytes 4194304 | tf_op jit(solution)/shard_map/relation/pallas_call | solution.py:618
  167.1 50.9 %relation.2 = (f32[384,576]{1,0:T(8,128)}, bf16[384,1024]{1,0:T(8,128)(2,1)}) custom-call(s32[1]{0:T(128)} %get-tuple-element.325.refs_0_, f32[1]{0:T(128)} %get-tuple-element.323.refs_1_, f32[384,1024]{1,0:T(8,128)} %get-tuple-element.127.refs_2_.refs_1_, bf16[384,1024]{1,0:T(8,128)(2,1)} %get-tuple-element.128.refs_3_.refs_2_, ...), custom_call_target="tpu_custom_call" | custom-call | flops 30000001024 | bytes 4194304 | tf_op jit(solution)/shard_map/relation/pallas_call | solution.py:618
  218.2 1.3 add.232
  220.6 11.7 %feed_back.3 = (f32[384,768]{1,0:T(8,128)}, f32[384,768]{1,0:T(8,128)}, f32[384,8]{1,0:T(8,128)}, f32[384,1024]{1,0:T(8,128)}, bf16[384,1024]{1,0:T(8,128)(2,1)}) custom-call(s32[1]{0:T(128)} %get-tuple-element.326.refs_0_, f32[384,1024]{1,0:T(8,128)} %get-tuple-element.135.refs_2_.refs_1_, bf16[384,1024]{1,0:T(8,128)(2,1)} %get-tuple-element.136.refs_3_.refs_2_, ...), custom_call_target="tpu_custom_call" | custom-call | flops 4000000000 | bytes 4194304 | tf_op jit(solution)/shard_map/feed_back/pallas_call | solution.py:618
  233.6 10.0 %feed_back.2 = (f32[384,768]{1,0:T(8,128)}, f32[384,768]{1,0:T(8,128)}, f32[384,8]{1,0:T(8,128)}, f32[384,1024]{1,0:T(8,128)}, bf16[384,1024]{1,0:T(8,128)(2,1)}) custom-call(s32[1]{0:T(128)} %get-tuple-element.325.refs_0_, f32[384,1024]{1,0:T(8,128)} %get-tuple-element.127.refs_2_.refs_1_, bf16[384,1024]{1,0:T(8,128)(2,1)} %get-tuple-element.128.refs_3_.refs_2_, ...), custom_call_target="tpu_custom_call" | custom-call | flops 4000000000 | bytes 4194304 | tf_op jit(solution)/shard_map/feed_back/pallas_call | solution.py:618
  244.9 2.0 maximum_add_fusion
  249.0 1.5 collective-permute-start.22
  251.5 19.7 %collective-permute-start.18 = (bf16[2,1,1,1,24,576]{5,4,3,2,1,0:T(8,128)(2,1)S(1)}, bf16[2,1,1,1,24,576]{5,4,3,2,1,0:T(8,128)(2,1)S(1)}, u32[]{:S(2)}, u32[]{:S(2)}) collective-permute-start(bf16[2,1,1,1,24,576]{5,4,3,2,1,0:T(8,128)(2,1)S(1)} %dynamic-slice_convert_fusion.8), channel_id=1, source_target_pairs={{0,8},{2,10},{4,12},{6,14},{8,0},{10,2},{12,4},{14,6},{16,24},{18,... | collective-permute-start | bytes 165896 | tf_op jit(solution)/shard_map/ppermute | solution.py:688
  271.3 17.5 %attend_back.2 = (f32[384,768]{1,0:T(8,128)}, f32[384,8]{1,0:T(8,128)}, f32[192,8]{1,0:T(8,128)}) custom-call(s32[1]{0:T(128)} %get-tuple-element.325.refs_0_, bf16[384,1024]{1,0:T(8,128)(2,1)} %get-tuple-element.107.refs_1_, bf16[384,1024]{1,0:T(8,128)(2,1)} %get-tuple-element.109.refs_2_, bf16[384,1024]{1,0:T(8,128)(2,1)} %copy-done.30, ...), custom_call_target="tpu_custom_call" | custom-call | flops 15000000512 | bytes 4194304 | tf_op jit(solution)/shard_map/attend_back/pallas_call | solution.py:618
  289.8 25.9 %attend_back.3 = (f32[384,768]{1,0:T(8,128)}, f32[384,8]{1,0:T(8,128)}, f32[192,8]{1,0:T(8,128)}) custom-call(s32[1]{0:T(128)} %get-tuple-element.326.refs_0_, bf16[384,1024]{1,0:T(8,128)(2,1)} %get-tuple-element.117.refs_1_, bf16[384,1024]{1,0:T(8,128)(2,1)} %get-tuple-element.125.refs_2_, bf16[384,1024]{1,0:T(8,128)(2,1)} %copy-done.29, ...), custom_call_target="tpu_custom_call" | custom-call | flops 15000000512 | bytes 4194304 | tf_op jit(solution)/shard_map/attend_back/pallas_call | solution.py:618
  315.7 1.4 add.228
  317.5 3.2 collective-permute-start.25
  322.7 1.8 collective-permute-done.25
  324.5 3.0 collective-permute-done.24
  328.1 31.9 %all_to_all.14 = bf16[16,24,776]{2,1,0:T(8,128)(2,1)S(1)} all-to-all(bf16[16,24,776]{2,1,0:T(8,128)(2,1)S(1)} %bitcast.87), channel_id=1, replica_groups=mesh['dp'=16,'ffn'=2] {'dp'}, dimensions={0} | all-to-all | bytes 1191936 | tf_op jit(solution)/shard_map/all_to_all | solution.py:703
  364.6 2.5 all-to-all-start.1
  367.4 6.8 %all-to-all-done.1 = f32[32,1,128]{2,1,0:T(1,128)S(1)} async-done(((f32[32,1,128]{2,1,0:T(1,128)}), f32[32,1,128]{2,1,0:T(1,128)S(1)}, u32[]{:S(2)}, u32[]{:S(2)}) %all-to-all-start.1) | async-done | bytes 16416 | tf_op jit(solution)/shard_map/all_to_all | solution.py:710
  (196 shorter events, 35.2 us)
Async XLA Ops:
  2.6 15.4 %collective-permute-start.1 = (bf16[1,1,1,1,24,776]{5,4,0,3,2,1:T(8,128)(2,1)S(1)}, bf16[1,1,1,1,24,776]{5,4,0,3,2,1:T(8,128)(2,1)S(1)}, u32[]{:S(2)}, u32[]{:S(2)}) collective-permute-start(bf16[1,1,1,1,24,776]{5,4,0,3,2,1:T(8,128)(2,1)S(1)} %pad_maximum_fusion.3), channel_id=1, source_target_pairs={{0,16},{2,18},{4,20},{6,22},{8,24},{10,26},{12,28},{14,30},{16,0},... | collective-permute-start | bytes 111752 | tf_op jit(solution)/shard_map/ppermute | solution.py:646
  8.7 17.1 %collective-permute-start = (bf16[1,1,1,1,24,2112]{5,4,0,1,3,2:T(8,128)(2,1)S(1)}, bf16[1,1,1,1,24,2112]{5,4,0,1,3,2:T(8,128)(2,1)S(1)}, u32[]{:S(2)}, u32[]{:S(2)}) collective-permute-start(bf16[1,1,1,1,24,2112]{5,4,0,1,3,2:T(8,128)(2,1)S(1)} %pad_maximum_fusion.1), channel_id=1, source_target_pairs={{0,16},{2,18},{4,20},{6,22},{8,24},{10,26},{12,28},{14,30},{16,0},... | collective-permute-start | bytes 304136 | tf_op jit(solution)/shard_map/ppermute | solution.py:646
  18.1 7.9 %collective-permute-start.3 = (bf16[2,1,1,1,24,776]{5,4,0,3,2,1:T(8,128)(2,1)S(1)}, bf16[2,1,1,1,24,776]{5,4,0,3,2,1:T(8,128)(2,1)S(1)}, u32[]{:S(2)}, u32[]{:S(2)}) collective-permute-start(bf16[2,1,1,1,24,776]{5,4,0,3,2,1:T(8,128)(2,1)S(1)} %fusion.5), channel_id=1, source_target_pairs={{0,8},{2,10},{4,12},{6,14},{8,0},{10,2},{12,4},{14,6},{16,24},{18,... | collective-permute-start | bytes 223496 | tf_op jit(solution)/shard_map/ppermute | solution.py:646
  25.9 9.9 %collective-permute-start.2 = (bf16[2,1,1,1,24,2112]{5,4,0,1,3,2:T(8,128)(2,1)S(1)}, bf16[2,1,1,1,24,2112]{5,4,0,1,3,2:T(8,128)(2,1)S(1)}, u32[]{:S(2)}, u32[]{:S(2)}) collective-permute-start(bf16[2,1,1,1,24,2112]{5,4,0,1,3,2:T(8,128)(2,1)S(1)} %maximum_select_fusion.6), channel_id=1, source_target_pairs={{0,8},{2,10},{4,12},{6,14},{8,0},{10,2},{12,4},{14,6},{16,24},{18,... | collective-permute-start | bytes 608264 | tf_op jit(solution)/shard_map/ppermute | solution.py:646
  26.1 9.4 %collective-permute-start.5 = (bf16[2,2,1,1,24,776]{5,4,3,2,1,0:T(8,128)(2,1)S(1)}, bf16[2,2,1,1,24,776]{5,4,3,2,1,0:T(8,128)(2,1)S(1)}, u32[]{:S(2)}, u32[]{:S(2)}) collective-permute-start(bf16[2,2,1,1,24,776]{5,4,3,2,1,0:T(8,128)(2,1)S(1)} %copy.193), channel_id=1, source_target_pairs={{0,4},{2,6},{4,0},{6,2},{8,12},{10,14},{12,8},{14,10},{16,20},{18,... | collective-permute-start | bytes 446984 | tf_op jit(solution)/shard_map/ppermute | solution.py:646
  35.6 8.5 %collective-permute-start.6 = (bf16[2,2,2,1,24,776]{5,4,3,2,1,0:T(8,128)(2,1)S(1)}, bf16[2,2,2,1,24,776]{5,4,3,2,1,0:T(8,128)(2,1)S(1)}, u32[]{:S(2)}, u32[]{:S(2)}) collective-permute-start(bf16[2,2,2,1,24,776]{5,4,3,2,1,0:T(8,128)(2,1)S(1)} %maximum_select_fusion.5), channel_id=1, source_target_pairs={{0,2},{2,0},{4,6},{6,4},{8,10},{10,8},{12,14},{14,12},{16,18},{18,... | collective-permute-start | bytes 893960 | tf_op jit(solution)/shard_map/ppermute | solution.py:646
  35.8 10.1 %collective-permute-start.4 = (bf16[2,2,1,1,24,2112]{5,4,0,1,3,2:T(8,128)(2,1)S(1)}, bf16[2,2,1,1,24,2112]{5,4,0,1,3,2:T(8,128)(2,1)S(1)}, u32[]{:S(2)}, u32[]{:S(2)}) collective-permute-start(bf16[2,2,1,1,24,2112]{5,4,0,1,3,2:T(8,128)(2,1)S(1)} %maximum_select_fusion.3), channel_id=1, source_target_pairs={{0,4},{2,6},{4,0},{6,2},{8,12},{10,14},{12,8},{14,10},{16,20},{18,... | collective-permute-start | bytes 1216520 | tf_op jit(solution)/shard_map/ppermute | solution.py:646
  46.1 22.8 %collective-permute-start.8 = (bf16[2,2,2,1,24,2112]{5,4,0,1,3,2:T(8,128)(2,1)S(1)}, bf16[2,2,2,1,24,2112]{5,4,0,1,3,2:T(8,128)(2,1)S(1)}, u32[]{:S(2)}, u32[]{:S(2)}) collective-permute-start(bf16[2,2,2,1,24,2112]{5,4,0,1,3,2:T(8,128)(2,1)S(1)} %maximum_select_fusion.1), channel_id=1, source_target_pairs={{0,2},{2,0},{4,6},{6,4},{8,10},{10,8},{12,14},{14,12},{16,18},{18,... | collective-permute-start | bytes 2433032 | tf_op jit(solution)/shard_map/ppermute | solution.py:646
  59.6 10.8 %collective-permute-start.12 = (bf16[384,1024]{1,0:T(8,128)(2,1)}, bf16[384,1024]{1,0:T(8,128)(2,1)S(1)}, u32[]{:S(2)}, u32[]{:S(2)}) collective-permute-start(bf16[384,1024]{1,0:T(8,128)(2,1)} %get-tuple-element.125.refs_2_), channel_id=1, source_target_pairs={{0,1},{1,0},{2,3},{3,2},{4,5},{5,4},{6,7},{7,6},{8,9},{9,8},{10,11... | collective-permute-start | bytes 2359304 | tf_op jit(solution)/shard_map/ppermute | solution.py:646
  68.3 12.7 %collective-permute-start.7 = (bf16[384,1024]{1,0:T(8,128)(2,1)}, bf16[384,1024]{1,0:T(8,128)(2,1)S(1)}, u32[]{:S(2)}, u32[]{:S(2)}) collective-permute-start(bf16[384,1024]{1,0:T(8,128)(2,1)} %get-tuple-element.109.refs_2_), channel_id=1, source_target_pairs={{0,1},{1,0},{2,3},{3,2},{4,5},{5,4},{6,7},{7,6},{8,9},{9,8},{10,11... | collective-permute-start | bytes 2359304 | tf_op jit(solution)/shard_map/ppermute | solution.py:646
  79.3 10.0 %collective-permute-start.13 = (bf16[384,1024]{1,0:T(8,128)(2,1)}, bf16[384,1024]{1,0:T(8,128)(2,1)S(1)}, u32[]{:S(2)}, u32[]{:S(2)}) collective-permute-start(bf16[384,1024]{1,0:T(8,128)(2,1)} %get-tuple-element.136.refs_3_.refs_2_), channel_id=1, source_target_pairs={{0,1},{1,0},{2,3},{3,2},{4,5},{5,4},{6,7},{7,6},{8,9},{9,8},{10,11... | collective-permute-start | bytes 2359304 | tf_op jit(solution)/shard_map/ppermute | solution.py:646
  88.8 77.4 %collective-permute-start.9 = (bf16[384,1024]{1,0:T(8,128)(2,1)}, bf16[384,1024]{1,0:T(8,128)(2,1)S(1)}, u32[]{:S(2)}, u32[]{:S(2)}) collective-permute-start(bf16[384,1024]{1,0:T(8,128)(2,1)} %get-tuple-element.128.refs_3_.refs_2_), channel_id=1, source_target_pairs={{0,1},{1,0},{2,3},{3,2},{4,5},{5,4},{6,7},{7,6},{8,9},{9,8},{10,11... | collective-permute-start | bytes 2359304 | tf_op jit(solution)/shard_map/ppermute | solution.py:646
  166.2 53.5 %collective-permute-start.14 = (bf16[384,1024]{1,0:T(8,128)(2,1)}, bf16[384,1024]{1,0:T(8,128)(2,1)S(1)}, u32[]{:S(2)}, u32[]{:S(2)}) collective-permute-start(bf16[384,1024]{1,0:T(8,128)(2,1)} %get-tuple-element.137.refs_4_), channel_id=1, source_target_pairs={{0,1},{1,0},{2,3},{3,2},{4,5},{5,4},{6,7},{7,6},{8,9},{9,8},{10,11... | collective-permute-start | bytes 2359304 | tf_op jit(solution)/shard_map/ppermute | solution.py:646
  218.1 14.6 %collective-permute-start.10 = (bf16[384,1024]{1,0:T(8,128)(2,1)}, bf16[384,1024]{1,0:T(8,128)(2,1)S(1)}, u32[]{:S(2)}, u32[]{:S(2)}) collective-permute-start(bf16[384,1024]{1,0:T(8,128)(2,1)} %get-tuple-element.129.refs_4_), channel_id=1, source_target_pairs={{0,1},{1,0},{2,3},{3,2},{4,5},{5,4},{6,7},{7,6},{8,9},{9,8},{10,11... | collective-permute-start | bytes 2359304 | tf_op jit(solution)/shard_map/ppermute | solution.py:646
  219.6 24.2 %collective-permute-start.16 = (bf16[2,2,2,1,24,576]{5,4,3,2,1,0:T(8,128)(2,1)S(1)}, bf16[2,2,2,1,24,576]{5,4,3,2,1,0:T(8,128)(2,1)S(1)}, u32[]{:S(2)}, u32[]{:S(2)}) collective-permute-start(bf16[2,2,2,1,24,576]{5,4,3,2,1,0:T(8,128)(2,1)S(1)} %dynamic-slice_convert_fusion.3), channel_id=1, source_target_pairs={{0,2},{2,0},{4,6},{6,4},{8,10},{10,8},{12,14},{14,12},{16,18},{18,... | collective-permute-start | bytes 663560 | tf_op jit(solution)/shard_map/ppermute | solution.py:688
  232.2 56.7 %collective-permute-start.15 = (bf16[384,1024]{1,0:T(8,128)(2,1)}, bf16[384,1024]{1,0:T(8,128)(2,1)S(1)}, u32[]{:S(2)}, u32[]{:S(2)}) collective-permute-start(bf16[384,1024]{1,0:T(8,128)(2,1)} %get-tuple-element.141.refs_5_), channel_id=1, source_target_pairs={{0,1},{1,0},{2,3},{3,2},{4,5},{5,4},{6,7},{7,6},{8,9},{9,8},{10,11... | collective-permute-start | bytes 2359304 | tf_op jit(solution)/shard_map/ppermute | solution.py:646
  243.6 7.9 %collective-permute-start.11 = (bf16[384,1024]{1,0:T(8,128)(2,1)}, bf16[384,1024]{1,0:T(8,128)(2,1)S(1)}, u32[]{:S(2)}, u32[]{:S(2)}) collective-permute-start(bf16[384,1024]{1,0:T(8,128)(2,1)} %get-tuple-element.133.refs_5_), channel_id=1, source_target_pairs={{0,1},{1,0},{2,3},{3,2},{4,5},{5,4},{6,7},{7,6},{8,9},{9,8},{10,11... | collective-permute-start | bytes 2359304 | tf_op jit(solution)/shard_map/ppermute | solution.py:646
  243.9 6.6 %collective-permute-start.17 = (bf16[2,2,1,1,24,576]{5,4,3,2,1,0:T(8,128)(2,1)S(1)}, bf16[2,2,1,1,24,576]{5,4,3,2,1,0:T(8,128)(2,1)S(1)}, u32[]{:S(2)}, u32[]{:S(2)}) collective-permute-start(bf16[2,2,1,1,24,576]{5,4,3,2,1,0:T(8,128)(2,1)S(1)} %dynamic-slice_convert_fusion.4), channel_id=1, source_target_pairs={{0,4},{2,6},{4,0},{6,2},{8,12},{10,14},{12,8},{14,10},{16,20},{18,... | collective-permute-start | bytes 331784 | tf_op jit(solution)/shard_map/ppermute | solution.py:688
  247.9 69.3 %collective-permute-start.20 = (bf16[2,2,1,1,24,1536]{5,4,3,2,1,0:T(8,128)(2,1)S(1)}, bf16[2,2,1,1,24,1536]{5,4,3,2,1,0:T(8,128)(2,1)S(1)}, u32[]{:S(2)}, u32[]{:S(2)}) collective-permute-start(bf16[2,2,1,1,24,1536]{5,4,3,2,1,0:T(8,128)(2,1)S(1)} %get-tuple-element.283), channel_id=1, source_target_pairs={{0,2},{2,0},{4,6},{6,4},{8,10},{10,8},{12,14},{14,12},{16,18},{18,... | collective-permute-start | bytes 884744 | tf_op jit(solution)/shard_map/ppermute | solution.py:688
  249.0 68.2 %collective-permute-start.22 = (bf16[2,2,1,1,24,1536]{5,4,3,2,1,0:T(8,128)(2,1)S(1)}, bf16[2,2,1,1,24,1536]{5,4,3,2,1,0:T(8,128)(2,1)S(1)}, u32[]{:S(2)}, u32[]{:S(2)}) collective-permute-start(bf16[2,2,1,1,24,1536]{5,4,3,2,1,0:T(8,128)(2,1)S(1)} %get-tuple-element.284), channel_id=1, source_target_pairs={{0,6},{2,4},{4,2},{6,0},{8,14},{10,12},{12,10},{14,8},{16,22},{18,... | collective-permute-start | bytes 884744 | tf_op jit(solution)/shard_map/ppermute | solution.py:688
  250.5 66.7 %collective-permute-start.21 = (bf16[2,2,1,1,24,1536]{5,4,3,2,1,0:T(8,128)(2,1)S(1)}, bf16[2,2,1,1,24,1536]{5,4,3,2,1,0:T(8,128)(2,1)S(1)}, u32[]{:S(2)}, u32[]{:S(2)}) collective-permute-start(bf16[2,2,1,1,24,1536]{5,4,3,2,1,0:T(8,128)(2,1)S(1)} %get-tuple-element.285), channel_id=1, source_target_pairs={{0,4},{2,6},{4,0},{6,2},{8,12},{10,14},{12,8},{14,10},{16,20},{18,... | collective-permute-start | bytes 884744 | tf_op jit(solution)/shard_map/ppermute | solution.py:688
  251.5 37.3 %collective-permute-start.18 = (bf16[2,1,1,1,24,576]{5,4,3,2,1,0:T(8,128)(2,1)S(1)}, bf16[2,1,1,1,24,576]{5,4,3,2,1,0:T(8,128)(2,1)S(1)}, u32[]{:S(2)}, u32[]{:S(2)}) collective-permute-start(bf16[2,1,1,1,24,576]{5,4,3,2,1,0:T(8,128)(2,1)S(1)} %dynamic-slice_convert_fusion.8), channel_id=1, source_target_pairs={{0,8},{2,10},{4,12},{6,14},{8,0},{10,2},{12,4},{14,6},{16,24},{18,... | collective-permute-start | bytes 165896 | tf_op jit(solution)/shard_map/ppermute | solution.py:688
  288.9 32.5 %collective-permute-start.19 = (bf16[1,1,1,1,24,576]{5,4,3,2,1,0:T(8,128)(2,1)S(1)}, bf16[1,1,1,1,24,576]{5,4,3,2,1,0:T(8,128)(2,1)S(1)}, u32[]{:S(2)}, u32[]{:S(2)}) collective-permute-start(bf16[1,1,1,1,24,576]{5,4,3,2,1,0:T(8,128)(2,1)S(1)} %dynamic-slice_convert_fusion.10), channel_id=1, source_target_pairs={{0,16},{2,18},{4,20},{6,22},{8,24},{10,26},{12,28},{14,30},{16,0},... | collective-permute-start | bytes 82952 | tf_op jit(solution)/shard_map/ppermute | solution.py:688
  317.4 5.2 %collective-permute-start.23 = (bf16[1,1,1,1,24,1536]{5,4,3,2,1,0:T(8,128)(2,1)S(1)}, bf16[1,1,1,1,24,1536]{5,4,3,2,1,0:T(8,128)(2,1)S(1)}, u32[]{:S(2)}, u32[]{:S(2)}) collective-permute-start(bf16[1,1,1,1,24,1536]{5,4,3,2,1,0:T(8,128)(2,1)S(1)} %get-tuple-element.290), channel_id=1, source_target_pairs={{0,8},{2,10},{4,12},{6,14},{8,0},{10,2},{12,4},{14,6},{16,24},{18,... | collective-permute-start | bytes 221192 | tf_op jit(solution)/shard_map/ppermute | solution.py:688
  317.5 6.9 %collective-permute-start.25 = (bf16[1,1,1,1,24,1536]{5,4,3,2,1,0:T(8,128)(2,1)S(1)}, bf16[1,1,1,1,24,1536]{5,4,3,2,1,0:T(8,128)(2,1)S(1)}, u32[]{:S(2)}, u32[]{:S(2)}) collective-permute-start(bf16[1,1,1,1,24,1536]{5,4,3,2,1,0:T(8,128)(2,1)S(1)} %get-tuple-element.291), channel_id=1, source_target_pairs={{0,24},{2,26},{4,28},{6,30},{8,16},{10,18},{12,20},{14,22},{16,8},... | collective-permute-start | bytes 221192 | tf_op jit(solution)/shard_map/ppermute | solution.py:688
  320.7 6.8 %collective-permute-start.24 = (bf16[1,1,1,1,24,1536]{5,4,3,2,1,0:T(8,128)(2,1)S(1)}, bf16[1,1,1,1,24,1536]{5,4,3,2,1,0:T(8,128)(2,1)S(1)}, u32[]{:S(2)}, u32[]{:S(2)}) collective-permute-start(bf16[1,1,1,1,24,1536]{5,4,3,2,1,0:T(8,128)(2,1)S(1)} %get-tuple-element.292), channel_id=1, source_target_pairs={{0,16},{2,18},{4,20},{6,22},{8,24},{10,26},{12,28},{14,30},{16,0},... | collective-permute-start | bytes 221192 | tf_op jit(solution)/shard_map/ppermute | solution.py:688
  322.0 53.7 %copy-start.19 = (f32[24,768]{1,0:T(8,128)S(1)}, f32[24,768]{1,0:T(8,128)}, u32[]{:S(2)}) copy-start(f32[24,768]{1,0:T(8,128)} %param.34) | copy-start | bytes 221188
  322.0 53.7 %copy-start.20 = (f32[24,768]{1,0:T(8,128)S(1)}, f32[24,768]{1,0:T(8,128)}, u32[]{:S(2)}) copy-start(f32[24,768]{1,0:T(8,128)} %param.39) | copy-start | bytes 221188
  322.0 53.7 %copy-start.21 = (f32[24,768]{1,0:T(8,128)S(1)}, f32[24,768]{1,0:T(8,128)}, u32[]{:S(2)}) copy-start(f32[24,768]{1,0:T(8,128)} %param.38) | copy-start | bytes 221188
  322.0 53.7 %copy-start.22 = (f32[24,768]{1,0:T(8,128)S(1)}, f32[24,768]{1,0:T(8,128)}, u32[]{:S(2)}) copy-start(f32[24,768]{1,0:T(8,128)} %param.33) | copy-start | bytes 221188
  364.6 9.6 %all-to-all-start.1 = ((f32[32,1,128]{2,1,0:T(1,128)}), f32[32,1,128]{2,1,0:T(1,128)S(1)}, u32[]{:S(2)}, u32[]{:S(2)}) async-start(f32[32,1,128]{2,1,0:T(1,128)} %broadcast_in_dim.26), calls=%async_computation.1 | async-start | bytes 32768 | tf_op jit(solution)/shard_map/all_to_all | solution.py:710
  367.2 10.2 %collective-permute-start.26 = (f32[24,776]{1,0:T(8,128)S(1)}, f32[24,776]{1,0:T(8,128)S(1)}, u32[]{:S(2)}, u32[]{:S(2)}) collective-permute-start(f32[24,776]{1,0:T(8,128)S(1)} %convert_reduce_fusion), channel_id=1, source_target_pairs={{0,1},{1,0},{2,3},{3,2},{4,5},{5,4},{6,7},{7,6},{8,9},{9,8},{10,11... | collective-permute-start | bytes 223496 | tf_op jit(solution)/shard_map/ppermute | solution.py:646
  (35 other events, 474.6 us)

commit v3 on v2

--- a/solution.py
+++ b/solution.py
@@ -22,7 +22,7 @@
 LOG2_E = 1.4426950408889634
 BLOCK = 256
 SAFE_EXPONENT = 100.0
-VMEM_BYTES = 56 * 2**20
+VMEM_BYTES = 64 * 2**20 - 2**17
 F32 = jnp.float32
 BF16 = jnp.bfloat16
 
@@ -129,7 +129,6 @@
 
 
 def teacher_kernel(traffic, len_ref, rows_ref, weight_ref, qt_ref, k_ref, vt_ref, v_ref, bound_ref):
-    flat = weight_ref.shape[0] // 3
     size = qt_ref.shape[1]
     bound_ref[...] = jnp.zeros(bound_ref.shape, F32)
 
@@ -137,12 +136,14 @@
         where = lanes(block)
         traffic.take(block)
         rows = rows_ref[where, :]
-        projected = nt(weight_ref[...], rows).astype(BF16)
-        bound_ref[...] = jnp.maximum(bound_ref[...], squared_lengths(projected, size))
-        split_heads(projected[:flat], qt_ref, where, size)
-        split_pairs(projected[flat : 2 * flat], k_ref, where)
-        split_heads(projected[2 * flat :], vt_ref, where, size)
-        split_pairs(projected[2 * flat :], v_ref, where)
+        queries, keys, values = [nn(rows, weight_ref[index]).astype(BF16) for index in range(3)]
+        columns = [part.T for part in (queries, keys, values)]
+        bound_ref[...] = jnp.maximum(bound_ref[...], squared_lengths(jnp.concatenate(columns, axis=0), size))
+        split_heads(columns[0], qt_ref, where, size)
+        split_heads(columns[2], vt_ref, where, size)
+        for pair in range(k_ref.shape[0]):
+            k_ref[pair, where, :] = keys[:, 2 * size * pair : 2 * size * (pair + 1)]
+            v_ref[pair, where, :] = values[:, 2 * size * pair : 2 * size * (pair + 1)]
         traffic.give(block, 0, 1, 2, 3)
         return carry
 
@@ -275,6 +276,22 @@
 
 
 def relation_kernel(
+    chained, traffic, len_ref, weight_ref, ht_ref, own_ref, other_ref, rel_ref, vec_ref, tqt_ref, tk_ref, tvt_ref, tv_ref,
+    tbound_ref, *refs,
+):
+    earlier_ref, refs = (refs[0], refs[1:]) if chained else (None, refs)
+    grad_out_ref, dt_ref, refs = refs[0], refs[1], refs[2:]
+    grad_ref, refs = refs[0], refs[1:]
+    relation_body(
+        traffic, len_ref, weight_ref, ht_ref, own_ref, other_ref, rel_ref, vec_ref, tqt_ref, tk_ref, tvt_ref, tv_ref,
+        tbound_ref, grad_ref, dt_ref, *refs,
+    )
+    traffic.take_last()
+    grad = grad_ref[...] + earlier_ref[...] if chained else grad_ref[...]
+    grad_out_ref[...] = grad.astype(grad_out_ref.dtype)
+
+
+def relation_body(
     traffic, len_ref, weight_ref, ht_ref, own_ref, other_ref, rel_ref, vec_ref, tqt_ref, tk_ref, tvt_ref, tv_ref,
     tbound_ref, grad_ref, dt_ref,
     h2_ref, qt_ref, kt_ref, vt_ref, q_ref, k_ref, v_ref, dqt_ref, dvt_ref, dk_ref, dv_ref, bound_ref,
@@ -320,19 +337,21 @@
         return jnp.logical_and(attention <= SAFE_EXPONENT**2, relation <= SAFE_EXPONENT)
 
     safe = jnp.logical_and(exponents(bound_ref, scaling), exponents(tbound_ref, teacher_scaling))
+    pairs = heads // 2
     attention = (k_ref, qt_ref, q_ref, tk_ref, tqt_ref, kt_ref, dqt_ref, dk_ref)
     relation = (v_ref, vt_ref, v_ref, tv_ref, tvt_ref, vt_ref, dvt_ref, dv_ref)
-    tasks = [(2 * pair + half, refs) for pair in range(heads // 2) for refs in (attention, relation) for half in range(2)]
-
-    def steps(n, where, mask, grow):
+    tasks = [(half, refs) for refs in (attention, relation) for half in range(2)]
+
+    def steps(n, pair, where, mask, grow):
         column = where.start + lax.broadcasted_iota(jnp.int32, (1, BLOCK), 1)
         live = jnp.where(column < length, weight, 0.0)
         kept = {}
 
         def first(t):
-            head, (left, rightt, _, teacher_left, teacher_rightt, _, _, _) = tasks[t]
-            student = nn(left[head // 2, : n * BLOCK, :], pad_rows(rightt[head, :, where], head % 2, 2))
-            teacher = nn(teacher_left[head // 2, : n * BLOCK, :], pad_rows(teacher_rightt[head, :, where], head % 2, 2))
+            half, (left, rightt, _, teacher_left, teacher_rightt, _, _, _) = tasks[t]
+            head = 2 * pair + half
+            student = nn(left[pair, : n * BLOCK, :], pad_rows(rightt[head, :, where], half, 2))
+            teacher = nn(teacher_left[pair, : n * BLOCK, :], pad_rows(teacher_rightt[head, :, where], half, 2))
             return student, teacher
 
         def second(t, scores):
@@ -342,25 +361,27 @@
             return (student * student_part - teacher * teacher_part).astype(BF16)
 
         def third(t, grad):
-            head, (_, _, right, _, _, leftt, own_ref, running_ref) = tasks[t]
+            half, (_, _, right, _, _, leftt, own_ref, running_ref) = tasks[t]
+            head = 2 * pair + half
             own_ref[head, :, where] = (nn(leftt[head, :, : n * BLOCK], grad) * plain).astype(own_ref.dtype)
-            kept[head % 2] = grad
-            if head % 2 == 1:
-                queries = right[head // 2, where, :]
-                stacked = jnp.concatenate([pad_lanes(queries, half, size) for half in range(2)], axis=0)
-                running_ref[head // 2, : n * BLOCK, :] += nn(jnp.concatenate([kept[0], kept[1]], axis=1), stacked)
+            kept[half] = grad
+            if half == 1:
+                queries = right[pair, where, :]
+                stacked = jnp.concatenate([pad_lanes(queries, i, size) for i in range(2)], axis=0)
+                running_ref[pair, : n * BLOCK, :] += nn(jnp.concatenate([kept[0], kept[1]], axis=1), stacked)
 
         return first, second, third
 
     def fast(n):
-        def step(block, carry):
+        def step(index, carry):
             stages = steps(
-                n, lanes(block), lambda score: mask_tail(score, n, length), lambda score, scale: jnp.exp2(score * scale)
+                n, index % pairs, lanes(index // pairs), lambda score: mask_tail(score, n, length),
+                lambda score, scale: jnp.exp2(score * scale),
             )
             pipeline(len(tasks), *stages)
             return carry
 
-        lax.fori_loop(0, n, step, 0)
+        lax.fori_loop(0, n * pairs, step, 0)
 
     def slow():
         most = rows // BLOCK
@@ -369,15 +390,15 @@
         def grow(score, scale):
             return jnp.exp2(score * scale - jnp.max(score, axis=0, keepdims=True) * scale)
 
-        def step(block, carry):
+        def step(index, carry):
             first, second, third = steps(
-                most, lanes(block), lambda score: mask_tail(score, most, length, 0), grow
+                most, index % pairs, lanes(index // pairs), lambda score: mask_tail(score, most, length, 0), grow
             )
             for t in range(len(tasks)):
                 third(t, second(t, first(t)))
             return carry
 
-        lax.fori_loop(0, blocks, step, 0)
+        lax.fori_loop(0, blocks * pairs, step, 0)
 
     for_size(blocks, rows // BLOCK, safe, fast, slow)
     grad_ref[...] = jnp.zeros(grad_ref.shape, F32)
@@ -398,11 +419,13 @@
 
 
 def feed_back_kernel(
-    traffic, len_ref, ht_ref, own_ref, other_ref, down_own_ref, down_other_ref, zt_ref, slope_ref, in_ref, out_ref, vec_ref,
-    grad_in_ref, grad_out_ref, sums_ref, resid_ref, up_ref,
+    chained, traffic, len_ref, ht_ref, own_ref, other_ref, down_own_ref, down_other_ref, zt_ref, slope_ref, in_ref, out_ref, vec_ref, *refs,
 ):
-    grad_in_ref[...] = jnp.zeros(grad_in_ref.shape, F32)
-    grad_out_ref[...] = jnp.zeros(grad_out_ref.shape, F32)
+    earlier, refs = (refs[:2], refs[2:]) if chained else (None, refs)
+    total_ref, sums_out_ref, resid_ref, up_ref, refs = *refs[:4], refs[4:]
+    grad_ref, sums_ref = refs
+    hidden_units = in_ref.shape[1]
+    grad_ref[...] = jnp.zeros(grad_ref.shape, F32)
     sums_ref[...] = jnp.zeros(sums_ref.shape, F32)
 
     def step(block, carry):
@@ -417,20 +440,63 @@
         sums_ref[:, 1:2] += jnp.sum(grad * normed, axis=1, keepdims=True)
         sums_ref[:, 2:3] += jnp.sum(grad, axis=1, keepdims=True)
         branch = resid.astype(BF16)
-        grad_out_ref[...] += nt(branch, zt_ref[:, where])
+        grad_ref[:, hidden_units:] += nt(branch, zt_ref[:, where])
         pre_grad = (tn(out_ref[...], branch) * slope_ref[:, where].astype(F32)).astype(BF16)
-        grad_in_ref[...] += nt(hidden.astype(BF16), pre_grad)
+        grad_ref[:, :hidden_units] += nt(hidden.astype(BF16), pre_grad)
         up_ref[:, where] = nn(in_ref[...], pre_grad).astype(BF16)
-        traffic.give(block, 3, 4)
+        traffic.give(block, 2, 3)
         return carry
 
     lax.fori_loop(0, live_blocks(len_ref), step, 0)
+    traffic.take_last()
+    grad, sums = grad_ref[...], sums_ref[...]
+    if chained:
+        grad, sums = grad + earlier[0][...], sums + earlier[1][...]
+    total_ref[...] = grad.astype(total_ref.dtype)
+    sums_out_ref[...] = sums
 
 
 def attend_back_kernel(
+    chained, last, traffic, len_ref, core_ref, xt_ref, own_ref, other_ref, resid_ref, up_own_ref, up_other_ref, weight_ref, vec_ref,
+    qt_ref, kt_ref, q_ref, k_ref, v_ref, ot_ref, lse_ref, *refs,
+):
+    back_sums_ref, refs = (refs[0], refs[1:]) if last else (None, refs)
+    earlier, refs = (refs[:3], refs[3:]) if chained else (None, refs)
+    outs, refs = (refs[:1], refs[1:]) if last else (refs[:3], refs[3:])
+    running, refs = refs[:3], refs[3:]
+    grad_ref, sums_ref, head_sums_ref = running
+    for ref in running:
+        ref[...] = jnp.zeros(ref.shape, F32)
+    attend_back_body(
+        traffic, len_ref, xt_ref, own_ref, other_ref, resid_ref, up_own_ref, up_other_ref, weight_ref, vec_ref,
+        qt_ref, kt_ref, q_ref, k_ref, v_ref, ot_ref, lse_ref, grad_ref, sums_ref, head_sums_ref, *refs,
+    )
+    traffic.take_last()
+    if chained:
+        for ref, value in zip(running, earlier):
+            ref[...] += value[...]
+    if not last:
+        for ref, value in zip(outs, running):
+            ref[...] = value[...]
+        return
+    total_ref = outs[0]
+    columns, flat = grad_ref.shape[1], head_sums_ref.shape[0]
+    total_ref[:, :columns] = grad_ref[...].astype(BF16)
+    biases = head_sums_ref[:, 0:2].astype(BF16)
+    total_ref[:, columns : columns + 2] = jnp.zeros((total_ref.shape[0], 2), BF16)
+    for core in range(total_ref.shape[0] // flat):
+
+        @pl.when(core_ref[0] == core)
+        def _(core=core):
+            total_ref[core * flat : (core + 1) * flat, columns : columns + 2] = biases
+
+    total_ref[:, columns + 2 : columns + 5] = sums_ref[:, 0:3].astype(BF16)
+    total_ref[:, columns + 5 : columns + 8] = back_sums_ref[:, 0:3].astype(BF16)
+
+
+def attend_back_body(
     traffic, len_ref, xt_ref, own_ref, other_ref, resid_ref, up_own_ref, up_other_ref, weight_ref, vec_ref,
-    qt_ref, kt_ref, q_ref, k_ref, v_ref, ot_ref, lse_ref,
-    grad_ref, sums_ref, head_sums_ref,
+    qt_ref, kt_ref, q_ref, k_ref, v_ref, ot_ref, lse_ref, grad_ref, sums_ref, head_sums_ref,
     dot_ref, do_ref, inner_ref, dqt_ref, dk_ref, dv_ref,
 ):
     heads, size, rows = qt_ref.shape
@@ -439,9 +505,6 @@
     scaling = LOG2_E * plain
     blocks = live_blocks(len_ref)
     length = len_ref[0]
-    sums_ref[...] = jnp.zeros(sums_ref.shape, F32)
-    head_sums_ref[...] = jnp.zeros(head_sums_ref.shape, F32)
-    grad_ref[...] = jnp.zeros(grad_ref.shape, F32)
 
     def start(block, carry):
         where = lanes(block)
@@ -523,27 +586,31 @@
     def __init__(self, blocks, ins, outs, in_sems, out_sems):
         self.blocks, self.ins, self.outs, self.in_sems, self.out_sems = blocks, ins, outs, in_sems, out_sems
 
-    def copy(self, source, target, axis, block, sem):
-        if axis is not None:
-            where = (slice(None),) * axis + (lanes(block),)
-            source, target = source.at[where], target.at[where]
-        return pltpu.make_async_copy(source, target, sem)
+    def part(self, ref, axis, block):
+        return ref if axis is None else ref.at[(slice(None),) * axis + (lanes(block),)]
 
     def inward(self, index, block):
-        source, target, axis, _ = self.ins[index]
-        return self.copy(source, target, axis, block, self.in_sems.at[index, block])
+        source, target, axis, _, first = self.ins[index]
+        if axis is None:
+            if first:
+                source = source.at[:, first[0] : first[0] + first[1]]
+            return pltpu.make_async_copy(source, target, self.in_sems.at[index, 0])
+        return pltpu.make_async_copy(
+            self.part(source, axis, first + block), self.part(target, axis, block), self.in_sems.at[index, block]
+        )
 
     def outward(self, index, block):
         target, source, axis = self.outs[index]
-        return self.copy(source, target, axis, block, self.out_sems.at[index, block])
-
-    def chosen(self, group):
-        return [i for i, entry in enumerate(self.ins) if entry[2] is not None and entry[3] == group]
+        return pltpu.make_async_copy(
+            self.part(source, axis, block), self.part(target, axis, block), self.out_sems.at[index, block]
+        )
+
+    def chosen(self, group, whole=False):
+        return [i for i, entry in enumerate(self.ins) if (entry[2] is None) == whole and entry[3] == group]
 
     def start(self):
-        for index, entry in enumerate(self.ins):
-            if entry[2] is None:
-                self.inward(index, 0).start()
+        for index in self.chosen(0, whole=True):
+            self.inward(index, 0).start()
         for group in (0, 1):
             indices = self.chosen(group)
 
@@ -554,9 +621,10 @@
 
             if indices:
                 lax.fori_loop(0, self.blocks, step, 0)
-        for index, entry in enumerate(self.ins):
-            if entry[2] is None:
-                self.inward(index, 0).wait()
+        for index in self.chosen(1, whole=True):
+            self.inward(index, 0).start()
+        for index in self.chosen(0, whole=True):
+            self.inward(index, 0).wait()
 
     def take(self, block):
         for index in self.chosen(0):
@@ -570,6 +638,10 @@
 
         lax.fori_loop(0, self.blocks, step, 0)
 
+    def take_last(self):
+        for index in self.chosen(1, whole=True):
+            self.inward(index, 0).wait()
+
     def give(self, block, *indices):
         for index in indices:
             self.outward(index, block).start()
@@ -591,22 +663,35 @@
             self.outward(index, 0).wait()
 
 
-def call(kernel, name, scalars, arrays, outs, scratch=(), flops=0):
+def call(blocks, kernel, name, scalars, arrays, outs, scratch=(), flops=0):
     smem = pl.BlockSpec(memory_space=pltpu.SMEM)
     hbm = pl.BlockSpec(memory_space=pl.ANY)
-    most = max(array.shape[axis] // BLOCK for array, axis, _ in arrays if axis is not None)
+    arrays = [entry if len(entry) == 4 else (*entry, 0) for entry in arrays]
+
+    def held(array, axis, group, first):
+        shape = list(array.shape)
+        if axis is not None:
+            shape[axis] = blocks * BLOCK
+        elif first:
+            shape[1] = first[1]
+        return pltpu.VMEM(tuple(shape), array.dtype)
+
     count, ins, results = len(scalars), len(arrays), len(outs)
+    copied = [i for i in range(ins) if arrays[i][2] is not None]
 
     def body(*refs):
         scalar_refs, refs = refs[:count], refs[count:]
         in_refs, refs = refs[:ins], refs[ins:]
         out_refs, refs = refs[:results], refs[results:]
-        in_copies, refs = refs[:ins], refs[ins:]
+        in_copies = list(in_refs)
+        for index, ref in zip(copied, refs):
+            in_copies[index] = ref
+        refs = refs[len(copied) :]
         out_copies, refs = refs[:results], refs[results:]
         in_sems, out_sems, refs = refs[0], refs[1], refs[2:]
         traffic = Traffic(
             live_blocks(scalar_refs[0]),
-            [(ref, copy, axis, group) for ref, copy, (_, axis, group) in zip(in_refs, in_copies, arrays)],
+            [(in_refs[i], in_copies[i], *arrays[i][1:]) for i in copied],
             [(ref, copy, axis) for ref, copy, (_, _, axis) in zip(out_refs, out_copies, outs)],
             in_sems,
             out_sems,
@@ -619,26 +704,20 @@
         body,
         name=name,
         out_shape=tuple(jax.ShapeDtypeStruct(shape, dtype) for shape, dtype, _ in outs),
-        in_specs=[smem] * count + [hbm] * ins,
+        in_specs=[smem] * count
+        + [hbm if group is not None else pl.BlockSpec(memory_space=pltpu.VMEM) for _, _, group, _ in arrays],
         out_specs=tuple(hbm for _ in outs),
-        scratch_shapes=[pltpu.VMEM(array.shape, array.dtype) for array, _, _ in arrays]
+        scratch_shapes=[held(*arrays[i]) for i in copied]
         + [pltpu.VMEM(shape, dtype) for shape, dtype, _ in outs]
-        + [pltpu.SemaphoreType.DMA((ins, most)), pltpu.SemaphoreType.DMA((results, most))]
+        + [pltpu.SemaphoreType.DMA((ins, blocks)), pltpu.SemaphoreType.DMA((results, blocks))]
         + [pltpu.VMEM(shape, dtype) for shape, dtype in scratch],
         compiler_params=pltpu.CompilerParams(vmem_limit_bytes=VMEM_BYTES),
         cost_estimate=pl.CostEstimate(flops=flops, bytes_accessed=4 << 20, transcendentals=0),
-    )(*scalars, *(array for array, _, _ in arrays))
+    )(*scalars, *(entry[0] for entry in arrays))
 
 
 def exchange(part):
     return swap(part, "ffn", 0)
-
-
-def total(parts):
-    result = parts[0]
-    for part in parts[1:]:
-        result = result + part
-    return result
 
 
 def swap(value, axis, bit):
@@ -664,37 +743,10 @@
     return jnp.where(upper, jnp.concatenate([other, whole], axis=dim), jnp.concatenate([whole, other], axis=dim))
 
 
-def split_rows(value):
-    bits = dp_bits()
-    return value.reshape((2,) * bits + (value.shape[0] >> bits,) + value.shape[1:])
-
-
-def reduce_step(part, bits, tokens=()):
-    count = dp_bits()
-    dims = [count - 1 - bit for bit in bits]
-    mine = [bit_of("dp", bit) for bit in bits]
-
-    def piece(flips):
-        result = part
-        for dim, bit, flip in zip(dims, mine, flips):
-            result = lax.dynamic_slice_in_dim(result, 1 - bit if flip else bit, 1, dim)
-        return result
-
-    size = lax.axis_size("dp")
-    arrived = []
-    for code in range(1, 1 << len(bits)):
-        flips = [(code >> i) & 1 for i in range(len(bits))]
-        mask = sum(flip << bit for flip, bit in zip(flips, bits))
-        arrived.append(lax.ppermute(piece(flips).astype(BF16), "dp", [(i, i ^ mask) for i in range(size)]))
-    kept = piece([0] * len(bits))
-
-    def finish(*tokens):
-        result = kept
-        for other in arrived:
-            result = result + (after(other, *tokens) if tokens else other).astype(F32)
-        return result
-
-    return finish
+def gather_direct(shard, *tokens):
+    count = lax.axis_size("dp")
+    spread = after(jnp.broadcast_to(shard[None], (count,) + shard.shape), *tokens)
+    return lax.all_to_all(spread, "dp", 0, 0, tiled=True).reshape((-1,) + shard.shape[1:])
 
 
 def reduce_owner(value):
@@ -746,12 +798,12 @@
     matched = domain_ids[:, None] == jnp.arange(domain_weight.shape[0])[None, :]
     sequence_weight = jnp.sum(jnp.where(matched, domain_weight[None, :], 0.0), axis=1) / HEADS
 
-    teacher_w = teacher_qkv.reshape(teacher_qkv.shape[0], -1).T
+    teacher_w = teacher_qkv.transpose(1, 0, 2)
     statest = states.T
     live = [lengths[i : i + 1] for i in range(sequences)]
     weights = [sequence_weight[i : i + 1] for i in range(sequences)]
-    xt = [statest[:, i * rows : (i + 1) * rows] for i in range(sequences)]
     each = range(sequences)
+    launch = functools.partial(call, rows // BLOCK)
     act = ((features, rows), BF16)
     wide = ((features, rows), F32)
     head_t = ((heads, size, rows), BF16)
@@ -760,9 +812,9 @@
     bound_rows = -(-3 * heads // 8) * 8
 
     def project_teacher(i, token):
-        return call(
+        return launch(
             teacher_kernel, "teacher", (live[i],),
-            ((after(teacher_states[i * rows : (i + 1) * rows], token), 0, 0), (teacher_w, None, 0)),
+            ((after(teacher_states, *token), 0, 0, i * rows // BLOCK), (teacher_w, None, 0)),
             (
                 ((heads, teacher_size, rows), BF16, 2),
                 ((pairs, rows, 2 * teacher_size), BF16, 1),
@@ -774,34 +826,19 @@
         )
 
     attn_own = lax.dynamic_slice_in_dim(attn_a.reshape(shard, 4, features), core * flat, flat, 2).reshape(shard, 4 * flat)
-    bits = dp_bits()
-    unit = (1,) * bits
-    early = jnp.concatenate([attn_own, vec_d], axis=1).astype(BF16).reshape(unit + (shard, -1))
-    late = jnp.concatenate([ffn_in, ffn_out, attn_b.reshape(shard, 3 * flat)], axis=1).astype(BF16)
-    late = late.reshape(unit + (shard, -1))
-    teacher = []
-    for step, bit in enumerate(range(bits)[::-1]):
-        early_other = swap(early, "dp", bit)
-        late_other = swap(late, "dp", bit + 1) if step else None
-        if step == 0:
-            tokens = (teacher_w, statest)
-        elif step <= sequences:
-            teacher.append(project_teacher(step - 1, early))
-            tokens = teacher[-1]
-        else:
-            tokens = ()
-        early = gather_step(early, after(early_other, *tokens), bit)
-        if step:
-            late = gather_step(late, after(late_other, *tokens), bit + 1)
-    early = early.reshape(features, -1)
-    attn_full, vec_full = early[:, : 4 * flat], early[:, 4 * flat :].astype(F32)
+    early = gather_direct(jnp.concatenate([attn_own, vec_d], axis=1).astype(BF16))
+    teacher = [project_teacher(0, (statest,))]
+    late_feed = gather_direct(jnp.concatenate([ffn_in, ffn_out], axis=1).astype(BF16), *teacher[0])
+    teacher += [project_teacher(i, teacher[0]) for i in each[1:]]
+    early = after(early, *teacher[1])
+    vec_full = early[:, 4 * flat :].astype(F32)
     vec_own = lax.dynamic_slice_in_dim(vec_full, core * flat, flat, 0)
-    late_other = swap(late, "dp", 0)
+    attn_full = (early, None, 0, (0, 4 * flat))
 
     attended = [
-        call(
+        launch(
             attend_kernel, "attend", (live[i],),
-            ((after(xt[i], late), 1, 0), (attn_full, None, 0), (vec_own, None, 0)),
+            ((statest, 1, 0, i * rows // BLOCK), attn_full, (vec_own, None, 0)),
             ((*head_t, 2), (*head_t, 2), (*pair_rows, 1), (*pair_rows, 1), (*pair_rows, 1),
              ((heads, size, rows), F32, 2), ((heads, 8, rows), F32, 2), (*act, 1)),
             scratch=(((heads, size + 16, rows), BF16), ((-(-2 * heads // 8) * 8, BLOCK), F32)),
@@ -809,89 +846,85 @@
         )
         for i in each
     ]
-    late = gather_step(late, after(late_other, *attended), 0).reshape(features, -1)
-    in_full, out_full, rel_full = late[:, :hidden], late[:, hidden : 2 * hidden], late[:, 2 * hidden :]
+    in_full, out_full = (late_feed, None, 0, (0, hidden)), (late_feed, None, 0, (hidden, hidden))
+    late_rel = gather_direct(after(attn_b.reshape(shard, 3 * flat).astype(BF16), *attended[0]))
+    rel_full = (late_rel, None, 0)
     mixed_other = [exchange(attended[i][7]) for i in each]
     fed = [
-        call(
+        launch(
             feed_kernel, "feed", (live[i],),
-            ((xt[i], 1, 0), (attended[i][7], 1, 0), (mixed_other[i], 1, 0), (in_full, None, 0), (out_full, None, 0),
-             (vec_full, None, 0)),
+            ((statest, 1, 0, i * rows // BLOCK), (attended[i][7], 1, 0), (mixed_other[i], None, None), in_full,
+             out_full, (vec_full, None, 0)),
             ((*wide, 1), ((hidden, rows), BF16, 1), ((hidden, rows), BF16, 1), (*act, 1)),
             flops=3 * 10**9,
         )
         for i in each
     ]
     fed_other = [exchange(fed[i][3]) for i in each]
-    related = [
-        call(
-            relation_kernel, "relation", (live[i], weights[i]),
-            ((fed[i][0], 1, 0), (fed[i][3], 1, 0), (fed_other[i], 1, 0), (rel_full, None, 0), (vec_full, None, 0),
-             (teacher[i][0], 2, 1), (teacher[i][1], 1, 1), (teacher[i][2], 2, 1), (teacher[i][3], 1, 1),
-             (teacher[i][4], None, 0)),
-            (((features, 3 * flat), F32, None), (*act, 1)),
+
+    def relate(i, earlier):
+        last = i + 1 == sequences
+        return launch(
+            functools.partial(relation_kernel, bool(earlier)), "relation", (live[i], weights[i]),
+            ((fed[i][0], 1, 0), (fed[i][3], 1, 0), (fed_other[i], None, None), rel_full,
+             (vec_full, None, 0), (teacher[i][0], 2, 1), (teacher[i][1], 1, 1), (teacher[i][2], 2, 1),
+             (teacher[i][3], 1, 1), (teacher[i][4], None, 0), *((value, None, 1) for value in earlier)),
+            (((features, 3 * flat), BF16 if last else F32, None), (*act, 1)),
             scratch=(
-                act, head_t, head_t, head_t, pair_rows, pair_rows, pair_rows,
+                ((features, 3 * flat), F32), act, head_t, head_t, head_t, pair_rows, pair_rows, pair_rows,
                 head_t, ((heads, size, rows), F32),
                 ((pairs, rows, 2 * size), F32), ((pairs, rows, 2 * size), F32), ((bound_rows, BLOCK), F32),
             ),
             flops=30 * 10**9,
         )
-        for i in each
-    ]
-    down_other = [exchange(related[i][1]) for i in each]
-    rel_part = split_rows(total([related[i][0] for i in each]))
+
+    def feed_back(i, earlier):
+        last = i + 1 == sequences
+        sums = ((features, 8), F32)
+        return launch(
+            functools.partial(feed_back_kernel, bool(earlier)), "feed_back", (live[i],),
+            ((fed[i][0], 1, 0), (fed[i][3], 1, 0), (fed_other[i], None, None), (related[i][1], 1, 0),
+             (down_other[i], None, None), (fed[i][1], 1, 0), (fed[i][2], 1, 0), in_full,
+             out_full, (vec_full, None, 0), *((value, None, 1) for value in earlier)),
+            (((features, 2 * hidden), BF16 if last else F32, None), (*sums, None), (*wide, 1), (*act, 1)),
+            scratch=(((features, 2 * hidden), F32), sums),
+            flops=4 * 10**9,
+        )
+
+    def attend_back(i, earlier):
+        last = i + 1 == sequences
+        running = (((features, 4 * flat), F32), ((features, 8), F32), ((flat, 8), F32))
+        return launch(
+            functools.partial(attend_back_kernel, bool(earlier), last), "attend_back",
+            (live[i], core.reshape(1).astype(jnp.int32)),
+            ((statest, 1, 0, i * rows // BLOCK), (attended[i][7], 1, 0), (mixed_other[i], None, None), (fed_back[i][2], 1, 0),
+             (fed_back[i][3], 1, 0), (up_other[i], None, None), attn_full, (vec_full, None, 0),
+             (attended[i][0], 2, 1), (attended[i][1], 2, 1), (attended[i][2], 1, 1), (attended[i][3], 1, 1),
+             (attended[i][4], 1, 1), (attended[i][5], 2, 0), (attended[i][6], 2, 1),
+             *([(fed_back[i][1], None, 0)] if last else []), *((value, None, 1) for value in earlier)),
+            (((features, 4 * flat + 8), BF16, None),) if last else tuple((*spec, None) for spec in running),
+            scratch=running + (
+                head_t, pair_rows, ((heads, 8, rows), F32), head_t,
+                ((pairs, rows, 2 * size), F32), ((pairs, rows, 2 * size), F32),
+            ),
+            flops=15 * 10**9,
+        )
+
+    related, down_other = [], []
+    for i in each:
+        related.append(relate(i, related[-1][:1] if related else ()))
+        down_other.append(exchange(related[i][1]))
+    shard_rel = reduce_owner(related[-1][0])
     fed_back, up_other = [], []
     for i in each:
-        finish = reduce_step(rel_part, (i,))
-        fed_back.append(
-            call(
-                feed_back_kernel, "feed_back", (live[i],),
-                ((fed[i][0], 1, 0), (fed[i][3], 1, 0), (fed_other[i], 1, 0), (related[i][1], 1, 0), (down_other[i], 1, 0),
-                 (fed[i][1], 1, 0), (fed[i][2], 1, 0), (in_full, None, 0), (out_full, None, 0), (vec_full, None, 0)),
-                (((features, hidden), F32, None), ((features, hidden), F32, None), ((features, 8), F32, None),
-                 (*wide, 1), (*act, 1)),
-                flops=4 * 10**9,
-            )
-        )
-        rel_part = finish(*fed_back[i])
-        up_other.append(exchange(fed_back[i][4]))
-    feed_part = split_rows(
-        total([jnp.concatenate([fed_back[i][0], fed_back[i][1]], axis=1) for i in each])
-    )
+        fed_back.append(feed_back(i, fed_back[-1][:2] if fed_back else ()))
+        up_other.append(exchange(fed_back[i][3]))
+    shard_feed = reduce_owner(fed_back[-1][0])
     attended_back = []
-    groups = ((0, 1), tuple(range(2, bits)))
     for i in each:
-        finish_feed = reduce_step(feed_part, groups[i])
-        finish_rel = reduce_step(rel_part, (2 + i,)) if i + 1 < sequences else reduce_step(rel_part, tuple(range(2 + i, bits)))
-        attended_back.append(
-            call(
-                attend_back_kernel, "attend_back", (live[i],),
-                ((xt[i], 1, 0), (attended[i][7], 1, 0), (mixed_other[i], 1, 0), (fed_back[i][3], 1, 0),
-                 (fed_back[i][4], 1, 0), (up_other[i], 1, 0), (attn_full, None, 0), (vec_full, None, 0),
-                 (attended[i][0], 2, 1), (attended[i][1], 2, 1), (attended[i][2], 1, 1), (attended[i][3], 1, 1),
-                 (attended[i][4], 1, 1), (attended[i][5], 2, 0), (attended[i][6], 2, 1)),
-                (((features, 4 * flat), F32, None), ((features, 8), F32, None), ((flat, 8), F32, None)),
-                scratch=(
-                    head_t, pair_rows, ((heads, 8, rows), F32), head_t,
-                    ((pairs, rows, 2 * size), F32), ((pairs, rows, 2 * size), F32),
-                ),
-                flops=15 * 10**9,
-            )
-        )
-        feed_part = finish_feed(*attended_back[i])
-        rel_part = finish_rel(*attended_back[i])
-
-    shard_rel = rel_part.reshape(shard, -1)
-    shard_feed = feed_part.reshape(shard, -1)
+        attended_back.append(attend_back(i, attended_back[-1] if attended_back else ()))
     shard_in, shard_out = shard_feed[:, :hidden], shard_feed[:, hidden:]
-    back_sums = total([fed_back[i][2] for i in each])
-    first_sums = total([attended_back[i][1] for i in each])
-    head_sums = total([attended_back[i][2] for i in each])
-    placed = lax.dynamic_update_slice_in_dim(jnp.zeros((features, 2), F32), head_sums[:, :2], core * flat, 0)
-    attn_local = total([attended_back[i][0] for i in each])
-    own = jnp.concatenate([attn_local, placed, first_sums[:, :3], back_sums[:, :3]], axis=1)
-    own = reduce_owner(after(own, shard_rel, shard_feed))
+    own = reduce_owner(after(attended_back[-1][0], shard_rel, shard_feed))
     other = swap(own, "ffn", 0)
     grad_rel = shard_rel.reshape(attn_b.shape)
     upper = core == 1

time: 379 us -> 376 us (level); the launches traced: 381 us -> 369 us
  starting transfers between devices: 45.1 us -> 186 us
  Pallas kernels: 239 us -> 102 us
  waiting for transfers between devices: 18.4 us -> 51.9 us
  blocking collectives: 31.9 us -> 0 us
  local copies, waits for them, and re-layouts: 24.2 us -> 9.69 us
    all_to_all x0 -> x6, starting transfers between devices: none -> 179 us  [the longest x3 151 us: reduce_owner(): lax.all_to_all(value.astype(BF16).reshape((count, rows) + value.shape[1:]...]
    pallas_call x12, Pallas kernels: 239 us -> 102 us  [call(): pl.pallas_call(body, name=name, out_shape=tuple((jax.ShapeDtypeStruct(sha...]
    all_to_all x0 -> x6, waiting for transfers between devices: none -> 45.2 us  [the longest x3 25.8 us: reduce_owner(): lax.all_to_all(value.astype(BF16).reshape((count, rows) + value.shape[1:]...]
    all_to_all x1 -> x0, blocking collectives: 31.9 us -> none  [reduce_owner(): lax.all_to_all(value.astype(BF16).reshape((count, rows) + value.shape[1:]...]
    ppermute x10 -> x0, starting transfers between devices: 27.4 us -> none  [reduce_step(): lax.ppermute(piece(flips).astype(BF16), 'dp', [(i, i ^ mask) for i in ran...]
    ppermute x17 -> x9, starting transfers between devices: 15.1 us -> 2.83 us  [swap(): return lax.ppermute(value, axis, [(i, i ^ 1 << bit) for i in range(count)])]
    unnamed x80 -> x45, local copies, waits for them, and re-layouts: 13.2 us -> 2.45 us
    ppermute x17 -> x9, waiting for transfers between devices: 6.19 us -> 0.02 us  [swap(): return lax.ppermute(value, axis, [(i, i ^ 1 << bit) for i in range(count)])]
  transfers between devices with their start and end apart: 28 -> 16, of which waited for: 5 -> 6; matrix products, arithmetic and copies ran while one was open for 6% -> 4% of each run, Pallas kernels for 63% -> 28%
where the time goes in v3:
time: 376 us; the launch traced here: 369 us
  starting transfers between devices  186 us (49%)
  Pallas kernels  102 us (27%)
  waiting for transfers between devices  51.9 us (14%)
  other arithmetic  12.9 us (3%)
  local copies, waits for them, and re-layouts  9.69 us (3%)
  between operations  6.16 us (2%)
    all_to_all x3, starting transfers between devices, reduce_owner(): lax.all_to_all(value.astype(BF16).reshape((count, rows) + value.shape[1:]...  151 us
    pallas_call x12, Pallas kernels, call(): pl.pallas_call(body, name=name, out_shape=tuple((jax.ShapeDtypeStruct(sha...  102 us
    all_to_all x3, starting transfers between devices, gather_direct(): lax.all_to_all(spread, 'dp', 0, 0, tiled=True)  28 us
    all_to_all x3, waiting for transfers between devices, reduce_owner(): lax.all_to_all(value.astype(BF16).reshape((count, rows) + value.shape[1:]...  25.8 us
    all_to_all x3, waiting for transfers between devices, gather_direct(): lax.all_to_all(spread, 'dp', 0, 0, tiled=True)  19.4 us
  transfers between devices with their start and end apart: 16, of which 6 were waited for; matrix products, arithmetic and copies ran while one was open for 4% of the time, Pallas kernels for 28%

profile of v3, /device:TPU:0, one launch (start us, length us, event | category | flops | bytes accessed | tf_op | source)
XLA Modules:
  0.0 368.5 jit_solution(13299869572303161778)
XLA Ops:
  0.7 1.0 reshape.103
  2.7 0.9 broadcast_in_dim.20
  3.6 8.4 %all-to-all-start = ((bf16[16,24,776]{2,1,0:T(8,128)(2,1)}), bf16[16,24,776]{2,1,0:T(8,128)(2,1)}, u32[]{:S(2)}, u32[]{:S(2)}) async-start(bf16[16,24,776]{2,1,0:T(8,128)(2,1)} %broadcast_in_dim.20), calls=%async_computation | async-start | bytes 1376256 | tf_op jit(solution)/shard_map/all_to_all | solution.py:749
  12.0 1.7 copy.117
  14.9 4.1 %teacher.2 = (bf16[6,64,1024]{2,1,0:T(8,128)(2,1)}, bf16[3,1024,128]{2,1,0:T(8,128)(2,1)}, bf16[6,64,1024]{2,1,0:T(8,128)(2,1)}, bf16[3,1024,128]{2,1,0:T(8,128)(2,1)}, f32[24,256]{1,0:T(8,128)}) custom-call(s32[1]{0:T(128)} %get-tuple-element.254.refs_0_, bf16[2048,768]{1,0:T(8,128)(2,1)} %refs_1_.1, bf16[3,768,384]{2,1,0:T(8,128)(2,1)} %bitcast.20), custom_call_target="tpu_custom_call" | custom-call | flops 1811939328 | bytes 4194304 | tf_op jit(solution)/shard_map/teacher/pallas_call | solution.py:703
  19.8 1.1 broadcast_in_dim.21
  20.9 9.1 %all-to-all-done = bf16[16,24,776]{2,1,0:T(8,128)(2,1)} async-done(((bf16[16,24,776]{2,1,0:T(8,128)(2,1)}), bf16[16,24,776]{2,1,0:T(8,128)(2,1)}, u32[]{:S(2)}, u32[]{:S(2)}) %all-to-all-start) | async-done | bytes 596000 | tf_op jit(solution)/shard_map/all_to_all | solution.py:749
  30.0 4.6 %all-to-all-start.1 = ((bf16[16,24,1536]{2,1,0:T(8,128)(2,1)}), bf16[16,24,1536]{2,1,0:T(8,128)(2,1)}, u32[]{:S(2)}, u32[]{:S(2)}) async-start(bf16[16,24,1536]{2,1,0:T(8,128)(2,1)} %broadcast_in_dim.21), calls=%async_computation.1 | async-start | bytes 2359296 | tf_op jit(solution)/shard_map/all_to_all | solution.py:749
  34.6 4.1 %teacher.3 = (bf16[6,64,1024]{2,1,0:T(8,128)(2,1)}, bf16[3,1024,128]{2,1,0:T(8,128)(2,1)}, bf16[6,64,1024]{2,1,0:T(8,128)(2,1)}, bf16[3,1024,128]{2,1,0:T(8,128)(2,1)}, f32[24,256]{1,0:T(8,128)}) custom-call(s32[1]{0:T(128)} %get-tuple-element.255.refs_0_, bf16[2048,768]{1,0:T(8,128)(2,1)} %refs_1_.1, bf16[3,768,384]{2,1,0:T(8,128)(2,1)} %bitcast.21), custom_call_target="tpu_custom_call" | custom-call | flops 1811939328 | bytes 4194304 | tf_op jit(solution)/shard_map/teacher/pallas_call | solution.py:703
  38.8 0.9 slice_convert_fusion.refs_6_.refs_10_.refs_9_
  41.0 4.5 %attend.3 = (bf16[6,32,1024]{2,1,0:T(8,128)(2,1)}, bf16[6,32,1024]{2,1,0:T(8,128)(2,1)}, bf16[3,1024,64]{2,1,0:T(8,128)(2,1)}, bf16[3,1024,64]{2,1,0:T(8,128)(2,...) custom-call(s32[1]{0:T(128)} %get-tuple-element.254.refs_0_, ...), custom_call_target="tpu_custom_call" | custom-call | flops 6000000000 | bytes 4194304 | tf_op jit(solution)/shard_map/attend/pallas_call | solution.py:703
  47.4 4.6 %attend.2 = (bf16[6,32,1024]{2,1,0:T(8,128)(2,1)}, bf16[6,32,1024]{2,1,0:T(8,128)(2,1)}, bf16[3,1024,64]{2,1,0:T(8,128)(2,1)}, bf16[3,1024,64]{2,1,0:T(8,128)(2,...) custom-call(s32[1]{0:T(128)} %get-tuple-element.255.refs_0_, ...), custom_call_target="tpu_custom_call" | custom-call | flops 6000000000 | bytes 4194304 | tf_op jit(solution)/shard_map/attend/pallas_call | solution.py:703
  52.6 8.1 %all-to-all-done.1 = bf16[16,24,1536]{2,1,0:T(8,128)(2,1)} async-done(((bf16[16,24,1536]{2,1,0:T(8,128)(2,1)}), bf16[16,24,1536]{2,1,0:T(8,128)(2,1)}, u32[]{:S(2)}, u32[]{:S(2)}) %all-to-all-start.1) | async-done | bytes 1179680 | tf_op jit(solution)/shard_map/all_to_all | solution.py:749
  60.7 15.1 %all-to-all-start.2 = ((bf16[16,24,576]{2,1,0:T(8,128)(2,1)}), bf16[16,24,576]{2,1,0:T(8,128)(2,1)}, u32[]{:S(2)}, u32[]{:S(2)}) async-start(bf16[16,24,576]{2,1,0:T(8,128)(2,1)} %broadcast_in_dim.24), calls=%async_computation.2 | async-start | bytes 983040 | tf_op jit(solution)/shard_map/all_to_all | solution.py:749
  75.8 5.5 %feed.3 = (f32[384,1024]{1,0:T(8,128)}, bf16[768,1024]{1,0:T(8,128)(2,1)}, bf16[768,1024]{1,0:T(8,128)(2,1)}, bf16[384,1024]{1,0:T(8,128)(2,1)}) custom-call(s32[1]{0:T(128)} %get-tuple-element.254.refs_0_, bf16[384,2048]{1,0:T(8,128)(2,1)} %bitcast.12, bf16[384,1024]{1,0:T(8,128)(2,1)} %get-tuple-element.95.refs_2_.refs_3_, ...), custom_call_target="tpu_custom_call" | custom-call | flops 3000000000 | bytes 4194304 | tf_op jit(solution)/shard_map/feed/pallas_call | solution.py:703
  82.2 5.5 %feed.2 = (f32[384,1024]{1,0:T(8,128)}, bf16[768,1024]{1,0:T(8,128)(2,1)}, bf16[768,1024]{1,0:T(8,128)(2,1)}, bf16[384,1024]{1,0:T(8,128)(2,1)}) custom-call(s32[1]{0:T(128)} %get-tuple-element.255.refs_0_, bf16[384,2048]{1,0:T(8,128)(2,1)} %bitcast.13, bf16[384,1024]{1,0:T(8,128)(2,1)} %get-tuple-element.84.refs_2_.refs_3_, ...), custom_call_target="tpu_custom_call" | custom-call | flops 3000000000 | bytes 4194304 | tf_op jit(solution)/shard_map/feed/pallas_call | solution.py:703
  88.3 2.2 all-to-all-done.2
  90.5 21.0 %relation.2 = (f32[384,576]{1,0:T(8,128)}, bf16[384,1024]{1,0:T(8,128)(2,1)}) custom-call(s32[1]{0:T(128)} %get-tuple-element.254.refs_0_, f32[1]{0:T(128)} %get-tuple-element.252.refs_1_, f32[384,1024]{1,0:T(8,128)} %get-tuple-element.97.refs_2_.refs_1_, bf16[384,1024]{1,0:T(8,128)(2,1)} %get-tuple-element.98.refs_3_.refs_2_, ...), custom_call_target="tpu_custom_call" | custom-call | flops 30000001024 | bytes 4194304 | tf_op jit(solution)/shard_map/relation/pallas_call | solution.py:703
  111.6 21.1 %relation.3 = (bf16[384,576]{1,0:T(8,128)(2,1)}, bf16[384,1024]{1,0:T(8,128)(2,1)}) custom-call(s32[1]{0:T(128)} %get-tuple-element.255.refs_0_, f32[1]{0:T(128)} %get-tuple-element.253.refs_1_, f32[384,1024]{1,0:T(8,128)} %get-tuple-element.86.refs_2_.refs_1_, bf16[384,1024]{1,0:T(8,128)(2,1)} %get-tuple-element.87.refs_3_.refs_2_, ...), custom_call_target="tpu_custom_call" | custom-call | flops 30000001024 | bytes 4194304 | tf_op jit(solution)/shard_map/relation/pallas_call | solution.py:703
  133.3 99.9 %all-to-all-start.3 = ((bf16[16,24,576]{2,1,0:T(8,128)(2,1)}), bf16[16,24,576]{2,1,0:T(8,128)(2,1)}, u32[]{:S(2)}, u32[]{:S(2)}) async-start(bf16[16,24,576]{2,1,0:T(8,128)(2,1)} %bitcast.18), calls=%async_computation.3 | async-start | bytes 983040 | tf_op jit(solution)/shard_map/all_to_all | solution.py:755
  233.1 7.7 %feed_back.2 = (f32[384,1536]{1,0:T(8,128)}, f32[384,8]{1,0:T(8,128)}, f32[384,1024]{1,0:T(8,128)}, bf16[384,1024]{1,0:T(8,128)(2,1)}) custom-call(s32[1]{0:T(128)} %get-tuple-element.254.refs_0_, f32[384,1024]{1,0:T(8,128)} %get-tuple-element.97.refs_2_.refs_1_, bf16[384,1024]{1,0:T(8,128)(2,1)} %get-tuple-element.98.refs_3_.refs_2_, ...), custom_call_target="tpu_custom_call" | custom-call | flops 4000000000 | bytes 4194304 | tf_op jit(solution)/shard_map/feed_back/pallas_call | solution.py:703
  241.1 7.5 %feed_back.3 = (bf16[384,1536]{1,0:T(8,128)(2,1)}, f32[384,8]{1,0:T(8,128)}, f32[384,1024]{1,0:T(8,128)}, bf16[384,1024]{1,0:T(8,128)(2,1)}) custom-call(s32[1]{0:T(128)} %get-tuple-element.255.refs_0_, f32[384,1024]{1,0:T(8,128)} %get-tuple-element.86.refs_2_.refs_1_, bf16[384,1024]{1,0:T(8,128)(2,1)} %get-tuple-element.87.refs_3_.refs_2_, ...), custom_call_target="tpu_custom_call" | custom-call | flops 4000000000 | bytes 4194304 | tf_op jit(solution)/shard_map/feed_back/pallas_call | solution.py:703
  249.1 16.5 %all-to-all-start.4 = ((bf16[16,24,1536]{2,1,0:T(8,128)(2,1)}), bf16[16,24,1536]{2,1,0:T(8,128)(2,1)}, u32[]{:S(2)}, u32[]{:S(2)}) async-start(bf16[16,24,1536]{2,1,0:T(8,128)(2,1)} %bitcast.16), calls=%async_computation.4 | async-start | bytes 2359296 | tf_op jit(solution)/shard_map/all_to_all | solution.py:755
  265.6 1.1 convert_reduce_fusion.2
  266.7 8.1 %attend_back.2 = (f32[384,768]{1,0:T(8,128)}, f32[384,8]{1,0:T(8,128)}, f32[192,8]{1,0:T(8,128)}) custom-call(s32[1]{0:T(128)} %get-tuple-element.254.refs_0_, s32[1]{0:T(128)} %bitcast.refs_1_, bf16[384,2048]{1,0:T(8,128)(2,1)} %bitcast.14, bf16[384,1024]{1,0:T(8,128)(2,1)} %get-tuple-element.95.refs_2_.refs_3_, ...), custom_call_target="tpu_custom_call" | custom-call | flops 15000000512 | bytes 4194304 | tf_op jit(solution)/shard_map/attend_back/pallas_call | solution.py:703
  274.8 8.4 %attend_back.3 = bf16[384,776]{1,0:T(8,128)(2,1)} custom-call(s32[1]{0:T(128)} %get-tuple-element.255.refs_0_, s32[1]{0:T(128)} %bitcast.refs_1_, bf16[384,2048]{1,0:T(8,128)(2,1)} %bitcast.15, bf16[384,1024]{1,0:T(8,128)(2,1)} %get-tuple-element.84.refs_2_.refs_3_, bf16[384,1024]{1,0:T(8,128)(2,1)} %collective-permute-done.refs_3_.refs_4_, ...), custom_call_target="tpu_custom_call" | custom-call | flops 15000000512 | bytes 4194304 | tf_op jit(solution)/shard_map/attend_back/pallas_call | solution.py:703
  283.2 9.5 %all-to-all-done.4 = bf16[16,24,1536]{2,1,0:T(8,128)(2,1)} async-done(((bf16[16,24,1536]{2,1,0:T(8,128)(2,1)}), bf16[16,24,1536]{2,1,0:T(8,128)(2,1)}, u32[]{:S(2)}, u32[]{:S(2)}) %all-to-all-start.4) | async-done | bytes 1179680 | tf_op jit(solution)/shard_map/all_to_all | solution.py:755
  292.7 1.4 convert_reduce_fusion
  294.2 34.9 %all-to-all-start.5 = ((bf16[16,24,776]{2,1,0:T(8,128)(2,1)}), bf16[16,24,776]{2,1,0:T(8,128)(2,1)S(1)}, u32[]{:S(2)}, u32[]{:S(2)}) async-start(bf16[16,24,776]{2,1,0:T(8,128)(2,1)} %bitcast.17), calls=%async_computation.5 | async-start | bytes 1376256 | tf_op jit(solution)/shard_map/all_to_all | solution.py:755
  330.4 16.4 %all-to-all-done.5 = bf16[16,24,776]{2,1,0:T(8,128)(2,1)S(1)} async-done(((bf16[16,24,776]{2,1,0:T(8,128)(2,1)}), bf16[16,24,776]{2,1,0:T(8,128)(2,1)S(1)}, u32[]{:S(2)}, u32[]{:S(2)}) %all-to-all-start.5) | async-done | bytes 596000 | tf_op jit(solution)/shard_map/all_to_all | solution.py:755
  351.4 3.5 all-to-all-start.6
  355.4 6.7 %all-to-all-done.6 = f32[32,1,128]{2,1,0:T(1,128)S(1)} async-done(((f32[32,1,128]{2,1,0:T(1,128)}), f32[32,1,128]{2,1,0:T(1,128)S(1)}, u32[]{:S(2)}, u32[]{:S(2)}) %all-to-all-start.6) | async-done | bytes 16416 | tf_op jit(solution)/shard_map/all_to_all | solution.py:762
  (99 shorter events, 17.3 us)
Async XLA Ops:
  0.6 11.3 %copy-start = (bf16[2048,384]{1,0:T(8,128)(2,1)S(1)}, bf16[2048,384]{1,0:T(8,128)(2,1)}, u32[]{:S(2)}) copy-start(bf16[2048,384]{1,0:T(8,128)(2,1)} %param.21) | copy-start | bytes 4718596
  3.6 26.4 %all-to-all-start = ((bf16[16,24,776]{2,1,0:T(8,128)(2,1)}), bf16[16,24,776]{2,1,0:T(8,128)(2,1)}, u32[]{:S(2)}, u32[]{:S(2)}) async-start(bf16[16,24,776]{2,1,0:T(8,128)(2,1)} %broadcast_in_dim.20), calls=%async_computation | async-start | bytes 1376256 | tf_op jit(solution)/shard_map/all_to_all | solution.py:749
  12.0 2.3 copy-start.19
  30.0 30.6 %all-to-all-start.1 = ((bf16[16,24,1536]{2,1,0:T(8,128)(2,1)}), bf16[16,24,1536]{2,1,0:T(8,128)(2,1)}, u32[]{:S(2)}, u32[]{:S(2)}) async-start(bf16[16,24,1536]{2,1,0:T(8,128)(2,1)} %broadcast_in_dim.21), calls=%async_computation.1 | async-start | bytes 2359296 | tf_op jit(solution)/shard_map/all_to_all | solution.py:749
  45.5 30.3 %collective-permute-start.2 = (bf16[384,1024]{1,0:T(8,128)(2,1)}, bf16[384,1024]{1,0:T(8,128)(2,1)}, u32[]{:S(2)}, u32[]{:S(2)}) collective-permute-start(bf16[384,1024]{1,0:T(8,128)(2,1)} %get-tuple-element.95.refs_2_.refs_3_), channel_id=1, source_target_pairs={{0,1},{1,0},{2,3},{3,2},{4,5},{5,4},{6,7},{7,6},{8,9},{9,8},{10,11... | collective-permute-start | bytes 2359304 | tf_op jit(solution)/shard_map/ppermute | solution.py:725
  52.1 30.1 %collective-permute-start = (bf16[384,1024]{1,0:T(8,128)(2,1)}, bf16[384,1024]{1,0:T(8,128)(2,1)}, u32[]{:S(2)}, u32[]{:S(2)}) collective-permute-start(bf16[384,1024]{1,0:T(8,128)(2,1)} %get-tuple-element.84.refs_2_.refs_3_), channel_id=1, source_target_pairs={{0,1},{1,0},{2,3},{3,2},{4,5},{5,4},{6,7},{7,6},{8,9},{9,8},{10,11... | collective-permute-start | bytes 2359304 | tf_op jit(solution)/shard_map/ppermute | solution.py:725
  60.7 29.9 %all-to-all-start.2 = ((bf16[16,24,576]{2,1,0:T(8,128)(2,1)}), bf16[16,24,576]{2,1,0:T(8,128)(2,1)}, u32[]{:S(2)}, u32[]{:S(2)}) async-start(bf16[16,24,576]{2,1,0:T(8,128)(2,1)} %broadcast_in_dim.24), calls=%async_computation.2 | async-start | bytes 983040 | tf_op jit(solution)/shard_map/all_to_all | solution.py:749
  75.8 5.6 %copy-start.20 = (f32[8]{0:T(128)S(1)}, f32[8]{0:T(128)}, u32[]{:S(2)}) copy-start(f32[8]{0:T(128)} %param.25) | copy-start | bytes 100
  75.8 5.6 %copy-start.21 = (s32[2]{0:T(128)S(1)}, s32[2]{0:T(128)}, u32[]{:S(2)}) copy-start(s32[2]{0:T(128)} %param.24) | copy-start | bytes 28
  81.3 9.2 %collective-permute-start.3 = (bf16[384,1024]{1,0:T(8,128)(2,1)}, bf16[384,1024]{1,0:T(8,128)(2,1)}, u32[]{:S(2)}, u32[]{:S(2)}) collective-permute-start(bf16[384,1024]{1,0:T(8,128)(2,1)} %get-tuple-element.98.refs_3_.refs_2_), channel_id=1, source_target_pairs={{0,1},{1,0},{2,3},{3,2},{4,5},{5,4},{6,7},{7,6},{8,9},{9,8},{10,11... | collective-permute-start | bytes 2359304 | tf_op jit(solution)/shard_map/ppermute | solution.py:725
  87.7 23.9 %collective-permute-start.1 = (bf16[384,1024]{1,0:T(8,128)(2,1)}, bf16[384,1024]{1,0:T(8,128)(2,1)}, u32[]{:S(2)}, u32[]{:S(2)}) collective-permute-start(bf16[384,1024]{1,0:T(8,128)(2,1)} %get-tuple-element.87.refs_3_.refs_2_), channel_id=1, source_target_pairs={{0,1},{1,0},{2,3},{3,2},{4,5},{5,4},{6,7},{7,6},{8,9},{9,8},{10,11... | collective-permute-start | bytes 2359304 | tf_op jit(solution)/shard_map/ppermute | solution.py:725
  111.5 121.6 %collective-permute-start.5 = (bf16[384,1024]{1,0:T(8,128)(2,1)}, bf16[384,1024]{1,0:T(8,128)(2,1)}, u32[]{:S(2)}, u32[]{:S(2)}) collective-permute-start(bf16[384,1024]{1,0:T(8,128)(2,1)} %get-tuple-element.103.refs_4_), channel_id=1, source_target_pairs={{0,1},{1,0},{2,3},{3,2},{4,5},{5,4},{6,7},{7,6},{8,9},{9,8},{10,11... | collective-permute-start | bytes 2359304 | tf_op jit(solution)/shard_map/ppermute | solution.py:725
  132.7 108.4 %collective-permute-start.4 = (bf16[384,1024]{1,0:T(8,128)(2,1)}, bf16[384,1024]{1,0:T(8,128)(2,1)}, u32[]{:S(2)}, u32[]{:S(2)}) collective-permute-start(bf16[384,1024]{1,0:T(8,128)(2,1)} %get-tuple-element.100.refs_4_), channel_id=1, source_target_pairs={{0,1},{1,0},{2,3},{3,2},{4,5},{5,4},{6,7},{7,6},{8,9},{9,8},{10,11... | collective-permute-start | bytes 2359304 | tf_op jit(solution)/shard_map/ppermute | solution.py:725
  133.3 115.8 %all-to-all-start.3 = ((bf16[16,24,576]{2,1,0:T(8,128)(2,1)}), bf16[16,24,576]{2,1,0:T(8,128)(2,1)}, u32[]{:S(2)}, u32[]{:S(2)}) async-start(bf16[16,24,576]{2,1,0:T(8,128)(2,1)} %bitcast.18), calls=%async_computation.3 | async-start | bytes 983040 | tf_op jit(solution)/shard_map/all_to_all | solution.py:755
  240.9 25.8 %collective-permute-start.7 = (bf16[384,1024]{1,0:T(8,128)(2,1)}, bf16[384,1024]{1,0:T(8,128)(2,1)}, u32[]{:S(2)}, u32[]{:S(2)}) collective-permute-start(bf16[384,1024]{1,0:T(8,128)(2,1)} %get-tuple-element.119.refs_6_), channel_id=1, source_target_pairs={{0,1},{1,0},{2,3},{3,2},{4,5},{5,4},{6,7},{7,6},{8,9},{9,8},{10,11... | collective-permute-start | bytes 2359304 | tf_op jit(solution)/shard_map/ppermute | solution.py:725
  248.7 26.2 %collective-permute-start.6 = (bf16[384,1024]{1,0:T(8,128)(2,1)}, bf16[384,1024]{1,0:T(8,128)(2,1)}, u32[]{:S(2)}, u32[]{:S(2)}) collective-permute-start(bf16[384,1024]{1,0:T(8,128)(2,1)} %get-tuple-element.109.refs_6_), channel_id=1, source_target_pairs={{0,1},{1,0},{2,3},{3,2},{4,5},{5,4},{6,7},{7,6},{8,9},{9,8},{10,11... | collective-permute-start | bytes 2359304 | tf_op jit(solution)/shard_map/ppermute | solution.py:725
  249.1 43.7 %all-to-all-start.4 = ((bf16[16,24,1536]{2,1,0:T(8,128)(2,1)}), bf16[16,24,1536]{2,1,0:T(8,128)(2,1)}, u32[]{:S(2)}, u32[]{:S(2)}) async-start(bf16[16,24,1536]{2,1,0:T(8,128)(2,1)} %bitcast.16), calls=%async_computation.4 | async-start | bytes 2359296 | tf_op jit(solution)/shard_map/all_to_all | solution.py:755
  294.2 69.3 %copy-start.4 = (f32[24,768]{1,0:T(8,128)S(1)}, f32[24,768]{1,0:T(8,128)}, u32[]{:S(2)}) copy-start(f32[24,768]{1,0:T(8,128)} %param.29) | copy-start | bytes 221188
  294.2 69.3 %copy-start.6 = (f32[24,768]{1,0:T(8,128)S(1)}, f32[24,768]{1,0:T(8,128)}, u32[]{:S(2)}) copy-start(f32[24,768]{1,0:T(8,128)} %param.28) | copy-start | bytes 221188
  294.2 69.3 %copy-start.10 = (f32[24,768]{1,0:T(8,128)S(1)}, f32[24,768]{1,0:T(8,128)}, u32[]{:S(2)}) copy-start(f32[24,768]{1,0:T(8,128)} %param.34) | copy-start | bytes 221188
  294.2 69.3 %copy-start.11 = (f32[24,768]{1,0:T(8,128)S(1)}, f32[24,768]{1,0:T(8,128)}, u32[]{:S(2)}) copy-start(f32[24,768]{1,0:T(8,128)} %param.39) | copy-start | bytes 221188
  294.2 69.3 %copy-start.12 = (f32[24,768]{1,0:T(8,128)S(1)}, f32[24,768]{1,0:T(8,128)}, u32[]{:S(2)}) copy-start(f32[24,768]{1,0:T(8,128)} %param.38) | copy-start | bytes 221188
  294.2 69.3 %copy-start.13 = (f32[24,768]{1,0:T(8,128)S(1)}, f32[24,768]{1,0:T(8,128)}, u32[]{:S(2)}) copy-start(f32[24,768]{1,0:T(8,128)} %param.33) | copy-start | bytes 221188
  294.2 52.5 %all-to-all-start.5 = ((bf16[16,24,776]{2,1,0:T(8,128)(2,1)}), bf16[16,24,776]{2,1,0:T(8,128)(2,1)S(1)}, u32[]{:S(2)}, u32[]{:S(2)}) async-start(bf16[16,24,776]{2,1,0:T(8,128)(2,1)} %bitcast.17), calls=%async_computation.5 | async-start | bytes 1376256 | tf_op jit(solution)/shard_map/all_to_all | solution.py:755
  329.1 35.3 %copy-start.7 = (f32[24,3,192]{2,0,1:T(8,128)S(1)}, f32[24,3,192]{2,0,1:T(8,128)}, u32[]{:S(2)}) copy-start(f32[24,3,192]{2,0,1:T(8,128)} %param.30) | copy-start | bytes 165892
  329.1 35.3 %copy-start.14 = (f32[24,3,192]{2,0,1:T(8,128)S(1)}, f32[24,3,192]{2,0,1:T(8,128)}, u32[]{:S(2)}) copy-start(f32[24,3,192]{2,0,1:T(8,128)} %param.35) | copy-start | bytes 165892
  329.1 35.2 %copy-start.15 = (f32[24,3,192]{2,0,1:T(8,128)S(1)}, f32[24,3,192]{2,0,1:T(8,128)}, u32[]{:S(2)}) copy-start(f32[24,3,192]{2,0,1:T(8,128)} %param.40) | copy-start | bytes 165892
  348.2 17.3 %copy-start.1 = (f32[24,1536]{1,0:T(8,128)S(1)}, f32[24,1536]{1,0:T(8,128)}, u32[]{:S(2)}) copy-start(f32[24,1536]{1,0:T(8,128)} %param.27) | copy-start | bytes 442372
  348.2 17.3 %copy-start.8 = (f32[24,1536]{1,0:T(8,128)S(1)}, f32[24,1536]{1,0:T(8,128)}, u32[]{:S(2)}) copy-start(f32[24,1536]{1,0:T(8,128)} %param.32) | copy-start | bytes 442372
  348.2 17.3 %copy-start.9 = (f32[24,1536]{1,0:T(8,128)S(1)}, f32[24,1536]{1,0:T(8,128)}, u32[]{:S(2)}) copy-start(f32[24,1536]{1,0:T(8,128)} %param.37) | copy-start | bytes 442372
  351.4 10.6 %all-to-all-start.6 = ((f32[32,1,128]{2,1,0:T(1,128)}), f32[32,1,128]{2,1,0:T(1,128)S(1)}, u32[]{:S(2)}, u32[]{:S(2)}) async-start(f32[32,1,128]{2,1,0:T(1,128)} %broadcast_in_dim.25), calls=%async_computation.6 | async-start | bytes 32768 | tf_op jit(solution)/shard_map/all_to_all | solution.py:762
  355.0 10.2 %collective-permute-start.8 = (f32[24,776]{1,0:T(8,128)S(1)}, f32[24,776]{1,0:T(8,128)S(1)}, u32[]{:S(2)}, u32[]{:S(2)}) collective-permute-start(f32[24,776]{1,0:T(8,128)S(1)} %convert_reduce_fusion.1), channel_id=1, source_target_pairs={{0,1},{1,0},{2,3},{3,2},{4,5},{5,4},{6,7},{7,6},{8,9},{9,8},{10,11... | collective-permute-start | bytes 223496 | tf_op jit(solution)/shard_map/ppermute | solution.py:725
  (6 other events, 9.9 us)

commit v4 on v3

--- a/solution.py
+++ b/solution.py
@@ -22,7 +22,8 @@
 LOG2_E = 1.4426950408889634
 BLOCK = 256
 SAFE_EXPONENT = 100.0
-VMEM_BYTES = 64 * 2**20 - 2**17
+HELD = -1
+VMEM_BYTES = 24 * 2**20
 F32 = jnp.float32
 BF16 = jnp.bfloat16
 
@@ -644,11 +645,12 @@
 
     def give(self, block, *indices):
         for index in indices:
-            self.outward(index, block).start()
+            if self.outs[index][2] != HELD:
+                self.outward(index, block).start()
 
     def finish(self):
         whole = [i for i, entry in enumerate(self.outs) if entry[2] is None]
-        parts = [i for i, entry in enumerate(self.outs) if entry[2] is not None]
+        parts = [i for i, entry in enumerate(self.outs) if entry[2] not in (None, HELD)]
         for index in whole:
             self.outward(index, 0).start()
 
@@ -665,7 +667,8 @@
 
 def call(blocks, kernel, name, scalars, arrays, outs, scratch=(), flops=0):
     smem = pl.BlockSpec(memory_space=pltpu.SMEM)
-    hbm = pl.BlockSpec(memory_space=pl.ANY)
+    hbm = pl.BlockSpec(memory_space=pltpu.HBM)
+    vmem = pl.BlockSpec(memory_space=pltpu.VMEM)
     arrays = [entry if len(entry) == 4 else (*entry, 0) for entry in arrays]
 
     def held(array, axis, group, first):
@@ -677,17 +680,28 @@
         return pltpu.VMEM(tuple(shape), array.dtype)
 
     count, ins, results = len(scalars), len(arrays), len(outs)
-    copied = [i for i in range(ins) if arrays[i][2] is not None]
+    copied = [i for i in range(ins) if arrays[i][2] != HELD]
+    filled = [i for i in range(results) if outs[i][2] != HELD]
+
+    def view(ref, axis, group, first):
+        if group != HELD or not first:
+            return ref
+        if axis is None:
+            return ref.at[:, first[0] : first[0] + first[1]]
+        return ref.at[(slice(None),) * axis + (slice(first * BLOCK, (first + blocks) * BLOCK),)]
 
     def body(*refs):
         scalar_refs, refs = refs[:count], refs[count:]
         in_refs, refs = refs[:ins], refs[ins:]
         out_refs, refs = refs[:results], refs[results:]
-        in_copies = list(in_refs)
+        in_copies = [view(ref, *entry[1:]) for ref, entry in zip(in_refs, arrays)]
         for index, ref in zip(copied, refs):
             in_copies[index] = ref
         refs = refs[len(copied) :]
-        out_copies, refs = refs[:results], refs[results:]
+        out_copies = list(out_refs)
+        for index, ref in zip(filled, refs):
+            out_copies[index] = ref
+        refs = refs[len(filled) :]
         in_sems, out_sems, refs = refs[0], refs[1], refs[2:]
         traffic = Traffic(
             live_blocks(scalar_refs[0]),
@@ -703,17 +717,25 @@
     return pl.pallas_call(
         body,
         name=name,
-        out_shape=tuple(jax.ShapeDtypeStruct(shape, dtype) for shape, dtype, _ in outs),
+        out_shape=tuple(
+            (pltpu.VMEM if axis == HELD else pltpu.HBM)(shape, dtype) for shape, dtype, axis in outs
+        ),
         in_specs=[smem] * count
-        + [hbm if group is not None else pl.BlockSpec(memory_space=pltpu.VMEM) for _, _, group, _ in arrays],
-        out_specs=tuple(hbm for _ in outs),
+        + [vmem if group == HELD else hbm for _, _, group, _ in arrays],
+        out_specs=tuple(vmem if axis == HELD else hbm for _, _, axis in outs),
         scratch_shapes=[held(*arrays[i]) for i in copied]
-        + [pltpu.VMEM(shape, dtype) for shape, dtype, _ in outs]
+        + [pltpu.VMEM(*outs[i][:2]) for i in filled]
         + [pltpu.SemaphoreType.DMA((ins, blocks)), pltpu.SemaphoreType.DMA((results, blocks))]
         + [pltpu.VMEM(shape, dtype) for shape, dtype in scratch],
         compiler_params=pltpu.CompilerParams(vmem_limit_bytes=VMEM_BYTES),
         cost_estimate=pl.CostEstimate(flops=flops, bytes_accessed=4 << 20, transcendentals=0),
-    )(*scalars, *(entry[0] for entry in arrays))
+    )(
+        *scalars,
+        *(
+            pltpu.with_memory_space_constraint(array, pltpu.VMEM if group == HELD else pltpu.HBM)
+            for array, _, group, _ in arrays
+        ),
+    )
 
 
 def exchange(part):
@@ -749,17 +771,37 @@
     return lax.all_to_all(spread, "dp", 0, 0, tiled=True).reshape((-1,) + shard.shape[1:])
 
 
-def reduce_owner(value):
+def collect_kernel(shared_columns, shared_weight, squares_ref, spread_ref, own_ref, message_ref):
+    own = spread_ref[0].astype(F32)
+    for source in range(1, spread_ref.shape[0]):
+        own = own + spread_ref[source].astype(F32)
+    own_ref[...] = own
+    column = lax.broadcasted_iota(jnp.int32, own.shape, 1)
+    weights = jnp.where(column < own.shape[1] - shared_columns, 1.0, shared_weight)
+    squares = jnp.sum(jnp.sum(own * own * weights, axis=0, keepdims=True), axis=1, keepdims=True)
+    message_ref[...] = jnp.broadcast_to(squares + squares_ref[0], message_ref.shape)
+
+
+def collect(spread, squares, shared_columns, shared_weight):
+    vmem = pl.BlockSpec(memory_space=pltpu.VMEM)
+    count = lax.axis_size("dp") * lax.axis_size("ffn")
+    return pl.pallas_call(
+        functools.partial(collect_kernel, shared_columns, shared_weight),
+        name="collect",
+        out_shape=(pltpu.VMEM(spread.shape[1:], F32), pltpu.VMEM((count, 128), F32)),
+        in_specs=[pl.BlockSpec(memory_space=pltpu.SMEM), vmem],
+        out_specs=(vmem, vmem),
+    )(squares.reshape(1), pltpu.with_memory_space_constraint(spread, pltpu.VMEM))
+
+
+def send_owner(value):
     count = lax.axis_size("dp")
     rows = value.shape[0] // count
-    spread = lax.all_to_all(value.astype(BF16).reshape((count, rows) + value.shape[1:]), "dp", 0, 0, tiled=True)
+    return lax.all_to_all(value.astype(BF16).reshape((count, rows) + value.shape[1:]), "dp", 0, 0, tiled=True)
+
+
+def add_parts(spread):
     return jnp.sum(spread.astype(F32), axis=0)
-
-
-def all_sum(value):
-    count = lax.axis_size("dp") * lax.axis_size("ffn")
-    spread = jnp.broadcast_to(value.reshape(1, 1), (count, 128))
-    return jnp.sum(lax.all_to_all(spread, ("dp", "ffn"), 0, 0, tiled=True)[:, 0])
 
 
 def adam_update(weight, gradient, first, second, clipped, rate, decay):
@@ -827,10 +869,9 @@
 
     attn_own = lax.dynamic_slice_in_dim(attn_a.reshape(shard, 4, features), core * flat, flat, 2).reshape(shard, 4 * flat)
     early = gather_direct(jnp.concatenate([attn_own, vec_d], axis=1).astype(BF16))
-    teacher = [project_teacher(0, (statest,))]
-    late_feed = gather_direct(jnp.concatenate([ffn_in, ffn_out], axis=1).astype(BF16), *teacher[0])
-    teacher += [project_teacher(i, teacher[0]) for i in each[1:]]
-    early = after(early, *teacher[1])
+    teacher = [project_teacher(i, (statest,)) for i in each]
+    late_feed = gather_direct(jnp.concatenate([ffn_in, ffn_out], axis=1).astype(BF16), *teacher[0], *teacher[1])
+    early = after(early, *teacher[0], *teacher[1])
     vec_full = early[:, 4 * flat :].astype(F32)
     vec_own = lax.dynamic_slice_in_dim(vec_full, core * flat, flat, 0)
     attn_full = (early, None, 0, (0, 4 * flat))
@@ -853,7 +894,7 @@
     fed = [
         launch(
             feed_kernel, "feed", (live[i],),
-            ((statest, 1, 0, i * rows // BLOCK), (attended[i][7], 1, 0), (mixed_other[i], None, None), in_full,
+            ((statest, 1, 0, i * rows // BLOCK), (attended[i][7], 1, 0), (mixed_other[i], 1, HELD), in_full,
              out_full, (vec_full, None, 0)),
             ((*wide, 1), ((hidden, rows), BF16, 1), ((hidden, rows), BF16, 1), (*act, 1)),
             flops=3 * 10**9,
@@ -866,10 +907,10 @@
         last = i + 1 == sequences
         return launch(
             functools.partial(relation_kernel, bool(earlier)), "relation", (live[i], weights[i]),
-            ((fed[i][0], 1, 0), (fed[i][3], 1, 0), (fed_other[i], None, None), rel_full,
+            ((fed[i][0], 1, 0), (fed[i][3], 1, 0), (fed_other[i], 1, HELD), rel_full,
              (vec_full, None, 0), (teacher[i][0], 2, 1), (teacher[i][1], 1, 1), (teacher[i][2], 2, 1),
-             (teacher[i][3], 1, 1), (teacher[i][4], None, 0), *((value, None, 1) for value in earlier)),
-            (((features, 3 * flat), BF16 if last else F32, None), (*act, 1)),
+             (teacher[i][3], 1, 1), (teacher[i][4], None, 0), *((value, None, HELD) for value in earlier)),
+            (((features, 3 * flat), BF16 if last else F32, HELD), (*act, 1)),
             scratch=(
                 ((features, 3 * flat), F32), act, head_t, head_t, head_t, pair_rows, pair_rows, pair_rows,
                 head_t, ((heads, size, rows), F32),
@@ -883,10 +924,10 @@
         sums = ((features, 8), F32)
         return launch(
             functools.partial(feed_back_kernel, bool(earlier)), "feed_back", (live[i],),
-            ((fed[i][0], 1, 0), (fed[i][3], 1, 0), (fed_other[i], None, None), (related[i][1], 1, 0),
-             (down_other[i], None, None), (fed[i][1], 1, 0), (fed[i][2], 1, 0), in_full,
-             out_full, (vec_full, None, 0), *((value, None, 1) for value in earlier)),
-            (((features, 2 * hidden), BF16 if last else F32, None), (*sums, None), (*wide, 1), (*act, 1)),
+            ((fed[i][0], 1, 0), (fed[i][3], 1, 0), (fed_other[i], 1, 0), (related[i][1], 1, 0),
+             (down_other[i], None, HELD), (fed[i][1], 1, 0), (fed[i][2], 1, 0), in_full,
+             out_full, (vec_full, None, 0), *((value, None, HELD) for value in earlier)),
+            (((features, 2 * hidden), BF16 if last else F32, HELD), (*sums, HELD), (*wide, 1), (*act, HELD)),
             scratch=(((features, 2 * hidden), F32), sums),
             flops=4 * 10**9,
         )
@@ -897,12 +938,12 @@
         return launch(
             functools.partial(attend_back_kernel, bool(earlier), last), "attend_back",
             (live[i], core.reshape(1).astype(jnp.int32)),
-            ((statest, 1, 0, i * rows // BLOCK), (attended[i][7], 1, 0), (mixed_other[i], None, None), (fed_back[i][2], 1, 0),
-             (fed_back[i][3], 1, 0), (up_other[i], None, None), attn_full, (vec_full, None, 0),
+            ((statest, 1, 0, i * rows // BLOCK), (attended[i][7], 1, 0), (mixed_other[i], 1, 0), (fed_back[i][2], 1, 0),
+             (fed_back[i][3], 1, HELD), (up_other[i], None, HELD), attn_full, (vec_full, None, 0),
              (attended[i][0], 2, 1), (attended[i][1], 2, 1), (attended[i][2], 1, 1), (attended[i][3], 1, 1),
              (attended[i][4], 1, 1), (attended[i][5], 2, 0), (attended[i][6], 2, 1),
-             *([(fed_back[i][1], None, 0)] if last else []), *((value, None, 1) for value in earlier)),
-            (((features, 4 * flat + 8), BF16, None),) if last else tuple((*spec, None) for spec in running),
+             *([(fed_back[i][1], None, HELD)] if last else []), *((value, None, HELD) for value in earlier)),
+            (((features, 4 * flat + 8), BF16, HELD),) if last else tuple((*spec, HELD) for spec in running),
             scratch=running + (
                 head_t, pair_rows, ((heads, 8, rows), F32), head_t,
                 ((pairs, rows, 2 * size), F32), ((pairs, rows, 2 * size), F32),
@@ -914,17 +955,20 @@
     for i in each:
         related.append(relate(i, related[-1][:1] if related else ()))
         down_other.append(exchange(related[i][1]))
-    shard_rel = reduce_owner(related[-1][0])
+    sent_rel = send_owner(related[-1][0])
     fed_back, up_other = [], []
     for i in each:
         fed_back.append(feed_back(i, fed_back[-1][:2] if fed_back else ()))
         up_other.append(exchange(fed_back[i][3]))
-    shard_feed = reduce_owner(fed_back[-1][0])
+    sent_feed = send_owner(fed_back[-1][0])
     attended_back = []
     for i in each:
         attended_back.append(attend_back(i, attended_back[-1] if attended_back else ()))
+    sent_attn = send_owner(after(attended_back[-1][0], sent_rel, sent_feed))
+    shard_rel, shard_feed = add_parts(sent_rel), add_parts(sent_feed)
     shard_in, shard_out = shard_feed[:, :hidden], shard_feed[:, hidden:]
-    own = reduce_owner(after(attended_back[-1][0], shard_rel, shard_feed))
+    own, message = collect(sent_attn, jnp.sum(shard_feed * shard_feed) + jnp.sum(shard_rel * shard_rel), 6, 1.0 / cores)
+    grad_norm = jnp.sqrt(jnp.sum(lax.all_to_all(message, ("dp", "ffn"), 0, 0, tiled=True)[:, 0]))
     other = swap(own, "ffn", 0)
     grad_rel = shard_rel.reshape(attn_b.shape)
     upper = core == 1
@@ -935,14 +979,6 @@
     grad_attn = jnp.concatenate(columns, axis=1)
     grad_vec = jnp.concatenate([(low + high)[:, 4 * flat : 4 * flat + 2], own[:, 4 * flat + 2 :]], axis=1)
     gradients = (grad_attn, shard_in, shard_out, grad_rel, grad_vec)
-    shared = own[:, 4 * flat + 2 :]
-    squares = (
-        jnp.sum(own[:, : 4 * flat + 2] * own[:, : 4 * flat + 2])
-        + jnp.sum(shared * shared) / cores
-        + jnp.sum(shard_feed * shard_feed)
-        + jnp.sum(shard_rel * shard_rel)
-    )
-    grad_norm = jnp.sqrt(all_sum(squares))
     clipped = jnp.minimum(1.0, CLIP_NORM / grad_norm)
     masters = (attn_a, ffn_in, ffn_out, attn_b, vec_d)
     firsts = (mom1_attn_a, mom1_ffn_in, mom1_ffn_out, mom1_attn_b, mom1_vec_d)

time: 376 us -> 346 us (0.920)
  starting transfers between devices: 186 us -> 172 us
  waiting for transfers between devices: 51.9 us -> 38 us
  Pallas kernels: 102 us -> 108 us
  other arithmetic: 12.9 us -> 8.51 us
    all_to_all x4, starting transfers between devices: 155 us -> 116 us  [the longest x3 112 us: send_owner(): lax.all_to_all(value.astype(BF16).reshape((count, rows) + value.shape[1:]...]
    ppermute x9, starting transfers between devices: 2.83 us -> 37.5 us  [swap(): return lax.ppermute(value, axis, [(i, i ^ 1 << bit) for i in range(count)])]
    all_to_all x4, waiting for transfers between devices: 32.5 us -> 22.6 us  [the longest x3 16 us: send_owner(): lax.all_to_all(value.astype(BF16).reshape((count, rows) + value.shape[1:]...]
    all_to_all x3, starting transfers between devices: 28 us -> 19.2 us  [gather_direct(): lax.all_to_all(spread, 'dp', 0, 0, tiled=True)]
    pallas_call x12 -> x13, Pallas kernels: 102 us -> 108 us  [the longest x12 107 us: call(): pl.pallas_call(body, name=name, out_shape=tuple(((pltpu.VMEM if axis == H...]
    all_to_all x3, waiting for transfers between devices: 19.4 us -> 15.4 us  [gather_direct(): lax.all_to_all(spread, 'dp', 0, 0, tiled=True)]
  transfers between devices with their start and end apart: 16 -> 16, of which waited for: 6 -> 6; matrix products, arithmetic and copies ran while one was open for 4% -> 4% of each run, Pallas kernels for 28% -> 31%
where the time goes in v4:
time: 346 us; the launch traced here: 341 us
  starting transfers between devices  172 us (50%)
  Pallas kernels  108 us (31%)
  waiting for transfers between devices  38 us (11%)
  local copies, waits for them, and re-layouts  9.86 us (3%)
  other arithmetic  8.51 us (2%)
  between operations  4.87 us (1%)
    all_to_all x3, starting transfers between devices, send_owner(): lax.all_to_all(value.astype(BF16).reshape((count, rows) + value.shape[1:]...  112 us
    pallas_call x12, Pallas kernels, call(): pl.pallas_call(body, name=name, out_shape=tuple(((pltpu.VMEM if axis == H...  107 us
    ppermute x9, starting transfers between devices, swap(): return lax.ppermute(value, axis, [(i, i ^ 1 << bit) for i in range(count)])  37.5 us
    all_to_all x3, starting transfers between devices, gather_direct(): lax.all_to_all(spread, 'dp', 0, 0, tiled=True)  19.2 us
    all_to_all x3, waiting for transfers between devices, send_owner(): lax.all_to_all(value.astype(BF16).reshape((count, rows) + value.shape[1:]...  16 us
    all_to_all x3, waiting for transfers between devices, gather_direct(): lax.all_to_all(spread, 'dp', 0, 0, tiled=True)  15.4 us
  transfers between devices with their start and end apart: 16, of which 6 were waited for; matrix products, arithmetic and copies ran while one was open for 4% of the time, Pallas kernels for 31%

profile of v4, /device:TPU:0, one launch (start us, length us, event | category | flops | bytes accessed | tf_op | source)
XLA Modules:
  0.0 341.4 jit_solution(4629169796669762636)
XLA Ops:
  0.7 1.0 reshape.103
  2.7 0.9 broadcast_in_dim.18
  3.6 8.3 %all-to-all-start = ((bf16[16,24,776]{2,1,0:T(8,128)(2,1)}), bf16[16,24,776]{2,1,0:T(8,128)(2,1)S(1)}, u32[]{:S(2)}, u32[]{:S(2)}) async-start(bf16[16,24,776]{2,1,0:T(8,128)(2,1)} %broadcast_in_dim.18), calls=%async_computation | async-start | bytes 1376256 | tf_op jit(solution)/shard_map/all_to_all | solution.py:771
  12.0 1.6 copy.89
  14.2 6.1 %teacher.2 = (bf16[6,64,1024]{2,1,0:T(8,128)(2,1)}, bf16[3,1024,128]{2,1,0:T(8,128)(2,1)}, bf16[6,64,1024]{2,1,0:T(8,128)(2,1)}, bf16[3,1024,128]{2,1,0:T(8,128)(2,1)}, f32[24,256]{1,0:T(8,128)}) custom-call(s32[1]{0:T(128)} %get-tuple-element.222.refs_0_, bf16[2048,768]{1,0:T(8,128)(2,1)} %refs_1_.1, bf16[3,768,384]{2,1,0:T(8,128)(2,1)} %bitcast.36), custom_call_target="tpu_custom_call" | custom-call | flops 1811939328 | bytes 4194304 | tf_op jit(solution)/shard_map/teacher/pallas_call | solution.py:717
  20.3 4.1 %teacher.3 = (bf16[6,64,1024]{2,1,0:T(8,128)(2,1)}, bf16[3,1024,128]{2,1,0:T(8,128)(2,1)}, bf16[6,64,1024]{2,1,0:T(8,128)(2,1)}, bf16[3,1024,128]{2,1,0:T(8,128)(2,1)}, f32[24,256]{1,0:T(8,128)}) custom-call(s32[1]{0:T(128)} %get-tuple-element.223.refs_0_, bf16[2048,768]{1,0:T(8,128)(2,1)} %refs_1_.1, bf16[3,768,384]{2,1,0:T(8,128)(2,1)} %bitcast.37), custom_call_target="tpu_custom_call" | custom-call | flops 1811939328 | bytes 4194304 | tf_op jit(solution)/shard_map/teacher/pallas_call | solution.py:717
  24.5 1.1 broadcast_in_dim.19
  25.6 4.4 %all-to-all-done = bf16[16,24,776]{2,1,0:T(8,128)(2,1)S(1)} async-done(((bf16[16,24,776]{2,1,0:T(8,128)(2,1)}), bf16[16,24,776]{2,1,0:T(8,128)(2,1)S(1)}, u32[]{:S(2)}, u32[]{:S(2)}) %all-to-all-start) | async-done | bytes 596000 | tf_op jit(solution)/shard_map/all_to_all | solution.py:771
  29.9 4.8 %all-to-all-start.1 = ((bf16[16,24,1536]{2,1,0:T(8,128)(2,1)}), bf16[16,24,1536]{2,1,0:T(8,128)(2,1)S(1)}, u32[]{:S(2)}, u32[]{:S(2)}) async-start(bf16[16,24,1536]{2,1,0:T(8,128)(2,1)} %broadcast_in_dim.19), calls=%async_computation.1 | async-start | bytes 2359296 | tf_op jit(solution)/shard_map/all_to_all | solution.py:771
  36.1 8.7 %attend.3 = (bf16[6,32,1024]{2,1,0:T(8,128)(2,1)}, bf16[6,32,1024]{2,1,0:T(8,128)(2,1)}, bf16[3,1024,64]{2,1,0:T(8,128)(2,1)}, bf16[3,1024,64]{2,1,0:T(8,128)(2,...) custom-call(s32[1]{0:T(128)} %get-tuple-element.222.refs_0_, ...), custom_call_target="tpu_custom_call" | custom-call | flops 6000000000 | bytes 4194304 | tf_op jit(solution)/shard_map/attend/pallas_call | solution.py:717
  45.8 4.6 %attend.2 = (bf16[6,32,1024]{2,1,0:T(8,128)(2,1)}, bf16[6,32,1024]{2,1,0:T(8,128)(2,1)}, bf16[3,1024,64]{2,1,0:T(8,128)(2,1)}, bf16[3,1024,64]{2,1,0:T(8,128)(2,...) custom-call(s32[1]{0:T(128)} %get-tuple-element.223.refs_0_, ...), custom_call_target="tpu_custom_call" | custom-call | flops 6000000000 | bytes 4194304 | tf_op jit(solution)/shard_map/attend/pallas_call | solution.py:717
  50.9 10.2 %all-to-all-done.1 = bf16[16,24,1536]{2,1,0:T(8,128)(2,1)S(1)} async-done(((bf16[16,24,1536]{2,1,0:T(8,128)(2,1)}), bf16[16,24,1536]{2,1,0:T(8,128)(2,1)S(1)}, u32[]{:S(2)}, u32[]{:S(2)}) %all-to-all-start.1) | async-done | bytes 1179680 | tf_op jit(solution)/shard_map/all_to_all | solution.py:771
  61.1 6.1 %all-to-all-start.2 = ((bf16[16,24,576]{2,1,0:T(8,128)(2,1)}), bf16[16,24,576]{2,1,0:T(8,128)(2,1)S(1)}, u32[]{:S(2)}, u32[]{:S(2)}) async-start(bf16[16,24,576]{2,1,0:T(8,128)(2,1)} %broadcast_in_dim.22), calls=%async_computation.2 | async-start | bytes 983040 | tf_op jit(solution)/shard_map/all_to_all | solution.py:771
  67.3 6.9 %feed.3 = (f32[384,1024]{1,0:T(8,128)}, bf16[768,1024]{1,0:T(8,128)(2,1)}, bf16[768,1024]{1,0:T(8,128)(2,1)}, bf16[384,1024]{1,0:T(8,128)(2,1)}) custom-call(s32[1]{0:T(128)} %get-tuple-element.222.refs_0_, bf16[384,2048]{1,0:T(8,128)(2,1)} %bitcast.16, bf16[384,1024]{1,0:T(8,128)(2,1)} %get-tuple-element.95.refs_2_.refs_3_, ...), custom_call_target="tpu_custom_call" | custom-call | flops 3000000000 | bytes 4194304 | tf_op jit(solution)/shard_map/feed/pallas_call | solution.py:717
  75.0 4.3 %feed.2 = (f32[384,1024]{1,0:T(8,128)}, bf16[768,1024]{1,0:T(8,128)(2,1)}, bf16[768,1024]{1,0:T(8,128)(2,1)}, bf16[384,1024]{1,0:T(8,128)(2,1)}) custom-call(s32[1]{0:T(128)} %get-tuple-element.223.refs_0_, bf16[384,2048]{1,0:T(8,128)(2,1)} %bitcast.17, bf16[384,1024]{1,0:T(8,128)(2,1)} %get-tuple-element.84.refs_2_.refs_3_, ...), custom_call_target="tpu_custom_call" | custom-call | flops 3000000000 | bytes 4194304 | tf_op jit(solution)/shard_map/feed/pallas_call | solution.py:717
  81.6 25.1 %relation.2 = (f32[384,576]{1,0:T(8,128)S(1)}, bf16[384,1024]{1,0:T(8,128)(2,1)}) custom-call(s32[1]{0:T(128)} %get-tuple-element.222.refs_0_, f32[1]{0:T(128)} %get-tuple-element.220.refs_1_, f32[384,1024]{1,0:T(8,128)} %get-tuple-element.97.refs_2_.refs_1_, bf16[384,1024]{1,0:T(8,128)(2,1)} %get-tuple-element.98.refs_3_.refs_2_, ...), custom_call_target="tpu_custom_call" | custom-call | flops 30000001024 | bytes 4194304 | tf_op jit(solution)/shard_map/relation/pallas_call | solution.py:717
  106.7 23.9 %collective-permute-start.5 = (bf16[384,1024]{1,0:T(8,128)(2,1)}, bf16[384,1024]{1,0:T(8,128)(2,1)S(1)}, u32[]{:S(2)}, u32[]{:S(2)}) collective-permute-start(bf16[384,1024]{1,0:T(8,128)(2,1)} %get-tuple-element.103.refs_4_), channel_id=1, source_target_pairs={{0,1},{1,0},{2,3},{3,2},{4,5},{5,4},{6,7},{7,6},{8,9},{9,8},{10,11... | collective-permute-start | bytes 2359304 | tf_op jit(solution)/shard_map/ppermute | solution.py:747
  130.7 9.2 %relation.3 = (bf16[384,576]{1,0:T(8,128)(2,1)}, bf16[384,1024]{1,0:T(8,128)(2,1)}) custom-call(s32[1]{0:T(128)} %get-tuple-element.223.refs_0_, f32[1]{0:T(128)} %get-tuple-element.221.refs_1_, f32[384,1024]{1,0:T(8,128)} %get-tuple-element.86.refs_2_.refs_1_, bf16[384,1024]{1,0:T(8,128)(2,1)} %get-tuple-element.87.refs_3_.refs_2_, ...), custom_call_target="tpu_custom_call" | custom-call | flops 30000001024 | bytes 4194304 | tf_op jit(solution)/shard_map/relation/pallas_call | solution.py:717
  140.0 11.4 %collective-permute-start.4 = (bf16[384,1024]{1,0:T(8,128)(2,1)}, bf16[384,1024]{1,0:T(8,128)(2,1)S(1)}, u32[]{:S(2)}, u32[]{:S(2)}) collective-permute-start(bf16[384,1024]{1,0:T(8,128)(2,1)} %get-tuple-element.100.refs_4_), channel_id=1, source_target_pairs={{0,1},{1,0},{2,3},{3,2},{4,5},{5,4},{6,7},{7,6},{8,9},{9,8},{10,11... | collective-permute-start | bytes 2359304 | tf_op jit(solution)/shard_map/ppermute | solution.py:747
  151.3 71.2 %all-to-all-start.4 = ((bf16[16,24,576]{2,1,0:T(8,128)(2,1)}), bf16[16,24,576]{2,1,0:T(8,128)(2,1)}, u32[]{:S(2)}, u32[]{:S(2)}) async-start(bf16[16,24,576]{2,1,0:T(8,128)(2,1)} %bitcast.6), calls=%async_computation.4 | async-start | bytes 983040 | tf_op jit(solution)/shard_map/all_to_all | solution.py:800
  222.6 8.4 %feed_back.2 = (f32[384,1536]{1,0:T(8,128)S(1)}, f32[384,8]{1,0:T(8,128)S(1)}, f32[384,1024]{1,0:T(8,128)}, bf16[384,1024]{1,0:T(8,128)(2,1)S(1)}) custom-call(s32[1]{0:T(128)} %get-tuple-element.222.refs_0_, f32[384,1024]{1,0:T(8,128)} %get-tuple-element.97.refs_2_.refs_1_, bf16[384,1024]{1,0:T(8,128)(2,1)} %get-tuple-element.98.refs_3_.refs_2_, ...), custom_call_target="tpu_custom_call" | custom-call | flops 4000000000 | bytes 4194304 | tf_op jit(solution)/shard_map/feed_back/pallas_call | solution.py:717
  231.1 6.3 %feed_back.3 = (bf16[384,1536]{1,0:T(8,128)(2,1)}, f32[384,8]{1,0:T(8,128)S(1)}, f32[384,1024]{1,0:T(8,128)}, bf16[384,1024]{1,0:T(8,128)(2,1)S(1)}) custom-call(s32[1]{0:T(128)} %get-tuple-element.223.refs_0_, f32[384,1024]{1,0:T(8,128)} %get-tuple-element.86.refs_2_.refs_1_, bf16[384,1024]{1,0:T(8,128)(2,1)} %get-tuple-element.87.refs_3_.refs_2_, ...), custom_call_target="tpu_custom_call" | custom-call | flops 4000000000 | bytes 4194304 | tf_op jit(solution)/shard_map/feed_back/pallas_call | solution.py:717
  237.9 12.1 %all-to-all-start.3 = ((bf16[16,24,1536]{2,1,0:T(8,128)(2,1)}), bf16[16,24,1536]{2,1,0:T(8,128)(2,1)}, u32[]{:S(2)}, u32[]{:S(2)}) async-start(bf16[16,24,1536]{2,1,0:T(8,128)(2,1)} %bitcast.5), calls=%async_computation.3 | async-start | bytes 2359296 | tf_op jit(solution)/shard_map/all_to_all | solution.py:800
  250.1 16.5 %attend_back.2 = (f32[384,768]{1,0:T(8,128)S(1)}, f32[384,8]{1,0:T(8,128)S(1)}, f32[192,8]{1,0:T(8,128)S(1)}) custom-call(s32[1]{0:T(128)} %get-tuple-element.222.refs_0_, s32[1]{0:T(128)} %bitcast.8.refs_1_, bf16[384,2048]{1,0:T(8,128)(2,1)} %bitcast.18, bf16[384,1024]{1,0:T(8,128)(2,1)} %get-tuple-element.95.refs_2_.refs_3_, bf16[384,1024]{1,0:T(8,128)(2,1)} %copy-done.1, ...), custom_call_target="tpu_custom_call" | custom-call | flops 15000000512 | bytes 4194304 | tf_op jit(solution)/shard_map/attend_back/pallas_call | solution.py:717
  266.6 6.9 %attend_back.3 = bf16[384,776]{1,0:T(8,128)(2,1)} custom-call(s32[1]{0:T(128)} %get-tuple-element.223.refs_0_, s32[1]{0:T(128)} %bitcast.8.refs_1_, bf16[384,2048]{1,0:T(8,128)(2,1)} %bitcast.19, bf16[384,1024]{1,0:T(8,128)(2,1)} %get-tuple-element.84.refs_2_.refs_3_, bf16[384,1024]{1,0:T(8,128)(2,1)} %copy-done, f32[384,1024]{1,0:T(8,128)} %get-tuple-element.110.refs_5_, ...), custom_call_target="tpu_custom_call" | custom-call | flops 15000000512 | bytes 4194304 | tf_op jit(solution)/shard_map/attend_back/pallas_call | solution.py:717
  273.5 3.7 %all-to-all-done.3 = bf16[16,24,1536]{2,1,0:T(8,128)(2,1)} async-done(((bf16[16,24,1536]{2,1,0:T(8,128)(2,1)}), bf16[16,24,1536]{2,1,0:T(8,128)(2,1)}, u32[]{:S(2)}, u32[]{:S(2)}) %all-to-all-start.3) | async-done | bytes 1179680 | tf_op jit(solution)/shard_map/all_to_all | solution.py:800
  277.2 28.7 %all-to-all-start.5 = ((bf16[16,24,776]{2,1,0:T(8,128)(2,1)}), bf16[16,24,776]{2,1,0:T(8,128)(2,1)S(1)}, u32[]{:S(2)}, u32[]{:S(2)}) async-start(bf16[16,24,776]{2,1,0:T(8,128)(2,1)} %bitcast.9), calls=%async_computation.5 | async-start | bytes 1376256 | tf_op jit(solution)/shard_map/all_to_all | solution.py:800
  306.0 1.2 convert_reduce_fusion.1
  307.8 1.5 convert_reduce_fusion
  311.2 12.3 %all-to-all-done.5.spread_ref = bf16[16,24,776]{2,1,0:T(8,128)(2,1)S(1)} async-done(((bf16[16,24,776]{2,1,0:T(8,128)(2,1)}), bf16[16,24,776]{2,1,0:T(8,128)(2,1)S(1)}, u32[]{:S(2)}, u32[]{:S(2)}) %all-to-all-start.5) | async-done | bytes 596000 | tf_op jit(solution)/shard_map/all_to_all | solution.py:800
  324.3 3.5 %all-to-all-start.6 = ((f32[32,1,128]{2,1,0:T(1,128)}), f32[32,1,128]{2,1,0:T(1,128)S(1)}, u32[]{:S(2)}, u32[]{:S(2)}) async-start(f32[32,1,128]{2,1,0:T(1,128)} %bitcast.11), calls=%async_computation.6 | async-start | bytes 32768 | tf_op jit(solution)/shard_map/all_to_all | solution.py:971
  328.3 6.6 %all-to-all-done.6 = f32[32,1,128]{2,1,0:T(1,128)S(1)} async-done(((f32[32,1,128]{2,1,0:T(1,128)}), f32[32,1,128]{2,1,0:T(1,128)S(1)}, u32[]{:S(2)}, u32[]{:S(2)}) %all-to-all-start.6) | async-done | bytes 16416 | tf_op jit(solution)/shard_map/all_to_all | solution.py:971
  (111 shorter events, 14.9 us)
Async XLA Ops:
  0.6 11.3 %copy-start.4 = (bf16[2048,384]{1,0:T(8,128)(2,1)S(1)}, bf16[2048,384]{1,0:T(8,128)(2,1)}, u32[]{:S(2)}) copy-start(bf16[2048,384]{1,0:T(8,128)(2,1)} %param.21) | copy-start | bytes 4718596
  3.6 26.3 %all-to-all-start = ((bf16[16,24,776]{2,1,0:T(8,128)(2,1)}), bf16[16,24,776]{2,1,0:T(8,128)(2,1)S(1)}, u32[]{:S(2)}, u32[]{:S(2)}) async-start(bf16[16,24,776]{2,1,0:T(8,128)(2,1)} %broadcast_in_dim.18), calls=%async_computation | async-start | bytes 1376256 | tf_op jit(solution)/shard_map/all_to_all | solution.py:771
  29.9 31.2 %all-to-all-start.1 = ((bf16[16,24,1536]{2,1,0:T(8,128)(2,1)}), bf16[16,24,1536]{2,1,0:T(8,128)(2,1)S(1)}, u32[]{:S(2)}, u32[]{:S(2)}) async-start(bf16[16,24,1536]{2,1,0:T(8,128)(2,1)} %broadcast_in_dim.19), calls=%async_computation.1 | async-start | bytes 2359296 | tf_op jit(solution)/shard_map/all_to_all | solution.py:771
  36.1 8.8 %copy-start.13 = (f32[24,3,192]{2,0,1:T(8,128)S(1)}, f32[24,3,192]{2,0,1:T(8,128)}, u32[]{:S(2)}) copy-start(f32[24,3,192]{2,0,1:T(8,128)} %param.30) | copy-start | bytes 165892
  44.7 22.5 %collective-permute-start.2 = (bf16[384,1024]{1,0:T(8,128)(2,1)}, bf16[384,1024]{1,0:T(8,128)(2,1)S(1)}, u32[]{:S(2)}, u32[]{:S(2)}) collective-permute-start(bf16[384,1024]{1,0:T(8,128)(2,1)} %get-tuple-element.95.refs_2_.refs_3_), channel_id=1, source_target_pairs={{0,1},{1,0},{2,3},{3,2},{4,5},{5,4},{6,7},{7,6},{8,9},{9,8},{10,11... | collective-permute-start | bytes 2359304 | tf_op jit(solution)/shard_map/ppermute | solution.py:747
  50.4 24.6 %collective-permute-start = (bf16[384,1024]{1,0:T(8,128)(2,1)}, bf16[384,1024]{1,0:T(8,128)(2,1)S(1)}, u32[]{:S(2)}, u32[]{:S(2)}) collective-permute-start(bf16[384,1024]{1,0:T(8,128)(2,1)} %get-tuple-element.84.refs_2_.refs_3_), channel_id=1, source_target_pairs={{0,1},{1,0},{2,3},{3,2},{4,5},{5,4},{6,7},{7,6},{8,9},{9,8},{10,11... | collective-permute-start | bytes 2359304 | tf_op jit(solution)/shard_map/ppermute | solution.py:747
  61.1 19.7 %all-to-all-start.2 = ((bf16[16,24,576]{2,1,0:T(8,128)(2,1)}), bf16[16,24,576]{2,1,0:T(8,128)(2,1)S(1)}, u32[]{:S(2)}, u32[]{:S(2)}) async-start(bf16[16,24,576]{2,1,0:T(8,128)(2,1)} %broadcast_in_dim.22), calls=%async_computation.2 | async-start | bytes 983040 | tf_op jit(solution)/shard_map/all_to_all | solution.py:771
  67.2 7.0 %copy-start.27 = (f32[8]{0:T(128)S(1)}, f32[8]{0:T(128)}, u32[]{:S(2)}) copy-start(f32[8]{0:T(128)} %param.25) | copy-start | bytes 100
  74.1 6.7 %collective-permute-start.3 = (bf16[384,1024]{1,0:T(8,128)(2,1)}, bf16[384,1024]{1,0:T(8,128)(2,1)S(1)}, u32[]{:S(2)}, u32[]{:S(2)}) collective-permute-start(bf16[384,1024]{1,0:T(8,128)(2,1)} %get-tuple-element.98.refs_3_.refs_2_), channel_id=1, source_target_pairs={{0,1},{1,0},{2,3},{3,2},{4,5},{5,4},{6,7},{7,6},{8,9},{9,8},{10,11... | collective-permute-start | bytes 2359304 | tf_op jit(solution)/shard_map/ppermute | solution.py:747
  79.4 51.3 %collective-permute-start.1 = (bf16[384,1024]{1,0:T(8,128)(2,1)}, bf16[384,1024]{1,0:T(8,128)(2,1)S(1)}, u32[]{:S(2)}, u32[]{:S(2)}) collective-permute-start(bf16[384,1024]{1,0:T(8,128)(2,1)} %get-tuple-element.87.refs_3_.refs_2_), channel_id=1, source_target_pairs={{0,1},{1,0},{2,3},{3,2},{4,5},{5,4},{6,7},{7,6},{8,9},{9,8},{10,11... | collective-permute-start | bytes 2359304 | tf_op jit(solution)/shard_map/ppermute | solution.py:747
  80.8 25.9 %copy-start.3 = (bf16[384,1024]{1,0:T(8,128)(2,1)}, bf16[384,1024]{1,0:T(8,128)(2,1)S(1)}, u32[]{:S(2)}) copy-start(bf16[384,1024]{1,0:T(8,128)(2,1)S(1)} %collective-permute-done.3.refs_4_.refs_3_) | copy-start | bytes 2359300
  106.7 115.8 %collective-permute-start.5 = (bf16[384,1024]{1,0:T(8,128)(2,1)}, bf16[384,1024]{1,0:T(8,128)(2,1)S(1)}, u32[]{:S(2)}, u32[]{:S(2)}) collective-permute-start(bf16[384,1024]{1,0:T(8,128)(2,1)} %get-tuple-element.103.refs_4_), channel_id=1, source_target_pairs={{0,1},{1,0},{2,3},{3,2},{4,5},{5,4},{6,7},{7,6},{8,9},{9,8},{10,11... | collective-permute-start | bytes 2359304 | tf_op jit(solution)/shard_map/ppermute | solution.py:747
  130.7 9.3 %copy-start.2 = (bf16[384,1024]{1,0:T(8,128)(2,1)}, bf16[384,1024]{1,0:T(8,128)(2,1)S(1)}, u32[]{:S(2)}) copy-start(bf16[384,1024]{1,0:T(8,128)(2,1)S(1)} %collective-permute-done.1.refs_4_.refs_3_) | copy-start | bytes 2359300
  140.0 91.1 %collective-permute-start.4 = (bf16[384,1024]{1,0:T(8,128)(2,1)}, bf16[384,1024]{1,0:T(8,128)(2,1)S(1)}, u32[]{:S(2)}, u32[]{:S(2)}) collective-permute-start(bf16[384,1024]{1,0:T(8,128)(2,1)} %get-tuple-element.100.refs_4_), channel_id=1, source_target_pairs={{0,1},{1,0},{2,3},{3,2},{4,5},{5,4},{6,7},{7,6},{8,9},{9,8},{10,11... | collective-permute-start | bytes 2359304 | tf_op jit(solution)/shard_map/ppermute | solution.py:747
  151.3 86.6 %all-to-all-start.4 = ((bf16[16,24,576]{2,1,0:T(8,128)(2,1)}), bf16[16,24,576]{2,1,0:T(8,128)(2,1)}, u32[]{:S(2)}, u32[]{:S(2)}) async-start(bf16[16,24,576]{2,1,0:T(8,128)(2,1)} %bitcast.6), calls=%async_computation.4 | async-start | bytes 983040 | tf_op jit(solution)/shard_map/all_to_all | solution.py:800
  231.0 19.1 %collective-permute-start.7 = (bf16[384,1024]{1,0:T(8,128)(2,1)S(1)}, bf16[384,1024]{1,0:T(8,128)(2,1)S(1)}, u32[]{:S(2)}, u32[]{:S(2)}) collective-permute-start(bf16[384,1024]{1,0:T(8,128)(2,1)S(1)} %get-tuple-element.121.refs_6_), channel_id=1, source_target_pairs={{0,1},{1,0},{2,3},{3,2},{4,5},{5,4},{6,7},{7,6},{8,9},{9,8},{10,11... | collective-permute-start | bytes 2359304 | tf_op jit(solution)/shard_map/ppermute | solution.py:747
  237.4 29.2 %collective-permute-start.6 = (bf16[384,1024]{1,0:T(8,128)(2,1)S(1)}, bf16[384,1024]{1,0:T(8,128)(2,1)S(1)}, u32[]{:S(2)}, u32[]{:S(2)}) collective-permute-start(bf16[384,1024]{1,0:T(8,128)(2,1)S(1)} %get-tuple-element.111.refs_6_), channel_id=1, source_target_pairs={{0,1},{1,0},{2,3},{3,2},{4,5},{5,4},{6,7},{7,6},{8,9},{9,8},{10,11... | collective-permute-start | bytes 2359304 | tf_op jit(solution)/shard_map/ppermute | solution.py:747
  237.9 39.3 %all-to-all-start.3 = ((bf16[16,24,1536]{2,1,0:T(8,128)(2,1)}), bf16[16,24,1536]{2,1,0:T(8,128)(2,1)}, u32[]{:S(2)}, u32[]{:S(2)}) async-start(bf16[16,24,1536]{2,1,0:T(8,128)(2,1)} %bitcast.5), calls=%async_computation.3 | async-start | bytes 2359296 | tf_op jit(solution)/shard_map/all_to_all | solution.py:800
  277.2 46.3 %all-to-all-start.5 = ((bf16[16,24,776]{2,1,0:T(8,128)(2,1)}), bf16[16,24,776]{2,1,0:T(8,128)(2,1)S(1)}, u32[]{:S(2)}, u32[]{:S(2)}) async-start(bf16[16,24,776]{2,1,0:T(8,128)(2,1)} %bitcast.9), calls=%async_computation.5 | async-start | bytes 1376256 | tf_op jit(solution)/shard_map/all_to_all | solution.py:800
  305.9 30.5 %copy-start.12 = (f32[24,768]{1,0:T(8,128)S(1)}, f32[24,768]{1,0:T(8,128)}, u32[]{:S(2)}) copy-start(f32[24,768]{1,0:T(8,128)} %param.28) | copy-start | bytes 221188
  305.9 30.5 %copy-start.17 = (f32[24,768]{1,0:T(8,128)S(1)}, f32[24,768]{1,0:T(8,128)}, u32[]{:S(2)}) copy-start(f32[24,768]{1,0:T(8,128)} %param.34) | copy-start | bytes 221188
  305.9 30.5 %copy-start.18 = (f32[24,768]{1,0:T(8,128)S(1)}, f32[24,768]{1,0:T(8,128)}, u32[]{:S(2)}) copy-start(f32[24,768]{1,0:T(8,128)} %param.39) | copy-start | bytes 221188
  305.9 30.5 %copy-start.19 = (f32[24,768]{1,0:T(8,128)S(1)}, f32[24,768]{1,0:T(8,128)}, u32[]{:S(2)}) copy-start(f32[24,768]{1,0:T(8,128)} %param.38) | copy-start | bytes 221188
  306.0 30.5 %copy-start.20 = (f32[24,768]{1,0:T(8,128)S(1)}, f32[24,768]{1,0:T(8,128)}, u32[]{:S(2)}) copy-start(f32[24,768]{1,0:T(8,128)} %param.33) | copy-start | bytes 221188
  307.8 29.5 %copy-start.14 = (f32[24,3,192]{2,0,1:T(8,128)S(1)}, f32[24,3,192]{2,0,1:T(8,128)}, u32[]{:S(2)}) copy-start(f32[24,3,192]{2,0,1:T(8,128)} %param.30) | copy-start | bytes 165892
  307.8 29.5 %copy-start.21 = (f32[24,3,192]{2,0,1:T(8,128)S(1)}, f32[24,3,192]{2,0,1:T(8,128)}, u32[]{:S(2)}) copy-start(f32[24,3,192]{2,0,1:T(8,128)} %param.35) | copy-start | bytes 165892
  307.8 29.5 %copy-start.22 = (f32[24,3,192]{2,0,1:T(8,128)S(1)}, f32[24,3,192]{2,0,1:T(8,128)}, u32[]{:S(2)}) copy-start(f32[24,3,192]{2,0,1:T(8,128)} %param.40) | copy-start | bytes 165892
  324.3 14.0 %copy-start.7 = (f32[24,1536]{1,0:T(8,128)S(1)}, f32[24,1536]{1,0:T(8,128)}, u32[]{:S(2)}) copy-start(f32[24,1536]{1,0:T(8,128)} %param.27) | copy-start | bytes 442372
  324.3 14.0 %copy-start.15 = (f32[24,1536]{1,0:T(8,128)S(1)}, f32[24,1536]{1,0:T(8,128)}, u32[]{:S(2)}) copy-start(f32[24,1536]{1,0:T(8,128)} %param.32) | copy-start | bytes 442372
  324.3 14.1 %copy-start.16 = (f32[24,1536]{1,0:T(8,128)S(1)}, f32[24,1536]{1,0:T(8,128)}, u32[]{:S(2)}) copy-start(f32[24,1536]{1,0:T(8,128)} %param.37) | copy-start | bytes 442372
  324.3 10.6 %all-to-all-start.6 = ((f32[32,1,128]{2,1,0:T(1,128)}), f32[32,1,128]{2,1,0:T(1,128)S(1)}, u32[]{:S(2)}, u32[]{:S(2)}) async-start(f32[32,1,128]{2,1,0:T(1,128)} %bitcast.11), calls=%async_computation.6 | async-start | bytes 32768 | tf_op jit(solution)/shard_map/all_to_all | solution.py:971
  327.9 10.2 %collective-permute-start.8 = (f32[24,776]{1,0:T(8,128)S(1)}, f32[24,776]{1,0:T(8,128)S(1)}, u32[]{:S(2)}, u32[]{:S(2)}) collective-permute-start(f32[24,776]{1,0:T(8,128)S(1)} %get-tuple-element.127), channel_id=1, source_target_pairs={{0,1},{1,0},{2,3},{3,2},{4,5},{5,4},{6,7},{7,6},{8,9},{9,8},{10,11... | collective-permute-start | bytes 223496 | tf_op jit(solution)/shard_map/ppermute | solution.py:747
  (13 other events, 42.8 us)
